TPU v7x, 256 devices: a whole 4x4x8 slice. The times are simulated.
256 devices in a mesh: fsdp: 64 (over x, y_lo, z), rep: 4 (over y_hi, core).
Axes of the slice: x: 4, y: 4 (y_hi: 2, y_lo: 2; y = y_hi * 2 + y_lo), z: 8, core: 2. Of those that a mesh axis runs over, the one named last changes fastest.
Arguments:
- master: float32 [64, 256, 2880], P(None, 'rep', 'fsdp'), may hold values from -0.125 to 0.125
- placement: int32 [64], replicated, may hold values from 0 to 63, each once
- resident_gate_up: bfloat16 [64, 2880, 512], P('fsdp'), may hold values from -0.109375 to 0.109375
- resident_down: bfloat16 [64, 256, 2880], P('fsdp'), may hold values from -0.125 to 0.125
- hidden: bfloat16 [4, 256, 2880], P('rep'), may hold values from -6 to 6
- routes: int32 [4, 256, 4], P('rep'), may hold values from 0 to 7, all different within a row; in each aligned block of 4 rows (0 to 3, 4 to 7, ..., all dimensions but the last counted through in order) at most 3 rows name the same one
- norm_gain: bfloat16 [2880], replicated, may hold values from 0.099609375 to 1.8984375
- router: bfloat16 [2880, 8], P('rep'), may hold values from -0.21875 to 0.21875
Outputs:
- refreshed: bfloat16 [64, 256, 2880], P('fsdp')
- decoded: bfloat16 [4, 256, 2880], P('rep', 'fsdp')
Inputs may be any that keep to these rules, and one draw needn't show every extreme that they name: `placement`: each slot has exactly one owner. `routes`: the 4 experts of a token differ; in each aligned block of 4 tokens of a replica group no expert is chosen by more than 3 tokens, and in some block one expert is chosen by exactly 3.
All inputs are finite; a program needn't handle non-finite values.
Results may differ from a plain program's by a relative error of at most 0.0056.
Values may be sent and summed in bfloat16 or wider, within the bound.
No kernel may reach another device: no remote copies, remote signals or barrier semaphores. Data moves between devices by JAX's collectives and lax.ppermute only.
A program may use at most 64 MiB of HBM per device.

v0:
```python
import jax
import jax.numpy as jnp
from jax import lax
from jax.sharding import PartitionSpec as P

EXPERTS = 8
BLOCK = 32


lowest_power = -40
highest_power = 8


def owner_slots(placement):
    count = placement.shape[0]
    iota_owner = jnp.arange(count, dtype=jnp.int32)
    matches = placement[:, None] == iota_owner[None, :]
    return jnp.sum(jnp.where(matches, iota_owner[:, None], 0), axis=0)


def power_scales(amax):
    scale = jnp.full(amax.shape, 2.0**lowest_power, amax.dtype)
    inverse = jnp.full(amax.shape, 2.0 ** (-lowest_power), amax.dtype)
    for power in range(lowest_power, highest_power):
        above = amax > 6.0 * 2.0**power
        scale = jnp.where(above, scale * 2.0, scale)
        inverse = jnp.where(above, inverse * 0.5, inverse)
    return (scale, inverse)


def nearest_level(values):
    size = jnp.abs(values)
    level = (
        jnp.where(size >= 0.25, 0.5, 0.0)
        + jnp.where(size >= 0.75, 0.5, 0.0)
        + jnp.where(size >= 1.25, 0.5, 0.0)
        + jnp.where(size >= 1.75, 0.5, 0.0)
        + jnp.where(size >= 2.5, 1.0, 0.0)
        + jnp.where(size >= 3.5, 1.0, 0.0)
        + jnp.where(size >= 5.0, 2.0, 0.0)
    )
    return jnp.where(values < 0, -level, level)


def encode_blocks(master):
    slots, shard_rows, columns = master.shape
    grouped = master.reshape(slots, shard_rows // BLOCK, BLOCK, columns)
    amax = jnp.max(jnp.abs(grouped), axis=2)
    scale, inverse = power_scales(amax)
    code_values = nearest_level(grouped * inverse[:, :, None, :]).astype(jnp.bfloat16)
    return (code_values.reshape(slots, shard_rows, columns), scale.astype(jnp.bfloat16))


def decode_blocks(code_values, block_scale):
    slots, shard_rows, columns = code_values.shape
    blocks = block_scale.shape[1]
    grouped = code_values.reshape(slots, blocks, shard_rows // blocks, columns)
    widened = grouped.astype(jnp.float32) * block_scale.astype(jnp.float32)[:, :, None, :]
    return widened.astype(jnp.bfloat16).reshape(slots, shard_rows, columns)


def on_device(
    master, placement, resident_gate_up, resident_down, hidden, routes, norm_gain, router
):
    owners = owner_slots(placement)
    code_values, block_scale = encode_blocks(master)
    code_values = code_values[owners]
    block_scale = block_scale[owners]
    own_codes, own_scale = (
        lax.all_to_all(code_values, "fsdp", split_axis=0, concat_axis=2, tiled=True),
        lax.all_to_all(block_scale, "fsdp", split_axis=0, concat_axis=2, tiled=True),
    )
    own_rows = decode_blocks(own_codes, own_scale)
    refreshed = lax.all_gather(own_rows, "rep", axis=1, tiled=True)
    full_router = lax.all_gather(router, "rep", axis=0, tiled=True)
    tokens = hidden[0]
    chosen = routes[0]
    widened = tokens.astype(jnp.float32)
    normed = (
        widened
        * lax.rsqrt(jnp.mean(widened * widened, axis=-1, keepdims=True) + 1e-05)
        * norm_gain.astype(jnp.float32)
    ).astype(jnp.bfloat16)
    logits = jnp.dot(normed, full_router, preferred_element_type=jnp.float32)
    picked = jnp.take_along_axis(logits, chosen, axis=1)
    powered = jnp.exp(picked)
    probs = powered / jnp.sum(powered, axis=1, keepdims=True)
    fsdp_count = lax.axis_size("fsdp")
    split_count = fsdp_count // EXPERTS
    my_expert = owners[lax.axis_index("fsdp")] // split_count
    gate_up = resident_gate_up[0]
    down_rows = resident_down[0]
    hid_units = down_rows.shape[0]
    own_count = tokens.shape[0] // fsdp_count
    first_row = lax.axis_index("fsdp") * own_count
    token_weight = jnp.sum(probs * (chosen == my_expert).astype(jnp.float32), axis=1)
    projected = jnp.dot(normed, gate_up, preferred_element_type=jnp.float32)
    gate_part = projected[:, :hid_units]
    up_part = projected[:, hid_units:]
    activated = (
        token_weight[:, None] * gate_part * jax.nn.sigmoid(1.702 * gate_part) * (up_part + 1.0)
    ).astype(jnp.bfloat16)
    all_terms = jnp.dot(activated, down_rows, preferred_element_type=jnp.float32)
    mixed = lax.psum_scatter(all_terms, "fsdp", scatter_dimension=0, tiled=True)
    residual_rows = lax.dynamic_slice_in_dim(widened, first_row, own_count, 0)
    decoded = (residual_rows + mixed).astype(jnp.bfloat16)
    return (refreshed, decoded[None])


def solution(mesh):
    placed = (
        P(None, "rep", "fsdp"),
        P(),
        P("fsdp", None, None),
        P("fsdp", None, None),
        P("rep", None, None),
        P("rep", None, None),
        P(),
        P("rep", None),
    )
    return jax.shard_map(
        on_device,
        mesh=mesh,
        in_specs=placed,
        out_specs=(P("fsdp", None, None), P("rep", "fsdp", None)),
        check_vma=False,
    )
```

profile of v0, /device:TPU:32, one launch (start us, length us, event | category | flops | bytes accessed | tf_op | source)
XLA Modules:
  0.0 725.0 jit_solution(140988854695776949)
XLA Ops:
  8.0 0.0 copy-start
  8.0 0.9 select_reduce_fusion.1
  8.9 2.9 copy.83
  11.9 1.7 bitcast_reduce_fusion
  13.6 0.1 copy.84
  13.7 2.1 fusion.24
  15.8 1.2 gather_fusion.1
  17.1 12.6 %all-to-all-start.1 = ((bf16[64,2,45]{2,1,0:T(2,128)(2,1)}), bf16[64,2,45]{2,1,0:T(2,128)(2,1)S(1)}, u32[]{:S(2)}, u32[]{:S(2)}) async-start(bf16[64,2,45]{2,1,0:T(2,128)(2,1)} %gather_fusion.1), calls=%async_computation.1 | async-start | bytes 65536 | tf_op jit(solution)/shard_map/all_to_all | solution.py:71
  29.7 0.1 copy.132
  29.8 1.2 mul.609
  31.0 3.1 copy.134
  34.1 4.4 fusion.5
  38.5 2.7 gather_fusion
  41.2 3.0 reshape.310
  44.2 11.3 %all-to-all-start = ((bf16[64,2,1440]{2,1,0:T(2,128)(2,1)}), bf16[64,2,1440]{2,1,0:T(2,128)(2,1)S(1)}, u32[]{:S(2)}, u32[]{:S(2)}) async-start(bf16[64,2,1440]{2,1,0:T(2,128)(2,1)} %reshape.310), calls=%async_computation | async-start | bytes 786432 | tf_op jit(solution)/shard_map/all_to_all | solution.py:70
  55.4 0.0 all-gather.3.cloned.1.call-start
  55.5 0.1 reshape.281
  55.7 14.8 %all-to-all-done = bf16[64,2,1440]{2,1,0:T(2,128)(2,1)S(1)} async-done(((bf16[64,2,1440]{2,1,0:T(2,128)(2,1)}), bf16[64,2,1440]{2,1,0:T(2,128)(2,1)S(1)}, u32[]{:S(2)}, u32[]{:S(2)}) %all-to-all-start) | async-done | bytes 368672 | tf_op jit(solution)/shard_map/all_to_all | solution.py:70
  70.5 1.7 reshape.311
  72.2 2.4 convert_bitcast_fusion
  74.6 2.5 reshape.308
  77.0 2.7 copy.142
  79.8 2.0 fusion.16
  81.8 0.0 all-gather.3.cloned.1.call-update
  81.8 0.0 all-reduce.3.cloned.1.call-start
  81.8 0.6 dynamic_slice.10
  85.1 6.9 all-gather
  92.0 0.1 reshape.307
  92.1 0.1 copy.138
  92.3 0.1 copy.140
  92.4 0.1 reshape.300
  92.5 1.8 fusion.2
  94.3 1.9 fusion.8
  96.3 6.5 gather_fusion.2
  102.8 0.1 reshape.303
  103.0 0.1 fusion.23
  103.1 0.2 select_reduce_fusion
  103.3 3.4 fusion
  106.7 2.3 fusion.10
  109.0 0.0 all-reduce.3.cloned.1.call-update
  109.0 3.2 convert_element_type.94
  112.3 2.9 constant_dynamic-slice_fusion
  115.2 1.8 copy.137
  117.0 0.6 dynamic-slice.1
  118.3 0.0 all-gather.3.cloned.1.call-done
  118.3 2.5 copy.141
  120.9 595.1 %all-reduce.3.cloned.1.call-done = f32[256,2880]{1,0:T(8,128)} async-done(((f32[256,2880]{1,0:T(8,128)}), f32[256,2880]{1,0:T(8,128)}) %all-reduce.3.cloned.1.call-update) | async-done | bytes 2949136
  716.0 1.5 fusion.26
  (21 shorter events, 0.2 us)
Async XLA Ops:
  8.0 95.3 %copy-start = (bf16[1,2880,512]{2,1,0:T(8,128)(2,1)S(1)}, bf16[1,2880,512]{2,1,0:T(8,128)(2,1)}, u32[]{:S(2)}) copy-start(bf16[1,2880,512]{2,1,0:T(8,128)(2,1)} %param.10) | copy-start | bytes 8847364
  17.1 27.1 %all-to-all-start.1 = ((bf16[64,2,45]{2,1,0:T(2,128)(2,1)}), bf16[64,2,45]{2,1,0:T(2,128)(2,1)S(1)}, u32[]{:S(2)}, u32[]{:S(2)}) async-start(bf16[64,2,45]{2,1,0:T(2,128)(2,1)} %gather_fusion.1), calls=%async_computation.1 | async-start | bytes 65536 | tf_op jit(solution)/shard_map/all_to_all | solution.py:71
  44.2 26.3 %all-to-all-start = ((bf16[64,2,1440]{2,1,0:T(2,128)(2,1)}), bf16[64,2,1440]{2,1,0:T(2,128)(2,1)S(1)}, u32[]{:S(2)}, u32[]{:S(2)}) async-start(bf16[64,2,1440]{2,1,0:T(2,128)(2,1)} %reshape.310), calls=%async_computation | async-start | bytes 786432 | tf_op jit(solution)/shard_map/all_to_all | solution.py:70
  55.4 62.9 %all-gather.3.cloned.1.call-start = ((), (), s32[]{:S(2)}) async-start(), calls=%async_computation.2 | async-start | bytes 1884160 | tf_op jit(solution)/shard_map/all_gather | solution.py:74
  79.7 5.3 copy-start.4
  79.7 5.3 copy-start.3
  79.7 12.4 %copy-start.2 = (s32[1,256,4]{1,2,0:T(4,128)S(1)}, s32[1,256,4]{1,2,0:T(4,128)}, u32[]{:S(2)}) copy-start(s32[1,256,4]{1,2,0:T(4,128)} %param.13) | copy-start | bytes 12292
  81.8 634.2 %all-reduce.3.cloned.1.call-start = ((), (), s32[]{:S(2)}) async-start(), calls=%async_computation.3 | async-start | bytes 6029312
  103.3 3.4 copy-start.1
  112.3 4.8 copy-start.5
Sparse Core Ops, SparseCore 0:
  81.9 21.8 all-gather.2
Sparse Core Ops, SparseCore 1:
  109.1 606.8 all-reduce.2
where the time goes:
time: 727 us; the launch traced here: 725 us
  waiting for transfers between devices  610 us (84%)
  local copies, waits for them, and re-layouts  37.1 us (5%)
  starting transfers between devices  23.9 us (3%)
  other arithmetic  20.5 us (3%)
  between operations  18.9 us (3%)
  matrix products  7.61 us (1%)
    unnamed x3, waiting for transfers between devices  595 us
    all_to_all x1, waiting for transfers between devices, on_device(): lax.all_to_all(code_values, 'fsdp', split_axis=0, concat_axis=2, tiled=True)  14.8 us
  transfers between devices with their start and end apart: 4, of which 2 were waited for; matrix products, arithmetic and copies ran while one was open for 6% of the time, Pallas kernels for 0%

commit v1 on v0

v1 whole, which is shorter than its diff:
```python
import functools

import jax
import jax.numpy as jnp
from jax import lax
from jax.experimental import pallas as pl
from jax.experimental.pallas import tpu as pltpu
from jax.sharding import Mesh
from jax.sharding import PartitionSpec as P

D = 2880
SLOTS = 64
COLS = 45
HALF = 24
ROWS = 64
TOK = 256
HID = 256
CAP = 3
PLANE = 8
DEPTH = 8
PACKED = TOK // 4 * CAP

VMEM = pltpu.VMEM
SMEM = pltpu.SMEM
BF = jnp.bfloat16
F32 = jnp.float32

FSDP = ("x", "yl", "z")
REP = ("yh", "c")


def params(mib):
    return pltpu.CompilerParams(vmem_limit_bytes=mib * 2**20)


def nt(a, b):
    return lax.dot_general(a, b, (((1,), (1,)), ((), ())), preferred_element_type=F32)


def tn(a, b):
    return lax.dot_general(a, b, (((0,), (0,)), ((), ())), preferred_element_type=F32)


def nn(a, b):
    return lax.dot_general(a, b, (((1,), (0,)), ((), ())), preferred_element_type=F32)


def iota(shape, dim):
    return lax.broadcasted_iota(jnp.int32, shape, dim)


def invert(place_ref, slot_ref):
    def step(s, _):
        slot_ref[place_ref[s]] = s
        return 0

    lax.fori_loop(0, SLOTS, step, 0, unroll=8)


def encode_kernel(place_ref, master_ref, out_ref, slot_ref, held_ref):
    invert(place_ref, slot_ref)
    spread = (iota((128, 128), 0) == (iota((128, 128), 1) // 32) * 32 + 31).astype(F32).astype(BF)

    def encode(j, _):
        low = master_ref[j]
        high = master_ref[jnp.minimum(j + HALF, COLS - 1)]
        values = jnp.concatenate([low, high], axis=1)
        size = jnp.abs(values)
        top = size
        for shift in (1, 2, 4, 8, 16):
            top = jnp.maximum(top, pltpu.roll(top, shift, 1))
        top = jnp.maximum(top, 6.0 * 2.0**-40)
        lead = top * (2.0**23 + 1.0)
        lead = jnp.abs(lead - lead * (1.0 - 2.0**-24))
        scale = jnp.where(top > lead * 1.5, lead * 0.5, lead * 0.25)
        s = nn(scale.astype(BF), spread)
        out = jnp.where(size >= s * 0.25, s * 0.5, 0.0)
        out = jnp.where(size >= s * 0.75, s, out)
        out = jnp.where(size >= s * 1.25, s * 1.5, out)
        out = jnp.where(size >= s * 1.75, s * 2.0, out)
        out = jnp.where(size >= s * 2.5, s * 3.0, out)
        out = jnp.where(size >= s * 3.5, s * 4.0, out)
        out = jnp.where(size >= s * 5.0, s * 6.0, out)
        held_ref[pl.ds(pl.multiple_of(j * SLOTS, SLOTS), SLOTS), :] = jnp.where(values < 0, -out, out)
        return 0

    lax.fori_loop(0, HALF, encode, 0, unroll=2)

    def deal(o, _):
        out_ref[o] = held_ref[pl.ds(slot_ref[o], HALF, stride=SLOTS), :].astype(BF)
        return 0

    lax.fori_loop(0, SLOTS, deal, 0, unroll=8)


def encode(placement, master):
    return pl.pallas_call(
        encode_kernel,
        name="encode",
        out_shape=jax.ShapeDtypeStruct((SLOTS, HALF, 128), BF),
        in_specs=[pl.BlockSpec(memory_space=SMEM), pl.BlockSpec(memory_space=VMEM)],
        out_specs=pl.BlockSpec(memory_space=VMEM),
        scratch_shapes=[pltpu.SMEM((SLOTS,), jnp.int32), pltpu.VMEM((HALF * SLOTS, 128), F32)],
        compiler_params=params(24),
        cost_estimate=pl.CostEstimate(flops=10**9, bytes_accessed=4 * 10**6, transcendentals=0),
    )(placement, master)


GROUP = 16


def assemble_kernel(got_ref, out_ref, held_ref):
    low = iota((HALF, 128), 1) < ROWS
    for i in range(GROUP):
        for h in range(2):
            first = got_ref[2 * h, i].astype(F32)
            second = got_ref[2 * h + 1, i].astype(F32)
            upper = jnp.where(low, first, pltpu.roll(second, ROWS, 1))
            lower = jnp.where(low, pltpu.roll(first, ROWS, 1), second)
            lanes = slice(128 * h, 128 * h + 128)
            held_ref[COLS * i : COLS * i + HALF, lanes] = upper
            held_ref[COLS * i + HALF : COLS * (i + 1), lanes] = lower[: COLS - HALF]
    out_ref[...] = held_ref[...].astype(BF)


def assemble(got):
    rows = GROUP * COLS
    return pl.pallas_call(
        assemble_kernel,
        name="assemble",
        grid=(SLOTS // GROUP,),
        out_shape=jax.ShapeDtypeStruct((D, 4 * ROWS), BF),
        in_specs=[pl.BlockSpec((4, GROUP, HALF, 128), lambda g: (0, g, 0, 0))],
        out_specs=pl.BlockSpec((rows, 4 * ROWS), lambda g: (g, 0)),
        scratch_shapes=[pltpu.VMEM((rows, 4 * ROWS), F32)],
        compiler_params=params(24),
        cost_estimate=pl.CostEstimate(flops=10**9, bytes_accessed=4 * 10**6, transcendentals=0),
    )(got)


def expert_kernel(
    place_ref,
    hidden_ref,
    routes_ref,
    gain_ref,
    router_ref,
    gate_up_ref,
    down_ref,
    out_ref,
    rows_ref,
    merge_ref,
    slot_ref,
    normed_ref,
):
    invert(place_ref, slot_ref)
    plane = lax.axis_index("x") * 2 + lax.axis_index("yl")
    depth = lax.axis_index("z")
    owner = plane * DEPTH + depth
    mine = slot_ref[owner] // DEPTH

    total = jnp.zeros((1, TOK), F32)
    step = 576
    for at in range(0, D, step):
        part = hidden_ref[at : at + step, :].astype(F32)
        total = total + jnp.sum(part * part, axis=0, keepdims=True)
    factor = lax.rsqrt(total * (1.0 / D) + 1e-05)
    ones = jnp.ones((128, TOK), BF)
    for at in range(0, D, 128):
        size = min(128, D - at)
        gain = gain_ref[:, at : at + size].astype(F32)
        diagonal = jnp.where(
            iota((size, size), 0) == iota((size, size), 1), jnp.broadcast_to(gain, (size, size)), 0.0
        ).astype(BF)
        column = nn(diagonal, ones[:size])
        part = hidden_ref[at : at + size, :].astype(F32)
        normed_ref[at : at + size, :] = (part * factor * column).astype(BF)

    rep = lax.axis_index("yh") * 2 + lax.axis_index("c")
    logits = jnp.zeros((8, TOK), F32)
    for d in range(4):
        start = pl.multiple_of((rep ^ d) * 720, 720)
        logits = logits + nn(router_ref[d], normed_ref[pl.ds(start, 720), :])
    which = iota((8, TOK), 0)
    chosen = jnp.zeros((8, TOK), F32)
    for k in range(4):
        chosen = jnp.where(which == routes_ref[k : k + 1, :], 1.0, chosen)
    powered = jnp.where(chosen > 0, jnp.exp(logits), 0.0)
    weights = powered / jnp.sum(powered, axis=0, keepdims=True)
    weight = jnp.sum(jnp.where(which == mine, weights, 0.0), axis=0, keepdims=True)
    weight = jnp.transpose(jnp.broadcast_to(weight, (8, TOK)))[:, 0:1]

    earlier = (
        ((iota((TOK, TOK), 0) // 4) == (iota((TOK, TOK), 1) // 4))
        & (iota((TOK, TOK), 0) < iota((TOK, TOK), 1))
    ).astype(F32).astype(BF)
    rank = nn(chosen.astype(BF), earlier)
    turn = jnp.where(chosen > 0, rank, -1.0)
    my_turn = jnp.sum(jnp.where(which == mine, turn, 0.0), axis=0, keepdims=True)
    packed = iota((PACKED, TOK), 0)
    pack = (
        ((iota((PACKED, TOK), 1) // 4) == (packed // CAP))
        & (jnp.broadcast_to(my_turn, (PACKED, TOK)) == (packed % CAP).astype(F32))
    ).astype(F32).astype(BF)

    projected = tn(normed_ref[...], gate_up_ref[...])
    gate = projected[:, :HID]
    up = projected[:, HID:]
    activated = (weight * gate * jax.nn.sigmoid(1.702 * gate) * (up + 1.0)).astype(BF)
    activated = nn(pack, activated).astype(BF)
    for at in range(0, D, 640):
        size = min(640, D - at)
        out_ref[:, at : at + size] = nt(activated, down_ref[at : at + size, :]).astype(BF)

    own = (iota((8, TOK), 1) == iota((8, TOK), 0) + owner * 4).astype(F32).astype(BF)
    for at in range(0, D, 640):
        size = min(640, D - at)
        rows_ref[:, at : at + size] = nt(own, hidden_ref[at : at + size, :])[:4]

    pick = (iota((TOK, 128), 0) == iota((TOK, 128), 1) + plane * 32).astype(F32).astype(BF)
    turns = nn(turn.astype(BF), pick)
    per = 4 * DEPTH // 4 * CAP
    block = iota((per, 128), 0)
    parts = []
    for p in range(PLANE):
        expert = slot_ref[p * DEPTH + depth] // DEPTH
        theirs = jnp.sum(jnp.where(iota((8, 128), 0) == expert, turns, 0.0), axis=0, keepdims=True)
        parts.append(
            (
                ((iota((per, 128), 1) // 4) == (block // CAP))
                & (jnp.broadcast_to(theirs, (per, 128)) == (block % CAP).astype(F32))
            ).astype(F32)
        )
    merge_ref[...] = jnp.transpose(jnp.concatenate(parts, axis=0))[:32].astype(BF)


def expert_terms(placement, hidden, routes, gain, router, gate_up, down):
    return pl.pallas_call(
        expert_kernel,
        name="expert_terms",
        out_shape=(
            jax.ShapeDtypeStruct((PACKED, D), BF),
            jax.ShapeDtypeStruct((4, D), F32),
            jax.ShapeDtypeStruct((32, PACKED), BF),
        ),
        in_specs=[pl.BlockSpec(memory_space=SMEM)] + [pl.BlockSpec(memory_space=VMEM)] * 6,
        out_specs=(pl.BlockSpec(memory_space=VMEM),) * 3,
        scratch_shapes=[pltpu.SMEM((SLOTS,), jnp.int32), pltpu.VMEM((D, TOK), BF)],
        compiler_params=params(40),
        cost_estimate=pl.CostEstimate(flops=4 * 10**9, bytes_accessed=8 * 10**6, transcendentals=0),
    )(placement, hidden, routes, gain, router, gate_up, down)


def merge_kernel(merge_ref, got_ref, out_ref):
    for at in range(0, D, 640):
        size = min(640, D - at)
        part = nn(merge_ref[...], got_ref[:, at : at + size]).astype(BF)
        for z in range(DEPTH):
            out_ref[z, :, at : at + size] = part[4 * z : 4 * z + 4]


def merge_plane(merge, got):
    return pl.pallas_call(
        merge_kernel,
        name="merge_plane",
        out_shape=jax.ShapeDtypeStruct((DEPTH, 4, D), BF),
        in_specs=[pl.BlockSpec(memory_space=VMEM)] * 2,
        out_specs=pl.BlockSpec(memory_space=VMEM),
        compiler_params=params(16),
        cost_estimate=pl.CostEstimate(flops=10**8, bytes_accessed=10**6, transcendentals=0),
    )(merge, got)


def on_device(
    master, placement, resident_gate_up, resident_down, hidden, routes, norm_gain, router
):
    router_rows = router.T
    routers = [router_rows]
    for d in range(1, 4):
        pairs = [(r, r ^ d) for r in range(4)]
        routers.append(lax.ppermute(router_rows, REP, pairs))

    chunks = encode(placement, jnp.transpose(master, (2, 0, 1)))
    chunks = lax.all_to_all(chunks, FSDP, split_axis=0, concat_axis=0, tiled=True)
    chunks = lax.all_gather(chunks, REP, axis=0, tiled=False)

    terms, rows, merge = expert_terms(
        placement,
        hidden[0].T,
        routes[0].T,
        norm_gain[None],
        jnp.stack(routers),
        resident_gate_up[0],
        resident_down[0].T,
    )
    terms = lax.all_to_all(terms, ("x", "yl"), split_axis=0, concat_axis=0, tiled=True)
    terms = merge_plane(merge, terms)
    terms = lax.all_to_all(terms, "z", split_axis=0, concat_axis=0, tiled=True)
    decoded = (rows + jnp.sum(terms.astype(F32), axis=0)).astype(BF)
    refreshed = assemble(chunks).T
    return (refreshed[None], decoded[None])


def solution(mesh):
    cut = Mesh(mesh.devices.reshape(4, 2, 8, 2, 2), ("x", "yl", "z", "yh", "c"))
    placed = (
        P(None, REP, FSDP),
        P(),
        P(FSDP, None, None),
        P(FSDP, None, None),
        P(REP, None, None),
        P(REP, None, None),
        P(),
        P(REP, None),
    )
    return jax.shard_map(
        on_device,
        mesh=cut,
        in_specs=placed,
        out_specs=(P(FSDP, None, None), P(REP, FSDP, None)),
        check_vma=False,
    )
```

time: 727 us -> 99.5 us (0.14)
  waiting for transfers between devices: 610 us -> 12.1 us
  local copies, waits for them, and re-layouts: 37.1 us -> 6.94 us
  blocking collectives: 6.91 us -> 32 us
  other arithmetic: 20.5 us -> 0.72 us
  Pallas kernels: 0 us -> 16.1 us
  starting transfers between devices: 23.9 us -> 16.1 us
  matrix products: 7.61 us -> 0 us
    unnamed x3 -> x1, waiting for transfers between devices: 595 us -> 0.02 us
    all_to_all x0 -> x2, blocking collectives: none -> 32 us  [the longest x1 20.2 us: on_device(): lax.all_to_all(terms, ('x', 'yl'), split_axis=0, concat_axis=0, tiled=True)]
    pallas_call x0 -> x4, Pallas kernels: none -> 16.1 us  [the longest x1 9.54 us: encode(): pl.pallas_call(encode_kernel, name='encode', out_shape=jax.ShapeDtypeStru...]
    convert_element_type x7 -> x0, other arithmetic: 14.2 us -> none  [the longest x1 4.41 us: encode_blocks(): nearest_level(grouped * inverse[:, :, None, :]).astype(jnp.bfloat16)]
    all_to_all x2 -> x1, starting transfers between devices: 23.9 us -> 12.6 us  [on_device(): lax.all_to_all(chunks, FSDP, split_axis=0, concat_axis=0, tiled=True)]
    gather x6 -> x0, local copies, waits for them, and re-layouts: 10.8 us -> none  [the longest x4 6.91 us: on_device(): picked = jnp.take_along_axis(logits, chosen, axis=1)]
    dot_general x3 -> x0, matrix products: 7.61 us -> none  [the longest x1 3.39 us: on_device(): projected = jnp.dot(normed, gate_up, preferred_element_type=jnp.float32)]
    all_to_all x2 -> x1, waiting for transfers between devices: 14.8 us -> 7.84 us  [on_device(): lax.all_to_all(chunks, FSDP, split_axis=0, concat_axis=0, tiled=True)]
  transfers between devices with their start and end apart: 4 -> 5, of which waited for: 2 -> 3; matrix products, arithmetic and copies ran while one was open for 6% -> 1% of each run, Pallas kernels for 0% -> 4%
where the time goes in v1:
time: 99.5 us; the launch traced here: 98.1 us
  blocking collectives  32 us (32%)
  Pallas kernels  16.1 us (16%)
  starting transfers between devices  16.1 us (16%)
  between operations  14.1 us (14%)
  waiting for transfers between devices  12.1 us (12%)
  local copies, waits for them, and re-layouts  6.94 us (7%)
    all_to_all x1, blocking collectives, on_device(): lax.all_to_all(terms, ('x', 'yl'), split_axis=0, concat_axis=0, tiled=True)  20.2 us
    all_to_all x1, starting transfers between devices, on_device(): lax.all_to_all(chunks, FSDP, split_axis=0, concat_axis=0, tiled=True)  12.6 us
    all_to_all x1, blocking collectives, on_device(): terms = lax.all_to_all(terms, 'z', split_axis=0, concat_axis=0, tiled=True)  11.7 us
    pallas_call x1, Pallas kernels, encode(): pl.pallas_call(encode_kernel, name='encode', out_shape=jax.ShapeDtypeStru...  9.54 us
    all_to_all x1, waiting for transfers between devices, on_device(): lax.all_to_all(chunks, FSDP, split_axis=0, concat_axis=0, tiled=True)  7.84 us
    unnamed x22, local copies, waits for them, and re-layouts  6.93 us
    ppermute x3, waiting for transfers between devices, on_device(): routers.append(lax.ppermute(router_rows, REP, pairs))  4.24 us
    pallas_call x1, Pallas kernels, expert_terms(): pl.pallas_call(expert_kernel, name='expert_terms', out_shape=(jax.ShapeDt...  3.93 us
  transfers between devices with their start and end apart: 5, of which 3 were waited for; matrix products, arithmetic and copies ran while one was open for 1% of the time, Pallas kernels for 4%

profile of v1, /device:TPU:32, one launch (start us, length us, event | category | flops | bytes accessed | tf_op | source)
XLA Modules:
  0.0 98.1 jit_solution(3465583615039969557)
XLA Ops:
  7.2 0.0 copy-start.2
  7.2 1.4 %copy-done.2 = f32[64,64,45]{1,0,2:T(8,128)S(1)} copy-done((f32[64,64,45]{1,0,2:T(8,128)S(1)}, f32[64,64,45]{1,0,2:T(8,128)}, u32[]{:S(2)}) %copy-start.2) | copy-done | bytes 737304
  8.5 0.0 copy-start.6
  8.5 0.7 copy-done.6
  9.2 0.0 copy-start.9
  9.2 0.0 copy-start.10
  9.2 0.0 copy-start
  9.2 0.0 copy-start.5
  9.2 0.0 copy-start.7
  9.2 9.5 %encode.1 = bf16[64,24,128]{2,1,0:T(8,128)(2,1)} custom-call(s32[64]{0:T(128)S(1)} %copy-done.6, f32[45,64,64]{2,1,0:T(8,128)S(1)} %bitcast.29), custom_call_target="tpu_custom_call" | custom-call | flops 1000000000 | bytes 4000000 | tf_op jit(solution)/shard_map/encode/pallas_call | solution.py:97
  18.8 12.6 %all-to-all-start = ((bf16[64,24,128]{2,1,0:T(8,128)(2,1)}), bf16[64,24,128]{2,1,0:T(8,128)(2,1)S(1)}, u32[]{:S(2)}, u32[]{:S(2)}) async-start(bf16[64,24,128]{2,1,0:T(8,128)(2,1)} %encode.1), calls=%async_computation | async-start | bytes 786432 | tf_op jit(solution)/shard_map/all_to_all | solution.py:283
  31.4 0.0 all-gather.3.cloned.1.call-start
  31.4 0.0 copy-done.9
  31.4 0.1 collective-permute-start
  31.5 3.0 %collective-permute-start.1 = (bf16[8,720]{1,0:T(8,128)(2,1)S(1)}, bf16[8,720]{1,0:T(8,128)(2,1)S(1)}, u32[]{:S(2)}, u32[]{:S(2)}) collective-permute-start(bf16[8,720]{1,0:T(8,128)(2,1)S(1)} %bitcast.34), channel_id=1, source_target_pairs={{0,2},{1,3},{2,0},{3,1},{4,6},{5,7},{6,4},{7,5},{8,10},{9,11},{10,... | collective-permute-start | bytes 34568 | tf_op jit(solution)/shard_map/ppermute | solution.py:280
  34.5 0.4 collective-permute-start.2
  34.9 0.0 copy-done.10
  34.9 0.0 collective-permute-done
  34.9 1.9 %collective-permute-done.1 = bf16[8,720]{1,0:T(8,128)(2,1)S(1)} collective-permute-done((bf16[8,720]{1,0:T(8,128)(2,1)S(1)}, bf16[8,720]{1,0:T(8,128)(2,1)S(1)}, u32[]{:S(2)}, u32[]{:S(2)}) %collective-permute-start.1) | collective-permute-done | bytes 11552 | tf_op jit(solution)/shard_map/ppermute | solution.py:280
  36.8 2.3 %collective-permute-done.2 = bf16[8,720]{1,0:T(8,128)(2,1)S(1)} collective-permute-done((bf16[8,720]{1,0:T(8,128)(2,1)S(1)}, bf16[8,720]{1,0:T(8,128)(2,1)S(1)}, u32[]{:S(2)}, u32[]{:S(2)}) %collective-permute-start.2) | collective-permute-done | bytes 11552 | tf_op jit(solution)/shard_map/ppermute | solution.py:280
  39.2 7.8 %all-to-all-done = bf16[64,24,128]{2,1,0:T(8,128)(2,1)S(1)} async-done(((bf16[64,24,128]{2,1,0:T(8,128)(2,1)}), bf16[64,24,128]{2,1,0:T(8,128)(2,1)S(1)}, u32[]{:S(2)}, u32[]{:S(2)}) %all-to-all-start) | async-done | bytes 393248 | tf_op jit(solution)/shard_map/all_to_all | solution.py:283
  47.0 0.0 copy-start.8
  47.0 0.7 copy-done.8
  47.8 0.0 all-gather.3.cloned.1.call-update
  47.8 0.0 copy-done
  47.8 0.0 copy-done.5
  47.8 0.0 copy-done.7
  47.8 0.0 copy-start.3
  47.8 1.4 %copy-done.3 = bf16[1,256,2880]{1,2,0:T(8,128)(2,1)S(1)} copy-done((bf16[1,256,2880]{1,2,0:T(8,128)(2,1)S(1)}, bf16[1,256,2880]{1,2,0:T(8,128)(2,1)}, u32[]{:S(2)}) %copy-start.3) | copy-done | bytes 1474584
  49.2 0.0 copy-start.4
  49.2 1.4 %copy-done.4 = bf16[1,256,2880]{1,2,0:T(8,128)(2,1)S(1)} copy-done((bf16[1,256,2880]{1,2,0:T(8,128)(2,1)S(1)}, bf16[1,256,2880]{1,2,0:T(8,128)(2,1)}, u32[]{:S(2)}) %copy-start.4) | copy-done | bytes 1474584
  50.6 3.9 %expert_terms.1 = (bf16[192,2880]{1,0:T(8,128)(2,1)S(1)}, f32[4,2880]{1,0:T(4,128)S(1)}, bf16[32,192]{1,0:T(8,128)(2,1)S(1)}) custom-call(s32[64]{0:T(128)S(1)} %copy-done.7, bf16[2880,256]{1,0:T(8,128)(2,1)S(1)} %bitcast.30, s32[4,256]{1,0:T(4,128)S(1)} %bitcast.32, bf16[1,2880]{1,0:T(2,128)(2,1)S(1)} %broadcast_in_dim.10.gain_ref, ...), custom_call_target="tpu_custom_call" | custom-call | flops 4000000000 | bytes 8000000 | tf_op jit(solution)/shard_map/expert_terms/pallas_call | solution.py:237
  54.5 20.2 %all_to_all.21 = bf16[8,24,2880]{2,1,0:T(8,128)(2,1)S(1)} all-to-all(bf16[8,24,2880]{2,1,0:T(8,128)(2,1)S(1)} %bitcast.26), channel_id=1, replica_groups=mesh['x'=4,'yl'=2,'z'=8,'yh'=2,'c'=2] {'x','yl'}, dimensions={0} | all-to-all | bytes 2211840 | tf_op jit(solution)/shard_map/all_to_all | solution.py:295
  74.7 0.4 merge_plane.1
  75.1 11.7 %all_to_all.22 = bf16[8,4,2880]{2,1,0:T(4,128)(2,1)S(1)} all-to-all(bf16[8,4,2880]{2,1,0:T(4,128)(2,1)S(1)} %merge_plane.1), channel_id=1, replica_groups=mesh['x'=4,'yl'=2,'z'=8,'yh'=2,'c'=2] {'z'}, dimensions={0} | all-to-all | bytes 368640 | tf_op jit(solution)/shard_map/all_to_all | solution.py:297
  86.8 0.1 convert_reduce_fusion
  86.9 0.6 fusion
  87.5 0.0 all-gather.3.cloned.1.call-done
  87.5 0.0 copy-start.1
  87.5 1.4 %copy-done.1 = bf16[256,24,128]{2,1,0:T(8,128)(2,1)S(1)} copy-done((bf16[256,24,128]{2,1,0:T(8,128)(2,1)S(1)}, bf16[256,24,128]{2,1,0:T(8,128)(2,1)}, u32[]{:S(2)}) %copy-start.1) | copy-done | bytes 1572888
  88.9 2.3 %assemble.1 = bf16[2880,256]{1,0:T(8,128)(2,1)} custom-call(bf16[4,64,24,128]{3,2,1,0:T(8,128)(2,1)S(1)} %bitcast.28), custom_call_target="tpu_custom_call" | custom-call | flops 1000000000 | bytes 4000000 | tf_op jit(solution)/shard_map/assemble/pallas_call | solution.py:128
  (2 shorter events, 0.0 us)
Async XLA Ops:
  7.2 1.4 %copy-start.2 = (f32[64,64,45]{1,0,2:T(8,128)S(1)}, f32[64,64,45]{1,0,2:T(8,128)}, u32[]{:S(2)}) copy-start(f32[64,64,45]{1,0,2:T(8,128)} %param.8) | copy-start | bytes 2211844
  8.5 0.7 copy-start.6
  9.2 22.2 %copy-start.9 = (bf16[720,8]{0,1:T(8,128)(2,1)S(1)}, bf16[720,8]{0,1:T(8,128)(2,1)}, u32[]{:S(2)}) copy-start(bf16[720,8]{0,1:T(8,128)(2,1)} %param.15) | copy-start | bytes 34564
  9.2 25.7 %copy-start.10 = (bf16[2880]{0:T(1024)(128)(2,1)S(1)}, bf16[2880]{0:T(1024)(128)(2,1)}, u32[]{:S(2)}) copy-start(bf16[2880]{0:T(1024)(128)(2,1)} %param.14) | copy-start | bytes 17284
  9.2 38.6 %copy-start = (bf16[1,2880,512]{2,1,0:T(8,128)(2,1)S(1)}, bf16[1,2880,512]{2,1,0:T(8,128)(2,1)}, u32[]{:S(2)}) copy-start(bf16[1,2880,512]{2,1,0:T(8,128)(2,1)} %param.10) | copy-start | bytes 8847364
  9.2 38.6 %copy-start.5 = (s32[1,256,4]{1,2,0:T(4,128)S(1)}, s32[1,256,4]{1,2,0:T(4,128)}, u32[]{:S(2)}) copy-start(s32[1,256,4]{1,2,0:T(4,128)} %param.13) | copy-start | bytes 12292
  9.2 38.6 %copy-start.7 = (s32[64]{0:T(128)S(1)}, s32[64]{0:T(128)}, u32[]{:S(2)}) copy-start(s32[64]{0:T(128)} %place_ref.3) | copy-start | bytes 772
  18.8 28.3 %all-to-all-start = ((bf16[64,24,128]{2,1,0:T(8,128)(2,1)}), bf16[64,24,128]{2,1,0:T(8,128)(2,1)S(1)}, u32[]{:S(2)}, u32[]{:S(2)}) async-start(bf16[64,24,128]{2,1,0:T(8,128)(2,1)} %encode.1), calls=%async_computation | async-start | bytes 786432 | tf_op jit(solution)/shard_map/all_to_all | solution.py:283
  31.4 56.2 %all-gather.3.cloned.1.call-start = ((), (), s32[]{:S(2)}) async-start(), calls=%async_computation.3 | async-start | bytes 1966080 | tf_op jit(solution)/shard_map/all_gather | solution.py:284
  31.4 3.5 %collective-permute-start = (bf16[8,720]{1,0:T(8,128)(2,1)S(1)}, bf16[8,720]{1,0:T(8,128)(2,1)S(1)}, u32[]{:S(2)}, u32[]{:S(2)}) collective-permute-start(bf16[8,720]{1,0:T(8,128)(2,1)S(1)} %bitcast.33), channel_id=1, source_target_pairs={{0,1},{1,0},{2,3},{3,2},{4,5},{5,4},{6,7},{7,6},{8,9},{9,8},{10,11... | collective-permute-start | bytes 34568 | tf_op jit(solution)/shard_map/ppermute | solution.py:280
  31.5 5.3 %collective-permute-start.1 = (bf16[8,720]{1,0:T(8,128)(2,1)S(1)}, bf16[8,720]{1,0:T(8,128)(2,1)S(1)}, u32[]{:S(2)}, u32[]{:S(2)}) collective-permute-start(bf16[8,720]{1,0:T(8,128)(2,1)S(1)} %bitcast.34), channel_id=1, source_target_pairs={{0,2},{1,3},{2,0},{3,1},{4,6},{5,7},{6,4},{7,5},{8,10},{9,11},{10,... | collective-permute-start | bytes 34568 | tf_op jit(solution)/shard_map/ppermute | solution.py:280
  34.5 4.6 %collective-permute-start.2 = (bf16[8,720]{1,0:T(8,128)(2,1)S(1)}, bf16[8,720]{1,0:T(8,128)(2,1)S(1)}, u32[]{:S(2)}, u32[]{:S(2)}) collective-permute-start(bf16[8,720]{1,0:T(8,128)(2,1)S(1)} %bitcast.35), channel_id=1, source_target_pairs={{0,3},{1,2},{2,1},{3,0},{4,7},{5,6},{6,5},{7,4},{8,11},{9,10},{10,... | collective-permute-start | bytes 34568 | tf_op jit(solution)/shard_map/ppermute | solution.py:280
  47.0 0.7 copy-start.8
  47.8 1.4 %copy-start.3 = (bf16[1,256,2880]{1,2,0:T(8,128)(2,1)S(1)}, bf16[1,256,2880]{1,2,0:T(8,128)(2,1)}, u32[]{:S(2)}) copy-start(bf16[1,256,2880]{1,2,0:T(8,128)(2,1)} %param.12) | copy-start | bytes 4423684
  49.2 1.4 %copy-start.4 = (bf16[1,256,2880]{1,2,0:T(8,128)(2,1)S(1)}, bf16[1,256,2880]{1,2,0:T(8,128)(2,1)}, u32[]{:S(2)}) copy-start(bf16[1,256,2880]{1,2,0:T(8,128)(2,1)} %param.11) | copy-start | bytes 4423684
  87.5 1.4 %copy-start.1 = (bf16[256,24,128]{2,1,0:T(8,128)(2,1)S(1)}, bf16[256,24,128]{2,1,0:T(8,128)(2,1)}, u32[]{:S(2)}) copy-start(bf16[256,24,128]{2,1,0:T(8,128)(2,1)} %all-gather.3.cloned.1.call-done) | copy-start | bytes 4718596
Sparse Core Ops, SparseCore 0:
  47.9 33.6 all-gather.2

commit v2 on v1

--- a/solution.py
+++ b/solution.py
@@ -1,5 +1,3 @@
-import functools
-
 import jax
 import jax.numpy as jnp
 from jax import lax
@@ -57,34 +55,54 @@
     lax.fori_loop(0, SLOTS, step, 0, unroll=8)
 
 
-def encode_kernel(place_ref, master_ref, out_ref, slot_ref, held_ref):
+PAIRS = 12
+
+
+def round_blocks(values, spread):
+    size = jnp.abs(values)
+    top = size
+    for shift in (1, 2, 4, 8, 16):
+        top = jnp.maximum(top, pltpu.roll(top, shift, 1))
+    top = jnp.maximum(top, 6.0 * 2.0**-40)
+    lead = top * (2.0**23 + 1.0)
+    lead = jnp.abs(lead - lead * (1.0 - 2.0**-24))
+    scale = jnp.where(top > lead * 1.5, lead * 0.5, lead * 0.25)
+    s = nn(scale.astype(BF), spread)
+    out = jnp.where(size >= s * 0.25, s * 0.5, 0.0)
+    out = jnp.where(size >= s * 0.75, s, out)
+    out = jnp.where(size >= s * 1.25, s * 1.5, out)
+    out = jnp.where(size >= s * 1.75, s * 2.0, out)
+    out = jnp.where(size >= s * 2.5, s * 3.0, out)
+    out = jnp.where(size >= s * 3.5, s * 4.0, out)
+    out = jnp.where(size >= s * 5.0, s * 6.0, out)
+    return jnp.where(values < 0, -out, out)
+
+
+def encode_kernel(place_ref, master_ref, out_ref, slot_ref, held_ref, raw_ref, sems):
+    copies = []
+    for g in range(HALF // PAIRS):
+        at = g * PAIRS
+        wide = min(PAIRS, COLS - HALF - at)
+        for n, (start, size) in enumerate(((at, PAIRS), (HALF + at, wide))):
+            part = pl.ds(start, size)
+            copy = pltpu.make_async_copy(master_ref.at[part], raw_ref.at[part], sems.at[2 * g + n])
+            copy.start()
+            copies.append(copy)
     invert(place_ref, slot_ref)
     spread = (iota((128, 128), 0) == (iota((128, 128), 1) // 32) * 32 + 31).astype(F32).astype(BF)
-
-    def encode(j, _):
-        low = master_ref[j]
-        high = master_ref[jnp.minimum(j + HALF, COLS - 1)]
+    for g in range(HALF // PAIRS):
+        at = g * PAIRS
+        wide = min(PAIRS, COLS - HALF - at)
+        copies[2 * g].wait()
+        copies[2 * g + 1].wait()
+        low = raw_ref[at : at + PAIRS]
+        high = raw_ref[HALF + at : HALF + at + wide]
+        if wide < PAIRS:
+            high = jnp.concatenate([high, low[wide:]], axis=0)
+        low = low.reshape(PAIRS * SLOTS, ROWS)
+        high = high.reshape(PAIRS * SLOTS, ROWS)
         values = jnp.concatenate([low, high], axis=1)
-        size = jnp.abs(values)
-        top = size
-        for shift in (1, 2, 4, 8, 16):
-            top = jnp.maximum(top, pltpu.roll(top, shift, 1))
-        top = jnp.maximum(top, 6.0 * 2.0**-40)
-        lead = top * (2.0**23 + 1.0)
-        lead = jnp.abs(lead - lead * (1.0 - 2.0**-24))
-        scale = jnp.where(top > lead * 1.5, lead * 0.5, lead * 0.25)
-        s = nn(scale.astype(BF), spread)
-        out = jnp.where(size >= s * 0.25, s * 0.5, 0.0)
-        out = jnp.where(size >= s * 0.75, s, out)
-        out = jnp.where(size >= s * 1.25, s * 1.5, out)
-        out = jnp.where(size >= s * 1.75, s * 2.0, out)
-        out = jnp.where(size >= s * 2.5, s * 3.0, out)
-        out = jnp.where(size >= s * 3.5, s * 4.0, out)
-        out = jnp.where(size >= s * 5.0, s * 6.0, out)
-        held_ref[pl.ds(pl.multiple_of(j * SLOTS, SLOTS), SLOTS), :] = jnp.where(values < 0, -out, out)
-        return 0
-
-    lax.fori_loop(0, HALF, encode, 0, unroll=2)
+        held_ref[at * SLOTS : (at + PAIRS) * SLOTS, :] = round_blocks(values, spread)
 
     def deal(o, _):
         out_ref[o] = held_ref[pl.ds(slot_ref[o], HALF, stride=SLOTS), :].astype(BF)
@@ -98,10 +116,15 @@
         encode_kernel,
         name="encode",
         out_shape=jax.ShapeDtypeStruct((SLOTS, HALF, 128), BF),
-        in_specs=[pl.BlockSpec(memory_space=SMEM), pl.BlockSpec(memory_space=VMEM)],
+        in_specs=[pl.BlockSpec(memory_space=SMEM), pl.BlockSpec(memory_space=pl.ANY)],
         out_specs=pl.BlockSpec(memory_space=VMEM),
-        scratch_shapes=[pltpu.SMEM((SLOTS,), jnp.int32), pltpu.VMEM((HALF * SLOTS, 128), F32)],
-        compiler_params=params(24),
+        scratch_shapes=[
+            pltpu.SMEM((SLOTS,), jnp.int32),
+            VMEM((HALF * SLOTS, 128), F32),
+            VMEM((COLS, SLOTS, ROWS), F32),
+            pltpu.SemaphoreType.DMA((2 * HALF // PAIRS,)),
+        ],
+        compiler_params=params(60),
         cost_estimate=pl.CostEstimate(flops=10**9, bytes_accessed=4 * 10**6, transcendentals=0),
     )(placement, master)
 
@@ -109,12 +132,17 @@
 GROUP = 16
 
 
-def assemble_kernel(got_ref, out_ref, held_ref):
+def assemble_kernel(own_ref, across_ref, core_ref, both_ref, out_ref, held_ref):
     low = iota((HALF, 128), 1) < ROWS
+    half = lax.axis_index("yh")
+    core = lax.axis_index("c")
     for i in range(GROUP):
+        here = (own_ref[i].astype(F32), core_ref[i].astype(F32))
+        there = (across_ref[i].astype(F32), both_ref[i].astype(F32))
         for h in range(2):
-            first = got_ref[2 * h, i].astype(F32)
-            second = got_ref[2 * h + 1, i].astype(F32)
+            mine, other = (jnp.where(half == h, a, b) for a, b in zip(here, there))
+            first = jnp.where(core == 0, mine, other)
+            second = jnp.where(core == 0, other, mine)
             upper = jnp.where(low, first, pltpu.roll(second, ROWS, 1))
             lower = jnp.where(low, pltpu.roll(first, ROWS, 1), second)
             lanes = slice(128 * h, 128 * h + 128)
@@ -123,19 +151,19 @@
     out_ref[...] = held_ref[...].astype(BF)
 
 
-def assemble(got):
+def assemble(own, across, core, both):
     rows = GROUP * COLS
     return pl.pallas_call(
         assemble_kernel,
         name="assemble",
         grid=(SLOTS // GROUP,),
         out_shape=jax.ShapeDtypeStruct((D, 4 * ROWS), BF),
-        in_specs=[pl.BlockSpec((4, GROUP, HALF, 128), lambda g: (0, g, 0, 0))],
+        in_specs=[pl.BlockSpec((GROUP, HALF, 128), lambda g: (g, 0, 0))] * 4,
         out_specs=pl.BlockSpec((rows, 4 * ROWS), lambda g: (g, 0)),
-        scratch_shapes=[pltpu.VMEM((rows, 4 * ROWS), F32)],
+        scratch_shapes=[VMEM((rows, 4 * ROWS), F32)],
         compiler_params=params(24),
         cost_estimate=pl.CostEstimate(flops=10**9, bytes_accessed=4 * 10**6, transcendentals=0),
-    )(got)
+    )(own, across, core, both)
 
 
 def expert_kernel(
@@ -281,7 +309,6 @@
 
     chunks = encode(placement, jnp.transpose(master, (2, 0, 1)))
     chunks = lax.all_to_all(chunks, FSDP, split_axis=0, concat_axis=0, tiled=True)
-    chunks = lax.all_gather(chunks, REP, axis=0, tiled=False)
 
     terms, rows, merge = expert_terms(
         placement,
@@ -292,11 +319,15 @@
         resident_gate_up[0],
         resident_down[0].T,
     )
+    chunks, terms = lax.optimization_barrier((chunks, terms))
+    across = lax.ppermute(chunks, "yh", ((0, 1), (1, 0)))
+    core = lax.ppermute(chunks, "c", ((0, 1), (1, 0)))
+    both = lax.ppermute(across, "c", ((0, 1), (1, 0)))
     terms = lax.all_to_all(terms, ("x", "yl"), split_axis=0, concat_axis=0, tiled=True)
     terms = merge_plane(merge, terms)
     terms = lax.all_to_all(terms, "z", split_axis=0, concat_axis=0, tiled=True)
     decoded = (rows + jnp.sum(terms.astype(F32), axis=0)).astype(BF)
-    refreshed = assemble(chunks).T
+    refreshed = assemble(chunks, across, core, both).T
     return (refreshed[None], decoded[None])
 
 

time: 99.5 us -> 84.4 us (0.85)
  the two profiles are of different devices: /device:TPU:32 before, /device:TPU:1 now
where the time goes in v2:
time: 84.4 us; the launch traced here: 84 us
  waiting for transfers between devices  34.6 us (41%)
  starting transfers between devices  30.9 us (37%)
  Pallas kernels  13.8 us (16%)
  local copies, waits for them, and re-layouts  3.23 us (4%)
    ppermute x1, waiting for transfers between devices, on_device(): across = lax.ppermute(chunks, 'yh', ((0, 1), (1, 0)))  21.6 us
    all_to_all x1, starting transfers between devices, on_device(): lax.all_to_all(chunks, FSDP, split_axis=0, concat_axis=0, tiled=True)  13.5 us
    all_to_all x1, waiting for transfers between devices, on_device(): terms = lax.all_to_all(terms, 'z', split_axis=0, concat_axis=0, tiled=True)  8.17 us
    all_to_all x1, starting transfers between devices, on_device(): terms = lax.all_to_all(terms, 'z', split_axis=0, concat_axis=0, tiled=True)  6.12 us
    pallas_call x1, Pallas kernels, encode(): pl.pallas_call(encode_kernel, name='encode', out_shape=jax.ShapeDtypeStru...  5.77 us
    ppermute x3, waiting for transfers between devices, on_device(): routers.append(lax.ppermute(router_rows, REP, pairs))  4.82 us
    pallas_call x1, Pallas kernels, expert_terms(): pl.pallas_call(expert_kernel, name='expert_terms', out_shape=(jax.ShapeDt...  4.72 us
    all_to_all x1, starting transfers between devices, on_device(): lax.all_to_all(terms, ('x', 'yl'), split_axis=0, concat_axis=0, tiled=True)  4.72 us
  transfers between devices with their start and end apart: 9, of which 4 were waited for; matrix products, arithmetic and copies ran while one was open for 0% of the time, Pallas kernels for 10%

profile of v2, /device:TPU:1, one launch (start us, length us, event | category | flops | bytes accessed | tf_op | source)
XLA Modules:
  0.0 84.0 jit_solution(11520665616093463133)
XLA Ops:
  0.6 0.0 copy-start.5
  0.6 0.0 copy-start.6
  0.7 0.0 copy-start.1
  0.7 0.0 copy-start.3
  0.7 0.0 copy-start.4
  0.7 5.8 %encode.1 = bf16[64,24,128]{2,1,0:T(8,128)(2,1)} custom-call(s32[64]{0:T(128)} %place_ref.3, f32[45,64,64]{2,1,0:T(8,128)} %bitcast.36), custom_call_target="tpu_custom_call" | custom-call | flops 1000000000 | bytes 4000000 | tf_op jit(solution)/shard_map/encode/pallas_call | solution.py:115
  6.5 13.5 %all-to-all-start = ((bf16[64,24,128]{2,1,0:T(8,128)(2,1)}), bf16[64,24,128]{2,1,0:T(8,128)(2,1)S(1)}, u32[]{:S(2)}, u32[]{:S(2)}) async-start(bf16[64,24,128]{2,1,0:T(8,128)(2,1)} %encode.1), calls=%async_computation | async-start | bytes 786432 | tf_op jit(solution)/shard_map/all_to_all | solution.py:311
  20.0 0.0 copy-done.5
  20.0 2.7 %collective-permute-start.1 = (bf16[8,720]{1,0:T(8,128)(2,1)S(1)}, bf16[8,720]{1,0:T(8,128)(2,1)S(1)}, u32[]{:S(2)}, u32[]{:S(2)}) collective-permute-start(bf16[8,720]{1,0:T(8,128)(2,1)S(1)} %bitcast.29), channel_id=1, source_target_pairs={{0,2},{1,3},{2,0},{3,1},{4,6},{5,7},{6,4},{7,5},{8,10},{9,11},{10,... | collective-permute-start | bytes 34568 | tf_op jit(solution)/shard_map/ppermute | solution.py:308
  22.7 1.2 %collective-permute-start = (bf16[8,720]{1,0:T(8,128)(2,1)S(1)}, bf16[8,720]{1,0:T(8,128)(2,1)S(1)}, u32[]{:S(2)}, u32[]{:S(2)}) collective-permute-start(bf16[8,720]{1,0:T(8,128)(2,1)S(1)} %bitcast.30), channel_id=1, source_target_pairs={{0,1},{1,0},{2,3},{3,2},{4,5},{5,4},{6,7},{7,6},{8,9},{9,8},{10,11... | collective-permute-start | bytes 34568 | tf_op jit(solution)/shard_map/ppermute | solution.py:308
  23.9 0.2 collective-permute-start.2
  24.2 0.0 copy-done.6
  24.2 0.0 collective-permute-done.1
  24.2 0.6 collective-permute-done
  24.8 4.2 %collective-permute-done.2 = bf16[8,720]{1,0:T(8,128)(2,1)S(1)} collective-permute-done((bf16[8,720]{1,0:T(8,128)(2,1)S(1)}, bf16[8,720]{1,0:T(8,128)(2,1)S(1)}, u32[]{:S(2)}, u32[]{:S(2)}) %collective-permute-start.2) | collective-permute-done | bytes 11552 | tf_op jit(solution)/shard_map/ppermute | solution.py:308
  29.0 0.0 copy-done.1
  29.0 0.0 copy-done.3
  29.0 0.0 copy-done.4
  29.1 0.0 copy-start
  29.1 1.8 %copy-done = bf16[1,2880,512]{2,1,0:T(8,128)(2,1)S(1)} copy-done((bf16[1,2880,512]{2,1,0:T(8,128)(2,1)S(1)}, bf16[1,2880,512]{2,1,0:T(8,128)(2,1)}, u32[]{:S(2)}) %copy-start) | copy-done | bytes 2949144
  30.9 0.0 copy-start.2
  30.9 1.4 %copy-done.2 = bf16[1,256,2880]{1,2,0:T(8,128)(2,1)S(1)} copy-done((bf16[1,256,2880]{1,2,0:T(8,128)(2,1)S(1)}, bf16[1,256,2880]{1,2,0:T(8,128)(2,1)}, u32[]{:S(2)}) %copy-start.2) | copy-done | bytes 1474584
  32.3 4.7 %expert_terms.1 = (bf16[192,2880]{1,0:T(8,128)(2,1)}, f32[4,2880]{1,0:T(4,128)S(1)}, bf16[32,192]{1,0:T(8,128)(2,1)S(1)}) custom-call(s32[64]{0:T(128)S(1)} %copy-done.4, bf16[2880,256]{1,0:T(8,128)(2,1)S(1)} %bitcast.26, s32[4,256]{1,0:T(4,128)S(1)} %bitcast.28, bf16[1,2880]{1,0:T(2,128)(2,1)S(1)} %broadcast_in_dim.9.gain_ref, ...), custom_call_target="tpu_custom_call" | custom-call | flops 4000000000 | bytes 8000000 | tf_op jit(solution)/shard_map/expert_terms/pallas_call | solution.py:265
  37.0 0.0 all-to-all-done.own_ref
  37.0 4.7 %all-to-all-start.1 = ((bf16[8,24,2880]{2,1,0:T(8,128)(2,1)}), bf16[8,24,2880]{2,1,0:T(8,128)(2,1)S(1)}, u32[]{:S(2)}, u32[]{:S(2)}) async-start(bf16[8,24,2880]{2,1,0:T(8,128)(2,1)} %bitcast.15), calls=%async_computation.1 | async-start | bytes 2260992 | tf_op jit(solution)/shard_map/all_to_all | solution.py:326
  41.7 1.6 %collective-permute-start.3 = (bf16[64,24,128]{2,1,0:T(8,128)(2,1)S(1)}, bf16[64,24,128]{2,1,0:T(8,128)(2,1)S(1)}, u32[]{:S(2)}, u32[]{:S(2)}) collective-permute-start(bf16[64,24,128]{2,1,0:T(8,128)(2,1)S(1)} %all-to-all-done.own_ref), channel_id=1, source_target_pairs={{0,2},{2,0},{1,3},{3,1},{4,6},{6,4},{5,7},{7,5},{8,10},{10,8},{9,1... | collective-permute-start | bytes 1179656 | tf_op jit(solution)/shard_map/ppermute | solution.py:323
  43.3 0.2 collective-permute-start.4
  43.5 21.6 %collective-permute-done.3.across_ref = bf16[64,24,128]{2,1,0:T(8,128)(2,1)S(1)} collective-permute-done((bf16[64,24,128]{2,1,0:T(8,128)(2,1)S(1)}, bf16[64,24,128]{2,1,0:T(8,128)(2,1)S(1)}, u32[]{:S(2)}, u32[]{:S(2)}) %collective-permute-start.3) | collective-permute-done | bytes 393248 | tf_op jit(solution)/shard_map/ppermute | solution.py:323
  65.1 0.5 collective-permute-start.5
  65.7 0.0 all-to-all-done.1
  65.7 1.0 %merge_plane.1 = bf16[8,4,2880]{2,1,0:T(4,128)(2,1)} custom-call(bf16[32,192]{1,0:T(8,128)(2,1)S(1)} %get-tuple-element.10.merge_ref, bf16[192,2880]{1,0:T(8,128)(2,1)S(1)} %bitcast.24), custom_call_target="tpu_custom_call" | custom-call | flops 100000000 | bytes 1000000 | tf_op jit(solution)/shard_map/merge_plane/pallas_call | solution.py:290
  66.7 6.1 %all-to-all-start.2 = ((bf16[8,4,2880]{2,1,0:T(4,128)(2,1)}), bf16[8,4,2880]{2,1,0:T(4,128)(2,1)S(1)}, u32[]{:S(2)}, u32[]{:S(2)}) async-start(bf16[8,4,2880]{2,1,0:T(4,128)(2,1)} %merge_plane.1), calls=%async_computation.2 | async-start | bytes 376832 | tf_op jit(solution)/shard_map/all_to_all | solution.py:328
  72.8 0.0 collective-permute-done.4.core_ref
  72.8 0.0 collective-permute-done.5.both_ref
  72.8 2.3 %assemble.1 = bf16[2880,256]{1,0:T(8,128)(2,1)} custom-call(bf16[64,24,128]{2,1,0:T(8,128)(2,1)S(1)} %all-to-all-done.own_ref, bf16[64,24,128]{2,1,0:T(8,128)(2,1)S(1)} %collective-permute-done.3.across_ref, bf16[64,24,128]{2,1,0:T(8,128)(2,1)S(1)} %collective-permute-done.4.core_ref, bf16[64,24,128]{2,1,0:T(8,128)(2,1)S(1)} %collective-permute-done.5.both_ref), custom_call_target="tpu_custom_call" | custom-call | flops 1000000000 | bytes 4000000 | tf_op jit(solution)/shard_map/assemble/pallas_call | solution.py:156
  75.1 8.2 %all-to-all-done.2 = bf16[8,4,2880]{2,1,0:T(4,128)(2,1)S(1)} async-done(((bf16[8,4,2880]{2,1,0:T(4,128)(2,1)}), bf16[8,4,2880]{2,1,0:T(4,128)(2,1)S(1)}, u32[]{:S(2)}, u32[]{:S(2)}) %all-to-all-start.2) | async-done | bytes 184352 | tf_op jit(solution)/shard_map/all_to_all | solution.py:328
  83.3 0.1 convert_reduce_fusion
  83.4 0.6 fusion
  (2 shorter events, 0.0 us)
Async XLA Ops:
  0.6 19.3 %copy-start.5 = (bf16[720,8]{0,1:T(8,128)(2,1)S(1)}, bf16[720,8]{0,1:T(8,128)(2,1)}, u32[]{:S(2)}) copy-start(bf16[720,8]{0,1:T(8,128)(2,1)} %param.15) | copy-start | bytes 34564
  0.6 23.5 %copy-start.6 = (bf16[2880]{0:T(1024)(128)(2,1)S(1)}, bf16[2880]{0:T(1024)(128)(2,1)}, u32[]{:S(2)}) copy-start(bf16[2880]{0:T(1024)(128)(2,1)} %param.14) | copy-start | bytes 17284
  0.7 28.4 %copy-start.1 = (bf16[1,256,2880]{1,2,0:T(8,128)(2,1)S(1)}, bf16[1,256,2880]{1,2,0:T(8,128)(2,1)}, u32[]{:S(2)}) copy-start(bf16[1,256,2880]{1,2,0:T(8,128)(2,1)} %param.12) | copy-start | bytes 4423684
  0.7 28.4 %copy-start.3 = (s32[1,256,4]{1,2,0:T(4,128)S(1)}, s32[1,256,4]{1,2,0:T(4,128)}, u32[]{:S(2)}) copy-start(s32[1,256,4]{1,2,0:T(4,128)} %param.13) | copy-start | bytes 12292
  0.7 28.4 %copy-start.4 = (s32[64]{0:T(128)S(1)}, s32[64]{0:T(128)}, u32[]{:S(2)}) copy-start(s32[64]{0:T(128)} %place_ref.3) | copy-start | bytes 772
  6.5 30.5 %all-to-all-start = ((bf16[64,24,128]{2,1,0:T(8,128)(2,1)}), bf16[64,24,128]{2,1,0:T(8,128)(2,1)S(1)}, u32[]{:S(2)}, u32[]{:S(2)}) async-start(bf16[64,24,128]{2,1,0:T(8,128)(2,1)} %encode.1), calls=%async_computation | async-start | bytes 786432 | tf_op jit(solution)/shard_map/all_to_all | solution.py:311
  20.0 4.2 %collective-permute-start.1 = (bf16[8,720]{1,0:T(8,128)(2,1)S(1)}, bf16[8,720]{1,0:T(8,128)(2,1)S(1)}, u32[]{:S(2)}, u32[]{:S(2)}) collective-permute-start(bf16[8,720]{1,0:T(8,128)(2,1)S(1)} %bitcast.29), channel_id=1, source_target_pairs={{0,2},{1,3},{2,0},{3,1},{4,6},{5,7},{6,4},{7,5},{8,10},{9,11},{10,... | collective-permute-start | bytes 34568 | tf_op jit(solution)/shard_map/ppermute | solution.py:308
  22.7 2.1 %collective-permute-start = (bf16[8,720]{1,0:T(8,128)(2,1)S(1)}, bf16[8,720]{1,0:T(8,128)(2,1)S(1)}, u32[]{:S(2)}, u32[]{:S(2)}) collective-permute-start(bf16[8,720]{1,0:T(8,128)(2,1)S(1)} %bitcast.30), channel_id=1, source_target_pairs={{0,1},{1,0},{2,3},{3,2},{4,5},{5,4},{6,7},{7,6},{8,9},{9,8},{10,11... | collective-permute-start | bytes 34568 | tf_op jit(solution)/shard_map/ppermute | solution.py:308
  23.9 5.1 %collective-permute-start.2 = (bf16[8,720]{1,0:T(8,128)(2,1)S(1)}, bf16[8,720]{1,0:T(8,128)(2,1)S(1)}, u32[]{:S(2)}, u32[]{:S(2)}) collective-permute-start(bf16[8,720]{1,0:T(8,128)(2,1)S(1)} %bitcast.31), channel_id=1, source_target_pairs={{0,3},{1,2},{2,1},{3,0},{4,7},{5,6},{6,5},{7,4},{8,11},{9,10},{10,... | collective-permute-start | bytes 34568 | tf_op jit(solution)/shard_map/ppermute | solution.py:308
  29.1 1.8 %copy-start = (bf16[1,2880,512]{2,1,0:T(8,128)(2,1)S(1)}, bf16[1,2880,512]{2,1,0:T(8,128)(2,1)}, u32[]{:S(2)}) copy-start(bf16[1,2880,512]{2,1,0:T(8,128)(2,1)} %param.10) | copy-start | bytes 8847364
  30.9 1.4 %copy-start.2 = (bf16[1,256,2880]{1,2,0:T(8,128)(2,1)S(1)}, bf16[1,256,2880]{1,2,0:T(8,128)(2,1)}, u32[]{:S(2)}) copy-start(bf16[1,256,2880]{1,2,0:T(8,128)(2,1)} %param.11) | copy-start | bytes 4423684
  37.0 28.7 %all-to-all-start.1 = ((bf16[8,24,2880]{2,1,0:T(8,128)(2,1)}), bf16[8,24,2880]{2,1,0:T(8,128)(2,1)S(1)}, u32[]{:S(2)}, u32[]{:S(2)}) async-start(bf16[8,24,2880]{2,1,0:T(8,128)(2,1)} %bitcast.15), calls=%async_computation.1 | async-start | bytes 2260992 | tf_op jit(solution)/shard_map/all_to_all | solution.py:326
  41.7 23.4 %collective-permute-start.3 = (bf16[64,24,128]{2,1,0:T(8,128)(2,1)S(1)}, bf16[64,24,128]{2,1,0:T(8,128)(2,1)S(1)}, u32[]{:S(2)}, u32[]{:S(2)}) collective-permute-start(bf16[64,24,128]{2,1,0:T(8,128)(2,1)S(1)} %all-to-all-done.own_ref), channel_id=1, source_target_pairs={{0,2},{2,0},{1,3},{3,1},{4,6},{6,4},{5,7},{7,5},{8,10},{10,8},{9,1... | collective-permute-start | bytes 1179656 | tf_op jit(solution)/shard_map/ppermute | solution.py:323
  43.3 29.6 %collective-permute-start.4 = (bf16[64,24,128]{2,1,0:T(8,128)(2,1)S(1)}, bf16[64,24,128]{2,1,0:T(8,128)(2,1)S(1)}, u32[]{:S(2)}, u32[]{:S(2)}) collective-permute-start(bf16[64,24,128]{2,1,0:T(8,128)(2,1)S(1)} %all-to-all-done.own_ref), channel_id=1, source_target_pairs={{0,1},{1,0},{2,3},{3,2},{4,5},{5,4},{6,7},{7,6},{8,9},{9,8},{10,11... | collective-permute-start | bytes 1179656 | tf_op jit(solution)/shard_map/ppermute | solution.py:324
  65.1 7.7 %collective-permute-start.5 = (bf16[64,24,128]{2,1,0:T(8,128)(2,1)S(1)}, bf16[64,24,128]{2,1,0:T(8,128)(2,1)S(1)}, u32[]{:S(2)}, u32[]{:S(2)}) collective-permute-start(bf16[64,24,128]{2,1,0:T(8,128)(2,1)S(1)} %collective-permute-done.3.across_ref), channel_id=1, source_target_pairs={{0,1},{1,0},{2,3},{3,2},{4,5},{5,4},{6,7},{7,6},{8,9},{9,8},{10,11... | collective-permute-start | bytes 1179656 | tf_op jit(solution)/shard_map/ppermute | solution.py:325
  66.7 16.6 %all-to-all-start.2 = ((bf16[8,4,2880]{2,1,0:T(4,128)(2,1)}), bf16[8,4,2880]{2,1,0:T(4,128)(2,1)S(1)}, u32[]{:S(2)}, u32[]{:S(2)}) async-start(bf16[8,4,2880]{2,1,0:T(4,128)(2,1)} %merge_plane.1), calls=%async_computation.2 | async-start | bytes 376832 | tf_op jit(solution)/shard_map/all_to_all | solution.py:328

commit v3 on v2

--- a/solution.py
+++ b/solution.py
@@ -14,8 +14,11 @@
 TOK = 256
 HID = 256
 CAP = 3
-PLANE = 8
+SIDE = 4
 DEPTH = 8
+INNER = 16
+PIECES = 5
+PIECE = D // PIECES
 PACKED = TOK // 4 * CAP
 
 VMEM = pltpu.VMEM
@@ -29,6 +32,10 @@
 
 def params(mib):
     return pltpu.CompilerParams(vmem_limit_bytes=mib * 2**20)
+
+
+def in_hbm(x):
+    return pltpu.with_memory_space_constraint(x, pltpu.HBM)
 
 
 def nt(a, b):
@@ -78,7 +85,11 @@
     return jnp.where(values < 0, -out, out)
 
 
-def encode_kernel(place_ref, master_ref, out_ref, slot_ref, held_ref, raw_ref, sems):
+def encode_kernel(
+    place_hbm, master_ref, out_ref, place_ref, slot_ref, held_ref, raw_ref, sems, place_sem
+):
+    place_copy = pltpu.make_async_copy(place_hbm, place_ref, place_sem)
+    place_copy.start()
     copies = []
     for g in range(HALF // PAIRS):
         at = g * PAIRS
@@ -88,7 +99,6 @@
             copy = pltpu.make_async_copy(master_ref.at[part], raw_ref.at[part], sems.at[2 * g + n])
             copy.start()
             copies.append(copy)
-    invert(place_ref, slot_ref)
     spread = (iota((128, 128), 0) == (iota((128, 128), 1) // 32) * 32 + 31).astype(F32).astype(BF)
     for g in range(HALF // PAIRS):
         at = g * PAIRS
@@ -104,6 +114,9 @@
         values = jnp.concatenate([low, high], axis=1)
         held_ref[at * SLOTS : (at + PAIRS) * SLOTS, :] = round_blocks(values, spread)
 
+    place_copy.wait()
+    invert(place_ref, slot_ref)
+
     def deal(o, _):
         out_ref[o] = held_ref[pl.ds(slot_ref[o], HALF, stride=SLOTS), :].astype(BF)
         return 0
@@ -116,15 +129,17 @@
         encode_kernel,
         name="encode",
         out_shape=jax.ShapeDtypeStruct((SLOTS, HALF, 128), BF),
-        in_specs=[pl.BlockSpec(memory_space=SMEM), pl.BlockSpec(memory_space=pl.ANY)],
+        in_specs=[pl.BlockSpec(memory_space=pl.ANY)] * 2,
         out_specs=pl.BlockSpec(memory_space=VMEM),
         scratch_shapes=[
+            pltpu.SMEM((SLOTS,), jnp.int32),
             pltpu.SMEM((SLOTS,), jnp.int32),
             VMEM((HALF * SLOTS, 128), F32),
             VMEM((COLS, SLOTS, ROWS), F32),
             pltpu.SemaphoreType.DMA((2 * HALF // PAIRS,)),
+            pltpu.SemaphoreType.DMA(()),
         ],
-        compiler_params=params(60),
+        compiler_params=params(16),
         cost_estimate=pl.CostEstimate(flops=10**9, bytes_accessed=4 * 10**6, transcendentals=0),
     )(placement, master)
 
@@ -166,24 +181,31 @@
     )(own, across, core, both)
 
 
-def expert_kernel(
+def norm_kernel(
     place_ref,
     hidden_ref,
     routes_ref,
     gain_ref,
-    router_ref,
     gate_up_ref,
-    down_ref,
-    out_ref,
+    normed_ref,
+    projected_ref,
+    pack_ref,
     rows_ref,
     merge_ref,
     slot_ref,
-    normed_ref,
+    weight_ref,
+    sems,
 ):
+    copies = []
+    for n in range(PIECES):
+        part = pl.ds(n * PIECE, PIECE)
+        copy = pltpu.make_async_copy(gate_up_ref.at[part], weight_ref.at[part], sems.at[n])
+        copy.start()
+        copies.append(copy)
     invert(place_ref, slot_ref)
-    plane = lax.axis_index("x") * 2 + lax.axis_index("yl")
-    depth = lax.axis_index("z")
-    owner = plane * DEPTH + depth
+    column = lax.axis_index("x")
+    inner = lax.axis_index("yl") * DEPTH + lax.axis_index("z")
+    owner = column * INNER + inner
     mine = slot_ref[owner] // DEPTH
 
     total = jnp.zeros((1, TOK), F32)
@@ -199,24 +221,18 @@
         diagonal = jnp.where(
             iota((size, size), 0) == iota((size, size), 1), jnp.broadcast_to(gain, (size, size)), 0.0
         ).astype(BF)
-        column = nn(diagonal, ones[:size])
+        spread = nn(diagonal, ones[:size])
         part = hidden_ref[at : at + size, :].astype(F32)
-        normed_ref[at : at + size, :] = (part * factor * column).astype(BF)
-
-    rep = lax.axis_index("yh") * 2 + lax.axis_index("c")
-    logits = jnp.zeros((8, TOK), F32)
-    for d in range(4):
-        start = pl.multiple_of((rep ^ d) * 720, 720)
-        logits = logits + nn(router_ref[d], normed_ref[pl.ds(start, 720), :])
+        normed_ref[at : at + size, :] = (part * factor * spread).astype(BF)
+    projected = jnp.zeros((TOK, 2 * HID), F32)
+    for n in range(PIECES):
+        copies[n].wait()
+        part = slice(n * PIECE, (n + 1) * PIECE)
+        projected = projected + tn(normed_ref[part, :], weight_ref[part, :])
+    projected_ref[...] = projected
+
     which = iota((8, TOK), 0)
-    chosen = jnp.zeros((8, TOK), F32)
-    for k in range(4):
-        chosen = jnp.where(which == routes_ref[k : k + 1, :], 1.0, chosen)
-    powered = jnp.where(chosen > 0, jnp.exp(logits), 0.0)
-    weights = powered / jnp.sum(powered, axis=0, keepdims=True)
-    weight = jnp.sum(jnp.where(which == mine, weights, 0.0), axis=0, keepdims=True)
-    weight = jnp.transpose(jnp.broadcast_to(weight, (8, TOK)))[:, 0:1]
-
+    chosen = choices(routes_ref)
     earlier = (
         ((iota((TOK, TOK), 0) // 4) == (iota((TOK, TOK), 1) // 4))
         & (iota((TOK, TOK), 0) < iota((TOK, TOK), 1))
@@ -225,32 +241,24 @@
     turn = jnp.where(chosen > 0, rank, -1.0)
     my_turn = jnp.sum(jnp.where(which == mine, turn, 0.0), axis=0, keepdims=True)
     packed = iota((PACKED, TOK), 0)
-    pack = (
+    pack_ref[...] = (
         ((iota((PACKED, TOK), 1) // 4) == (packed // CAP))
         & (jnp.broadcast_to(my_turn, (PACKED, TOK)) == (packed % CAP).astype(F32))
     ).astype(F32).astype(BF)
-
-    projected = tn(normed_ref[...], gate_up_ref[...])
-    gate = projected[:, :HID]
-    up = projected[:, HID:]
-    activated = (weight * gate * jax.nn.sigmoid(1.702 * gate) * (up + 1.0)).astype(BF)
-    activated = nn(pack, activated).astype(BF)
-    for at in range(0, D, 640):
-        size = min(640, D - at)
-        out_ref[:, at : at + size] = nt(activated, down_ref[at : at + size, :]).astype(BF)
 
     own = (iota((8, TOK), 1) == iota((8, TOK), 0) + owner * 4).astype(F32).astype(BF)
     for at in range(0, D, 640):
         size = min(640, D - at)
         rows_ref[:, at : at + size] = nt(own, hidden_ref[at : at + size, :])[:4]
 
-    pick = (iota((TOK, 128), 0) == iota((TOK, 128), 1) + plane * 32).astype(F32).astype(BF)
+    local = 4 * INNER
+    pick = (iota((TOK, 128), 0) == iota((TOK, 128), 1) + column * local).astype(F32).astype(BF)
     turns = nn(turn.astype(BF), pick)
-    per = 4 * DEPTH // 4 * CAP
+    per = INNER * CAP
     block = iota((per, 128), 0)
     parts = []
-    for p in range(PLANE):
-        expert = slot_ref[p * DEPTH + depth] // DEPTH
+    for x in range(SIDE):
+        expert = slot_ref[x * INNER + inner] // DEPTH
         theirs = jnp.sum(jnp.where(iota((8, 128), 0) == expert, turns, 0.0), axis=0, keepdims=True)
         parts.append(
             (
@@ -258,39 +266,96 @@
                 & (jnp.broadcast_to(theirs, (per, 128)) == (block % CAP).astype(F32))
             ).astype(F32)
         )
-    merge_ref[...] = jnp.transpose(jnp.concatenate(parts, axis=0))[:32].astype(BF)
-
-
-def expert_terms(placement, hidden, routes, gain, router, gate_up, down):
+    merge_ref[...] = jnp.transpose(jnp.concatenate(parts, axis=0))[:local].astype(BF)
+
+
+def choices(routes_ref):
+    which = iota((8, TOK), 0)
+    chosen = jnp.zeros((8, TOK), F32)
+    for k in range(4):
+        chosen = jnp.where(which == routes_ref[k : k + 1, :], 1.0, chosen)
+    return chosen
+
+
+def norm_project(placement, hidden, routes, gain, gate_up):
     return pl.pallas_call(
-        expert_kernel,
+        norm_kernel,
+        name="norm_project",
+        out_shape=(
+            jax.ShapeDtypeStruct((D, TOK), BF),
+            jax.ShapeDtypeStruct((TOK, 2 * HID), F32),
+            jax.ShapeDtypeStruct((PACKED, TOK), BF),
+            jax.ShapeDtypeStruct((4, D), F32),
+            jax.ShapeDtypeStruct((4 * INNER, PACKED), BF),
+        ),
+        in_specs=[pl.BlockSpec(memory_space=SMEM)]
+        + [pl.BlockSpec(memory_space=VMEM)] * 3
+        + [pl.BlockSpec(memory_space=pl.ANY)],
+        out_specs=(pl.BlockSpec(memory_space=VMEM),) * 5,
+        scratch_shapes=[
+            pltpu.SMEM((SLOTS,), jnp.int32),
+            VMEM((D, 2 * HID), BF),
+            pltpu.SemaphoreType.DMA((PIECES,)),
+        ],
+        compiler_params=params(32),
+        cost_estimate=pl.CostEstimate(flops=3 * 10**9, bytes_accessed=8 * 10**6, transcendentals=0),
+    )(placement, hidden, routes, gain, gate_up)
+
+
+def terms_kernel(
+    place_ref, routes_ref, router_ref, normed_ref, projected_ref, pack_ref, down_ref, out_ref, slot_ref
+):
+    invert(place_ref, slot_ref)
+    owner = lax.axis_index("x") * INNER + lax.axis_index("yl") * DEPTH + lax.axis_index("z")
+    mine = slot_ref[owner] // DEPTH
+
+    rep = lax.axis_index("yh") * 2 + lax.axis_index("c")
+    logits = jnp.zeros((8, TOK), F32)
+    for d in range(4):
+        start = pl.multiple_of((rep ^ d) * 720, 720)
+        logits = logits + nn(router_ref[d], normed_ref[pl.ds(start, 720), :])
+    which = iota((8, TOK), 0)
+    chosen = choices(routes_ref)
+    powered = jnp.where(chosen > 0, jnp.exp(logits), 0.0)
+    weights = powered / jnp.sum(powered, axis=0, keepdims=True)
+    weight = jnp.sum(jnp.where(which == mine, weights, 0.0), axis=0, keepdims=True)
+    weight = jnp.transpose(jnp.broadcast_to(weight, (8, TOK)))[:, 0:1]
+
+    gate = projected_ref[:, :HID]
+    up = projected_ref[:, HID:]
+    activated = (weight * gate * jax.nn.sigmoid(1.702 * gate) * (up + 1.0)).astype(BF)
+    activated = nn(pack_ref[...], activated).astype(BF)
+    for at in range(0, D, 640):
+        size = min(640, D - at)
+        out_ref[:, at : at + size] = nt(activated, down_ref[at : at + size, :]).astype(BF)
+
+
+def expert_terms(placement, routes, router, normed, projected, pack, down):
+    return pl.pallas_call(
+        terms_kernel,
         name="expert_terms",
-        out_shape=(
-            jax.ShapeDtypeStruct((PACKED, D), BF),
-            jax.ShapeDtypeStruct((4, D), F32),
-            jax.ShapeDtypeStruct((32, PACKED), BF),
-        ),
+        out_shape=jax.ShapeDtypeStruct((PACKED, D), BF),
         in_specs=[pl.BlockSpec(memory_space=SMEM)] + [pl.BlockSpec(memory_space=VMEM)] * 6,
-        out_specs=(pl.BlockSpec(memory_space=VMEM),) * 3,
-        scratch_shapes=[pltpu.SMEM((SLOTS,), jnp.int32), pltpu.VMEM((D, TOK), BF)],
-        compiler_params=params(40),
-        cost_estimate=pl.CostEstimate(flops=4 * 10**9, bytes_accessed=8 * 10**6, transcendentals=0),
-    )(placement, hidden, routes, gain, router, gate_up, down)
+        out_specs=pl.BlockSpec(memory_space=VMEM),
+        scratch_shapes=[pltpu.SMEM((SLOTS,), jnp.int32)],
+        compiler_params=params(32),
+        cost_estimate=pl.CostEstimate(flops=10**9, bytes_accessed=4 * 10**6, transcendentals=0),
+    )(placement, routes, router, normed, projected, pack, down)
 
 
 def merge_kernel(merge_ref, got_ref, out_ref):
     for at in range(0, D, 640):
         size = min(640, D - at)
         part = nn(merge_ref[...], got_ref[:, at : at + size]).astype(BF)
-        for z in range(DEPTH):
-            out_ref[z, :, at : at + size] = part[4 * z : 4 * z + 4]
-
-
-def merge_plane(merge, got):
+        for n in range(INNER):
+            out_ref[n, :, at : at + size] = part[4 * n : 4 * n + 4]
+
+
+def merge_side(merge, got):
     return pl.pallas_call(
         merge_kernel,
-        name="merge_plane",
-        out_shape=jax.ShapeDtypeStruct((DEPTH, 4, D), BF),
+        name="merge_side",
+        out_shape=jax.ShapeDtypeStruct((INNER, 4, D), BF),
         in_specs=[pl.BlockSpec(memory_space=VMEM)] * 2,
         out_specs=pl.BlockSpec(memory_space=VMEM),
         compiler_params=params(16),
@@ -307,25 +372,24 @@
         pairs = [(r, r ^ d) for r in range(4)]
         routers.append(lax.ppermute(router_rows, REP, pairs))
 
-    chunks = encode(placement, jnp.transpose(master, (2, 0, 1)))
+    chunks = encode(in_hbm(placement), in_hbm(jnp.transpose(master, (2, 0, 1))))
     chunks = lax.all_to_all(chunks, FSDP, split_axis=0, concat_axis=0, tiled=True)
 
-    terms, rows, merge = expert_terms(
-        placement,
-        hidden[0].T,
-        routes[0].T,
-        norm_gain[None],
-        jnp.stack(routers),
-        resident_gate_up[0],
-        resident_down[0].T,
+    chosen = routes[0].T
+    normed, projected, pack, rows, merge = norm_project(
+        placement, hidden[0].T, chosen, norm_gain[None], in_hbm(resident_gate_up[0])
+    )
+    terms = expert_terms(
+        placement, chosen, jnp.stack(routers), normed, projected, pack, resident_down[0].T
     )
     chunks, terms = lax.optimization_barrier((chunks, terms))
+    terms = lax.all_to_all(terms, "x", split_axis=0, concat_axis=0, tiled=True)
     across = lax.ppermute(chunks, "yh", ((0, 1), (1, 0)))
     core = lax.ppermute(chunks, "c", ((0, 1), (1, 0)))
+    terms = merge_side(merge, terms)
+    across, _ = lax.optimization_barrier((across, terms))
     both = lax.ppermute(across, "c", ((0, 1), (1, 0)))
-    terms = lax.all_to_all(terms, ("x", "yl"), split_axis=0, concat_axis=0, tiled=True)
-    terms = merge_plane(merge, terms)
-    terms = lax.all_to_all(terms, "z", split_axis=0, concat_axis=0, tiled=True)
+    terms = lax.all_to_all(terms, ("yl", "z"), split_axis=0, concat_axis=0, tiled=True)
     decoded = (rows + jnp.sum(terms.astype(F32), axis=0)).astype(BF)
     refreshed = assemble(chunks, across, core, both).T
     return (refreshed[None], decoded[None])

time: 84.4 us -> 72.1 us (0.85)
  the two profiles are of different devices: /device:TPU:1 before, /device:TPU:32 now
where the time goes in v3:
time: 72.1 us; the launch traced here: 71.8 us
  starting transfers between devices  28.9 us (40%)
  waiting for transfers between devices  25.6 us (36%)
  Pallas kernels  15.6 us (22%)
  between operations  0.8 us (1%)
  other arithmetic  0.79 us (1%)
    all_to_all x1, starting transfers between devices, on_device(): lax.all_to_all(chunks, FSDP, split_axis=0, concat_axis=0, tiled=True)  12.6 us
    all_to_all x1, waiting for transfers between devices, on_device(): terms = lax.all_to_all(terms, 'x', split_axis=0, concat_axis=0, tiled=True)  11.7 us
    all_to_all x1, waiting for transfers between devices, on_device(): lax.all_to_all(terms, ('yl', 'z'), split_axis=0, concat_axis=0, tiled=True)  7.07 us
    all_to_all x1, starting transfers between devices, on_device(): lax.all_to_all(terms, ('yl', 'z'), split_axis=0, concat_axis=0, tiled=True)  5.83 us
    pallas_call x1, Pallas kernels, encode(): pl.pallas_call(encode_kernel, name='encode', out_shape=jax.ShapeDtypeStru...  5.22 us
    all_to_all x1, waiting for transfers between devices, on_device(): lax.all_to_all(chunks, FSDP, split_axis=0, concat_axis=0, tiled=True)  4.35 us
    pallas_call x1, Pallas kernels, norm_project(): pl.pallas_call(norm_kernel, name='norm_project', out_shape=(jax.ShapeDtyp...  3.7 us
    all_to_all x1, starting transfers between devices, on_device(): terms = lax.all_to_all(terms, 'x', split_axis=0, concat_axis=0, tiled=True)  3.53 us
  transfers between devices with their start and end apart: 9, of which 6 were waited for; matrix products, arithmetic and copies ran while one was open for 0% of the time, Pallas kernels for 14%

profile of v3, /device:TPU:32, one launch (start us, length us, event | category | flops | bytes accessed | tf_op | source)
XLA Modules:
  0.0 71.8 jit_solution(3161235016611861881)
XLA Ops:
  0.6 0.0 copy-start.4
  0.6 0.0 copy-start.5
  0.7 0.0 copy-start.1
  0.7 0.0 copy-start.2
  0.7 0.0 copy-start.3
  0.7 5.2 %encode.1 = bf16[64,24,128]{2,1,0:T(8,128)(2,1)} custom-call(s32[64]{0:T(128)} %place_ref.3, f32[45,64,64]{2,1,0:T(8,128)} %bitcast.37), custom_call_target="tpu_custom_call" | custom-call | flops 1000000000 | bytes 4000000 | tf_op jit(solution)/shard_map/encode/pallas_call | solution.py:128
  5.9 12.6 %all-to-all-start = ((bf16[64,24,128]{2,1,0:T(8,128)(2,1)}), bf16[64,24,128]{2,1,0:T(8,128)(2,1)S(1)}, u32[]{:S(2)}, u32[]{:S(2)}) async-start(bf16[64,24,128]{2,1,0:T(8,128)(2,1)} %encode.1), calls=%async_computation | async-start | bytes 786432 | tf_op jit(solution)/shard_map/all_to_all | solution.py:376
  18.5 0.0 copy-done.4
  18.5 0.1 collective-permute-start
  18.6 3.0 %collective-permute-start.1 = (bf16[8,720]{1,0:T(8,128)(2,1)S(1)}, bf16[8,720]{1,0:T(8,128)(2,1)S(1)}, u32[]{:S(2)}, u32[]{:S(2)}) collective-permute-start(bf16[8,720]{1,0:T(8,128)(2,1)S(1)} %bitcast.30), channel_id=1, source_target_pairs={{0,2},{1,3},{2,0},{3,1},{4,6},{5,7},{6,4},{7,5},{8,10},{9,11},{10,... | collective-permute-start | bytes 34568 | tf_op jit(solution)/shard_map/ppermute | solution.py:373
  21.6 0.4 collective-permute-start.2
  22.0 0.0 copy-done.5
  22.0 0.0 copy-done.1
  22.0 0.0 copy-done.2
  22.0 0.0 copy-done.3
  22.1 0.0 copy-start
  22.1 3.7 %norm_project.1 = (bf16[2880,256]{1,0:T(8,128)(2,1)S(1)}, f32[256,512]{1,0:T(8,128)S(1)}, bf16[192,256]{1,0:T(8,128)(2,1)S(1)}, f32[4,2880]{1,0:T(4,128)S(1)}, bf16[64,192]{1,0:T(8,128)(2,1)S(1)}) custom-call(s32[64]{0:T(128)S(1)} %copy-done.2, bf16[2880,256]{1,0:T(8,128)(2,1)S(1)} %bitcast.28, s32[4,256]{1,0:T(4,128)S(1)} %bitcast.26, ...), custom_call_target="tpu_custom_call" | custom-call | flops 3000000000 | bytes 8000000 | tf_op jit(solution)/shard_map/norm_project/pallas_call | solution.py:281
  25.8 0.0 collective-permute-done
  25.8 0.0 collective-permute-done.1
  25.8 0.7 collective-permute-done.2
  26.5 0.0 copy-done
  26.5 3.3 %expert_terms.1 = bf16[192,2880]{1,0:T(8,128)(2,1)} custom-call(s32[64]{0:T(128)S(1)} %copy-done.2, s32[4,256]{1,0:T(4,128)S(1)} %bitcast.27, bf16[4,8,720]{2,1,0:T(8,128)(2,1)S(1)} %pad_maximum_fusion.router_ref, bf16[2880,256]{1,0:T(8,128)(2,1)S(1)} %get-tuple-element.10.normed_ref, f32[256,512]{1,0:T(8,128)S(1)} %get-tuple-element.11.projected_ref, ...), custom_call_target="tpu_custom_call" | custom-call | flops 1000000000 | bytes 4000000 | tf_op jit(solution)/shard_map/expert_terms/pallas_call | solution.py:334
  29.8 4.3 %all-to-all-done.own_ref = bf16[64,24,128]{2,1,0:T(8,128)(2,1)S(1)} async-done(((bf16[64,24,128]{2,1,0:T(8,128)(2,1)}), bf16[64,24,128]{2,1,0:T(8,128)(2,1)S(1)}, u32[]{:S(2)}, u32[]{:S(2)}) %all-to-all-start) | async-done | bytes 393248 | tf_op jit(solution)/shard_map/all_to_all | solution.py:376
  34.2 3.5 %all-to-all-start.1 = ((bf16[4,48,2880]{2,1,0:T(8,128)(2,1)}), bf16[4,48,2880]{2,1,0:T(8,128)(2,1)S(1)}, u32[]{:S(2)}, u32[]{:S(2)}) async-start(bf16[4,48,2880]{2,1,0:T(8,128)(2,1)} %bitcast.14), calls=%async_computation.1 | async-start | bytes 2260992 | tf_op jit(solution)/shard_map/all_to_all | solution.py:386
  37.7 3.0 %collective-permute-start.3 = (bf16[64,24,128]{2,1,0:T(8,128)(2,1)S(1)}, bf16[64,24,128]{2,1,0:T(8,128)(2,1)S(1)}, u32[]{:S(2)}, u32[]{:S(2)}) collective-permute-start(bf16[64,24,128]{2,1,0:T(8,128)(2,1)S(1)} %all-to-all-done.own_ref), channel_id=1, source_target_pairs={{0,2},{2,0},{1,3},{3,1},{4,6},{6,4},{5,7},{7,5},{8,10},{10,8},{9,1... | collective-permute-start | bytes 1179656 | tf_op jit(solution)/shard_map/ppermute | solution.py:387
  40.7 11.7 %all-to-all-done.1 = bf16[4,48,2880]{2,1,0:T(8,128)(2,1)S(1)} async-done(((bf16[4,48,2880]{2,1,0:T(8,128)(2,1)}), bf16[4,48,2880]{2,1,0:T(8,128)(2,1)S(1)}, u32[]{:S(2)}, u32[]{:S(2)}) %all-to-all-start.1) | async-done | bytes 1105952 | tf_op jit(solution)/shard_map/all_to_all | solution.py:386
  52.4 1.1 %merge_side.1 = bf16[16,4,2880]{2,1,0:T(4,128)(2,1)} custom-call(bf16[64,192]{1,0:T(8,128)(2,1)S(1)} %get-tuple-element.14.merge_ref, bf16[192,2880]{1,0:T(8,128)(2,1)S(1)} %bitcast.24), custom_call_target="tpu_custom_call" | custom-call | flops 100000000 | bytes 1000000 | tf_op jit(solution)/shard_map/merge_side/pallas_call | solution.py:355
  53.5 5.8 %all-to-all-start.2 = ((bf16[16,4,2880]{2,1,0:T(4,128)(2,1)}), bf16[16,4,2880]{2,1,0:T(4,128)(2,1)S(1)}, u32[]{:S(2)}, u32[]{:S(2)}) async-start(bf16[16,4,2880]{2,1,0:T(4,128)(2,1)} %merge_side.1), calls=%async_computation.2 | async-start | bytes 753664 | tf_op jit(solution)/shard_map/all_to_all | solution.py:392
  59.4 0.0 collective-permute-start.4
  59.4 0.0 collective-permute-done.3.across_ref
  59.4 0.5 collective-permute-start.5
  59.9 1.2 %collective-permute-done.4.core_ref = bf16[64,24,128]{2,1,0:T(8,128)(2,1)S(1)} collective-permute-done((bf16[64,24,128]{2,1,0:T(8,128)(2,1)S(1)}, bf16[64,24,128]{2,1,0:T(8,128)(2,1)S(1)}, u32[]{:S(2)}, u32[]{:S(2)}) %collective-permute-start.4) | collective-permute-done | bytes 393248 | tf_op jit(solution)/shard_map/ppermute | solution.py:388
  61.1 0.6 collective-permute-done.5.both_ref
  61.7 2.2 %assemble.1 = bf16[2880,256]{1,0:T(8,128)(2,1)} custom-call(bf16[64,24,128]{2,1,0:T(8,128)(2,1)S(1)} %all-to-all-done.own_ref, bf16[64,24,128]{2,1,0:T(8,128)(2,1)S(1)} %collective-permute-done.3.across_ref, bf16[64,24,128]{2,1,0:T(8,128)(2,1)S(1)} %collective-permute-done.4.core_ref, bf16[64,24,128]{2,1,0:T(8,128)(2,1)S(1)} %collective-permute-done.5.both_ref), custom_call_target="tpu_custom_call" | custom-call | flops 1000000000 | bytes 4000000 | tf_op jit(solution)/shard_map/assemble/pallas_call | solution.py:171
  63.9 7.1 %all-to-all-done.2 = bf16[16,4,2880]{2,1,0:T(4,128)(2,1)S(1)} async-done(((bf16[16,4,2880]{2,1,0:T(4,128)(2,1)}), bf16[16,4,2880]{2,1,0:T(4,128)(2,1)S(1)}, u32[]{:S(2)}, u32[]{:S(2)}) %all-to-all-start.2) | async-done | bytes 368672 | tf_op jit(solution)/shard_map/all_to_all | solution.py:392
  71.0 0.2 convert_reduce_fusion
  71.1 0.6 fusion
  (2 shorter events, 0.0 us)
Async XLA Ops:
  0.6 17.9 %copy-start.4 = (bf16[720,8]{0,1:T(8,128)(2,1)S(1)}, bf16[720,8]{0,1:T(8,128)(2,1)}, u32[]{:S(2)}) copy-start(bf16[720,8]{0,1:T(8,128)(2,1)} %param.15) | copy-start | bytes 34564
  0.6 21.4 %copy-start.5 = (bf16[2880]{0:T(1024)(128)(2,1)S(1)}, bf16[2880]{0:T(1024)(128)(2,1)}, u32[]{:S(2)}) copy-start(bf16[2880]{0:T(1024)(128)(2,1)} %param.14) | copy-start | bytes 17284
  0.7 21.4 %copy-start.1 = (s32[1,256,4]{1,2,0:T(4,128)S(1)}, s32[1,256,4]{1,2,0:T(4,128)}, u32[]{:S(2)}) copy-start(s32[1,256,4]{1,2,0:T(4,128)} %param.13) | copy-start | bytes 12292
  0.7 21.4 %copy-start.2 = (s32[64]{0:T(128)S(1)}, s32[64]{0:T(128)}, u32[]{:S(2)}) copy-start(s32[64]{0:T(128)} %place_ref.3) | copy-start | bytes 772
  0.7 21.4 %copy-start.3 = (bf16[1,256,2880]{1,2,0:T(8,128)(2,1)S(1)}, bf16[1,256,2880]{1,2,0:T(8,128)(2,1)}, u32[]{:S(2)}) copy-start(bf16[1,256,2880]{1,2,0:T(8,128)(2,1)} %param.12) | copy-start | bytes 4423684
  5.9 28.3 %all-to-all-start = ((bf16[64,24,128]{2,1,0:T(8,128)(2,1)}), bf16[64,24,128]{2,1,0:T(8,128)(2,1)S(1)}, u32[]{:S(2)}, u32[]{:S(2)}) async-start(bf16[64,24,128]{2,1,0:T(8,128)(2,1)} %encode.1), calls=%async_computation | async-start | bytes 786432 | tf_op jit(solution)/shard_map/all_to_all | solution.py:376
  18.5 7.2 %collective-permute-start = (bf16[8,720]{1,0:T(8,128)(2,1)S(1)}, bf16[8,720]{1,0:T(8,128)(2,1)S(1)}, u32[]{:S(2)}, u32[]{:S(2)}) collective-permute-start(bf16[8,720]{1,0:T(8,128)(2,1)S(1)} %bitcast.29), channel_id=1, source_target_pairs={{0,1},{1,0},{2,3},{3,2},{4,5},{5,4},{6,7},{7,6},{8,9},{9,8},{10,11... | collective-permute-start | bytes 34568 | tf_op jit(solution)/shard_map/ppermute | solution.py:373
  18.6 7.1 %collective-permute-start.1 = (bf16[8,720]{1,0:T(8,128)(2,1)S(1)}, bf16[8,720]{1,0:T(8,128)(2,1)S(1)}, u32[]{:S(2)}, u32[]{:S(2)}) collective-permute-start(bf16[8,720]{1,0:T(8,128)(2,1)S(1)} %bitcast.30), channel_id=1, source_target_pairs={{0,2},{1,3},{2,0},{3,1},{4,6},{5,7},{6,4},{7,5},{8,10},{9,11},{10,... | collective-permute-start | bytes 34568 | tf_op jit(solution)/shard_map/ppermute | solution.py:373
  21.6 4.8 %collective-permute-start.2 = (bf16[8,720]{1,0:T(8,128)(2,1)S(1)}, bf16[8,720]{1,0:T(8,128)(2,1)S(1)}, u32[]{:S(2)}, u32[]{:S(2)}) collective-permute-start(bf16[8,720]{1,0:T(8,128)(2,1)S(1)} %bitcast.31), channel_id=1, source_target_pairs={{0,3},{1,2},{2,1},{3,0},{4,7},{5,6},{6,5},{7,4},{8,11},{9,10},{10,... | collective-permute-start | bytes 34568 | tf_op jit(solution)/shard_map/ppermute | solution.py:373
  22.1 4.4 %copy-start = (bf16[1,256,2880]{1,2,0:T(8,128)(2,1)S(1)}, bf16[1,256,2880]{1,2,0:T(8,128)(2,1)}, u32[]{:S(2)}) copy-start(bf16[1,256,2880]{1,2,0:T(8,128)(2,1)} %param.11) | copy-start | bytes 4423684
  34.2 18.3 %all-to-all-start.1 = ((bf16[4,48,2880]{2,1,0:T(8,128)(2,1)}), bf16[4,48,2880]{2,1,0:T(8,128)(2,1)S(1)}, u32[]{:S(2)}, u32[]{:S(2)}) async-start(bf16[4,48,2880]{2,1,0:T(8,128)(2,1)} %bitcast.14), calls=%async_computation.1 | async-start | bytes 2260992 | tf_op jit(solution)/shard_map/all_to_all | solution.py:386
  37.7 21.7 %collective-permute-start.3 = (bf16[64,24,128]{2,1,0:T(8,128)(2,1)S(1)}, bf16[64,24,128]{2,1,0:T(8,128)(2,1)S(1)}, u32[]{:S(2)}, u32[]{:S(2)}) collective-permute-start(bf16[64,24,128]{2,1,0:T(8,128)(2,1)S(1)} %all-to-all-done.own_ref), channel_id=1, source_target_pairs={{0,2},{2,0},{1,3},{3,1},{4,6},{6,4},{5,7},{7,5},{8,10},{10,8},{9,1... | collective-permute-start | bytes 1179656 | tf_op jit(solution)/shard_map/ppermute | solution.py:387
  53.5 17.4 %all-to-all-start.2 = ((bf16[16,4,2880]{2,1,0:T(4,128)(2,1)}), bf16[16,4,2880]{2,1,0:T(4,128)(2,1)S(1)}, u32[]{:S(2)}, u32[]{:S(2)}) async-start(bf16[16,4,2880]{2,1,0:T(4,128)(2,1)} %merge_side.1), calls=%async_computation.2 | async-start | bytes 753664 | tf_op jit(solution)/shard_map/all_to_all | solution.py:392
  59.4 1.7 %collective-permute-start.4 = (bf16[64,24,128]{2,1,0:T(8,128)(2,1)S(1)}, bf16[64,24,128]{2,1,0:T(8,128)(2,1)S(1)}, u32[]{:S(2)}, u32[]{:S(2)}) collective-permute-start(bf16[64,24,128]{2,1,0:T(8,128)(2,1)S(1)} %all-to-all-done.own_ref), channel_id=1, source_target_pairs={{0,1},{1,0},{2,3},{3,2},{4,5},{5,4},{6,7},{7,6},{8,9},{9,8},{10,11... | collective-permute-start | bytes 1179656 | tf_op jit(solution)/shard_map/ppermute | solution.py:388
  59.4 2.3 %collective-permute-start.5 = (bf16[64,24,128]{2,1,0:T(8,128)(2,1)S(1)}, bf16[64,24,128]{2,1,0:T(8,128)(2,1)S(1)}, u32[]{:S(2)}, u32[]{:S(2)}) collective-permute-start(bf16[64,24,128]{2,1,0:T(8,128)(2,1)S(1)} %collective-permute-done.3.across_ref), channel_id=1, source_target_pairs={{0,1},{1,0},{2,3},{3,2},{4,5},{5,4},{6,7},{7,6},{8,9},{9,8},{10,11... | collective-permute-start | bytes 1179656 | tf_op jit(solution)/shard_map/ppermute | solution.py:391

commit v4 on v3

v4 whole, which is shorter than its diff:
```python
import jax
import jax.numpy as jnp
from jax import lax
from jax.experimental import pallas as pl
from jax.experimental.pallas import tpu as pltpu
from jax.sharding import Mesh
from jax.sharding import PartitionSpec as P

D = 2880
SLOTS = 64
COLS = 45
HALF = 24
ROWS = 64
TOK = 256
HID = 256
CAP = 3
DEPTH = 8
PIECES = 5
PIECE = D // PIECES
SUB = 8
WIDE = 1152

VMEM = pltpu.VMEM
SMEM = pltpu.SMEM
BF = jnp.bfloat16
F32 = jnp.float32

FSDP = ("x", "yl", "z")
REP = ("yh", "c")


def params(mib):
    return pltpu.CompilerParams(vmem_limit_bytes=mib * 2**20)


def in_hbm(x):
    return pltpu.with_memory_space_constraint(x, pltpu.HBM)


def nt(a, b):
    return lax.dot_general(a, b, (((1,), (1,)), ((), ())), preferred_element_type=F32)


def tn(a, b):
    return lax.dot_general(a, b, (((0,), (0,)), ((), ())), preferred_element_type=F32)


def nn(a, b):
    return lax.dot_general(a, b, (((1,), (0,)), ((), ())), preferred_element_type=F32)


def iota(shape, dim):
    return lax.broadcasted_iota(jnp.int32, shape, dim)


def invert(place_ref, slot_ref):
    def step(s, _):
        slot_ref[place_ref[s]] = s
        return 0

    lax.fori_loop(0, SLOTS, step, 0, unroll=8)


PAIRS = 12


def round_blocks(values, spread):
    size = jnp.abs(values)
    top = size
    for shift in (1, 2, 4, 8, 16):
        top = jnp.maximum(top, pltpu.roll(top, shift, 1))
    top = jnp.maximum(top, 6.0 * 2.0**-40)
    lead = top * (2.0**23 + 1.0)
    lead = jnp.abs(lead - lead * (1.0 - 2.0**-24))
    scale = jnp.where(top > lead * 1.5, lead * 0.5, lead * 0.25)
    s = nn(scale.astype(BF), spread)
    out = jnp.where(size >= s * 0.25, s * 0.5, 0.0)
    out = jnp.where(size >= s * 0.75, s, out)
    out = jnp.where(size >= s * 1.25, s * 1.5, out)
    out = jnp.where(size >= s * 1.75, s * 2.0, out)
    out = jnp.where(size >= s * 2.5, s * 3.0, out)
    out = jnp.where(size >= s * 3.5, s * 4.0, out)
    out = jnp.where(size >= s * 5.0, s * 6.0, out)
    return jnp.where(values < 0, -out, out)


def encode_kernel(
    place_hbm, master_ref, out_ref, place_ref, slot_ref, held_ref, raw_ref, sems, place_sem
):
    place_copy = pltpu.make_async_copy(place_hbm, place_ref, place_sem)
    place_copy.start()
    copies = []
    for g in range(HALF // PAIRS):
        at = g * PAIRS
        wide = min(PAIRS, COLS - HALF - at)
        for n, (start, size) in enumerate(((at, PAIRS), (HALF + at, wide))):
            part = pl.ds(start, size)
            copy = pltpu.make_async_copy(master_ref.at[part], raw_ref.at[part], sems.at[2 * g + n])
            copy.start()
            copies.append(copy)
    spread = (iota((128, 128), 0) == (iota((128, 128), 1) // 32) * 32 + 31).astype(F32).astype(BF)
    for g in range(HALF // PAIRS):
        at = g * PAIRS
        wide = min(PAIRS, COLS - HALF - at)
        copies[2 * g].wait()
        copies[2 * g + 1].wait()
        low = raw_ref[at : at + PAIRS]
        high = raw_ref[HALF + at : HALF + at + wide]
        if wide < PAIRS:
            high = jnp.concatenate([high, low[wide:]], axis=0)
        low = low.reshape(PAIRS * SLOTS, ROWS)
        high = high.reshape(PAIRS * SLOTS, ROWS)
        values = jnp.concatenate([low, high], axis=1)
        held_ref[at * SLOTS : (at + PAIRS) * SLOTS, :] = round_blocks(values, spread)

    place_copy.wait()
    invert(place_ref, slot_ref)

    def deal(o, _):
        out_ref[o] = held_ref[pl.ds(slot_ref[o], HALF, stride=SLOTS), :].astype(BF)
        return 0

    lax.fori_loop(0, SLOTS, deal, 0, unroll=8)


def encode(placement, master):
    return pl.pallas_call(
        encode_kernel,
        name="encode",
        out_shape=jax.ShapeDtypeStruct((SLOTS, HALF, 128), BF),
        in_specs=[pl.BlockSpec(memory_space=pl.ANY)] * 2,
        out_specs=pl.BlockSpec(memory_space=VMEM),
        scratch_shapes=[
            pltpu.SMEM((SLOTS,), jnp.int32),
            pltpu.SMEM((SLOTS,), jnp.int32),
            VMEM((HALF * SLOTS, 128), F32),
            VMEM((COLS, SLOTS, ROWS), F32),
            pltpu.SemaphoreType.DMA((2 * HALF // PAIRS,)),
            pltpu.SemaphoreType.DMA(()),
        ],
        compiler_params=params(16),
        cost_estimate=pl.CostEstimate(flops=10**9, bytes_accessed=4 * 10**6, transcendentals=0),
    )(placement, master)


GROUP = 16


def assemble_kernel(own_ref, across_ref, core_ref, both_ref, out_ref, held_ref):
    low = iota((HALF, 128), 1) < ROWS
    half = lax.axis_index("yh")
    core = lax.axis_index("c")
    for i in range(GROUP):
        here = (own_ref[i].astype(F32), core_ref[i].astype(F32))
        there = (across_ref[i].astype(F32), both_ref[i].astype(F32))
        for h in range(2):
            mine, other = (jnp.where(half == h, a, b) for a, b in zip(here, there))
            first = jnp.where(core == 0, mine, other)
            second = jnp.where(core == 0, other, mine)
            upper = jnp.where(low, first, pltpu.roll(second, ROWS, 1))
            lower = jnp.where(low, pltpu.roll(first, ROWS, 1), second)
            lanes = slice(128 * h, 128 * h + 128)
            held_ref[COLS * i : COLS * i + HALF, lanes] = upper
            held_ref[COLS * i + HALF : COLS * (i + 1), lanes] = lower[: COLS - HALF]
    out_ref[...] = held_ref[...].astype(BF)


def assemble(own, across, core, both):
    rows = GROUP * COLS
    return pl.pallas_call(
        assemble_kernel,
        name="assemble",
        grid=(SLOTS // GROUP,),
        out_shape=jax.ShapeDtypeStruct((D, 4 * ROWS), BF),
        in_specs=[pl.BlockSpec((GROUP, HALF, 128), lambda g: (g, 0, 0))] * 4,
        out_specs=pl.BlockSpec((rows, 4 * ROWS), lambda g: (g, 0)),
        scratch_shapes=[VMEM((rows, 4 * ROWS), F32)],
        compiler_params=params(24),
        cost_estimate=pl.CostEstimate(flops=10**9, bytes_accessed=4 * 10**6, transcendentals=0),
    )(own, across, core, both)


def choices(routes_ref):
    which = iota((8, TOK), 0)
    chosen = jnp.zeros((8, TOK), F32)
    for k in range(4):
        chosen = jnp.where(which == routes_ref[k : k + 1, :], 1.0, chosen)
    return chosen


def turns(chosen):
    earlier = (
        ((iota((TOK, TOK), 0) // 4) == (iota((TOK, TOK), 1) // 4))
        & (iota((TOK, TOK), 0) < iota((TOK, TOK), 1))
    ).astype(F32).astype(BF)
    return jnp.where(chosen > 0, nn(chosen.astype(BF), earlier), -1.0)


def row_of(table, expert):
    return jnp.sum(jnp.where(iota((8, TOK), 0) == expert, table, 0.0), axis=0, keepdims=True)


def pack_rows(my_turn, wanted, valid):
    row = iota((SLOTS * SUB, TOK), 0)
    inside = (iota((SLOTS * SUB, TOK), 1) // 4) == row // SUB
    here = jnp.broadcast_to(my_turn, (SLOTS * SUB, TOK)) == wanted(row % SUB).astype(F32)
    return (inside & here & valid(row % SUB)).astype(F32).astype(BF)


PLACES = (
    (lambda s: s, lambda s: s < 3),
    (lambda s: s - 3, lambda s: (s >= 3) & (s < 6)),
    (lambda s: (s - 6) * 2, lambda s: s >= 6),
    (lambda s: s * 0 + 1, lambda s: s == 6),
)


def expert_kernel(
    place_ref,
    hidden_hbm,
    routes_ref,
    gain_ref,
    gate_up_hbm,
    down_hbm,
    out_ref,
    normed_ref,
    rows_ref,
    slot_ref,
    hidden_ref,
    gate_up_ref,
    down_ref,
    sems,
):
    copies = []
    for m, (hbm, ref) in enumerate(
        ((hidden_hbm, hidden_ref), (gate_up_hbm, gate_up_ref), (down_hbm, down_ref))
    ):
        for n in range(PIECES):
            part = pl.ds(n * PIECE, PIECE)
            copy = pltpu.make_async_copy(hbm.at[part], ref.at[part], sems.at[m * PIECES + n])
            copy.start()
            copies.append(copy)
    down_ref[D:, :] = jnp.zeros((64, HID), BF)
    invert(place_ref, slot_ref)
    owner = (lax.axis_index("x") * 2 + lax.axis_index("yl")) * DEPTH + lax.axis_index("z")
    mine = slot_ref[owner] // DEPTH
    my_turn = row_of(turns(choices(routes_ref)), mine)

    total = jnp.zeros((1, TOK), F32)
    for n in range(PIECES):
        copies[n].wait()
        part = hidden_ref[n * PIECE : (n + 1) * PIECE, :].astype(F32)
        total = total + jnp.sum(part * part, axis=0, keepdims=True)
    factor = lax.rsqrt(total * (1.0 / D) + 1e-05)
    ones = jnp.ones((128, TOK), BF)
    for at in range(0, D, 128):
        size = min(128, D - at)
        gain = gain_ref[:, at : at + size].astype(F32)
        diagonal = jnp.where(
            iota((size, size), 0) == iota((size, size), 1), jnp.broadcast_to(gain, (size, size)), 0.0
        ).astype(BF)
        spread = nn(diagonal, ones[:size])
        part = hidden_ref[at : at + size, :].astype(F32)
        normed_ref[at : at + size, :] = (part * factor * spread).astype(BF)

    projected = jnp.zeros((TOK, 2 * HID), F32)
    for n in range(PIECES):
        copies[PIECES + n].wait()
        part = slice(n * PIECE, (n + 1) * PIECE)
        projected = projected + tn(normed_ref[part, :], gate_up_ref[part, :])
    gate = projected[:, :HID]
    up = projected[:, HID:]
    activated = (gate * jax.nn.sigmoid(1.702 * gate) * (up + 1.0)).astype(BF)
    first, second, third, fourth = (
        nn(pack_rows(my_turn, *place), activated).astype(BF) for place in PLACES
    )
    near = jnp.concatenate([first, second, third], axis=1)
    far = jnp.concatenate([first, second, fourth], axis=1)
    for n in range(PIECES):
        copies[2 * PIECES + n].wait()

    def terms(lhs, at, size, last):
        parts = [down_ref[b : b + size, :] for b in (at, WIDE + at, last)]
        return nt(lhs, jnp.concatenate(parts, axis=1))

    end = 2 * WIDE
    for at in range(0, 512, 256):
        out_ref[:, at : at + 256] = terms(near, at, 256, end + at).astype(BF)
    out_ref[:, 512:640] = jnp.where(
        iota((SLOTS * SUB, 128), 1) < 64,
        terms(near, 512, 128, end + 512),
        terms(far, 512, 128, end - 64),
    ).astype(BF)
    for at in range(640, WIDE, 256):
        out_ref[:, at : at + 256] = terms(far, at, 256, end + at - 576).astype(BF)

    own = (iota((8, TOK), 1) == iota((8, TOK), 0) + owner * 4).astype(F32).astype(BF)
    for at in range(0, D, 640):
        size = min(640, D - at)
        rows_ref[:, at : at + size] = nt(own, hidden_ref[at : at + size, :])


def expert_terms(placement, hidden, routes, gain, gate_up, down):
    whole = pl.BlockSpec(memory_space=VMEM)
    return pl.pallas_call(
        expert_kernel,
        name="expert_terms",
        out_shape=(
            jax.ShapeDtypeStruct((SLOTS * SUB, WIDE), BF),
            jax.ShapeDtypeStruct((D, TOK), BF),
            jax.ShapeDtypeStruct((8, D), F32),
        ),
        in_specs=[
            pl.BlockSpec(memory_space=SMEM),
            pl.BlockSpec(memory_space=pl.ANY),
            whole,
            whole,
            pl.BlockSpec(memory_space=pl.ANY),
            pl.BlockSpec(memory_space=pl.ANY),
        ],
        out_specs=(whole,) * 3,
        scratch_shapes=[
            pltpu.SMEM((SLOTS,), jnp.int32),
            VMEM((D, TOK), BF),
            VMEM((D, 2 * HID), BF),
            VMEM((D + 64, HID), BF),
            pltpu.SemaphoreType.DMA((3 * PIECES,)),
        ],
        compiler_params=params(32),
        cost_estimate=pl.CostEstimate(flops=3 * 10**9, bytes_accessed=8 * 10**6, transcendentals=0),
    )(placement, hidden, routes, gain, gate_up, down)


def weigh_kernel(place_ref, routes_ref, router_ref, normed_ref, out_ref, slot_ref):
    invert(place_ref, slot_ref)
    owner = (lax.axis_index("x") * 2 + lax.axis_index("yl")) * DEPTH + lax.axis_index("z")

    rep = lax.axis_index("yh") * 2 + lax.axis_index("c")
    logits = jnp.zeros((8, TOK), F32)
    for d in range(4):
        start = pl.multiple_of((rep ^ d) * 720, 720)
        logits = logits + nn(router_ref[d], normed_ref[pl.ds(start, 720), :])
    chosen = choices(routes_ref)
    powered = jnp.where(chosen > 0, jnp.exp(logits), 0.0)
    weights = powered / jnp.sum(powered, axis=0, keepdims=True)
    turn = turns(chosen)

    lanes = SLOTS * SUB
    source = iota((8, lanes), 1) // SUB
    sub = iota((8, lanes), 1) % SUB
    expert = jnp.zeros((8, lanes), jnp.int32)
    for o in range(SLOTS):
        expert = jnp.where(source == o, slot_ref[o] // DEPTH, expert)
    match = expert == iota((8, lanes), 0)
    their_turn = jnp.zeros((8, lanes), F32)
    their_weight = jnp.zeros((8, lanes), F32)
    for i in range(4):
        mine = iota((8, TOK), 1) == owner * 4 + i
        token = iota((8, lanes), 0) == i
        for table, kind in ((turn, 0), (weights, 1)):
            column = jnp.sum(jnp.where(mine, table, 0.0), axis=1, keepdims=True)
            row = jnp.sum(jnp.where(match, column, 0.0), axis=0, keepdims=True)
            row = jnp.broadcast_to(row, (8, lanes))
            if kind == 0:
                their_turn = jnp.where(token, row, their_turn)
            else:
                their_weight = jnp.where(token, row, their_weight)
    their_weight = jnp.where(iota((8, lanes), 0) < 4, their_weight, 0.0)
    for n, (wanted, valid) in enumerate(PLACES):
        here = valid(sub) & (their_turn == wanted(sub).astype(F32))
        table = jnp.where(here, their_weight, 0.0)
        upper = table.astype(BF).astype(F32)
        both = jnp.concatenate([upper, table - upper], axis=0)
        out_ref[16 * n : 16 * n + 16, :] = both.astype(BF)


def weigh(placement, routes, router, normed):
    return pl.pallas_call(
        weigh_kernel,
        name="weigh",
        out_shape=jax.ShapeDtypeStruct((64, SLOTS * SUB), BF),
        in_specs=[pl.BlockSpec(memory_space=SMEM)] + [pl.BlockSpec(memory_space=VMEM)] * 3,
        out_specs=pl.BlockSpec(memory_space=VMEM),
        scratch_shapes=[pltpu.SMEM((SLOTS,), jnp.int32)],
        compiler_params=params(16),
        cost_estimate=pl.CostEstimate(flops=10**9, bytes_accessed=2 * 10**6, transcendentals=0),
    )(placement, routes, router, normed)


def finish_kernel(table_ref, got_ref, rows_ref, out_ref):
    mixed = []
    both = nn(table_ref[...], got_ref[...])
    for n in range(4):
        mixed.append(both[16 * n : 16 * n + 8] + both[16 * n + 8 : 16 * n + 16])
    rest = mixed[2] + pltpu.roll(mixed[3], WIDE // 2, 1)
    for at, part in ((0, mixed[0]), (WIDE, mixed[1]), (2 * WIDE, rest)):
        size = min(WIDE, D - at)
        out = rows_ref[:, at : at + size] + part[:, :size]
        out_ref[:, at : at + size] = out[:4].astype(BF)


def finish(table, got, rows):
    return pl.pallas_call(
        finish_kernel,
        name="finish",
        out_shape=jax.ShapeDtypeStruct((4, D), BF),
        in_specs=[pl.BlockSpec(memory_space=VMEM)] * 3,
        out_specs=pl.BlockSpec(memory_space=VMEM),
        compiler_params=params(16),
        cost_estimate=pl.CostEstimate(flops=10**8, bytes_accessed=10**6, transcendentals=0),
    )(table, got, rows)


def on_device(
    master, placement, resident_gate_up, resident_down, hidden, routes, norm_gain, router
):
    chunks = encode(in_hbm(placement), in_hbm(jnp.transpose(master, (2, 0, 1))))
    chunks = lax.all_to_all(chunks, FSDP, split_axis=0, concat_axis=0, tiled=True)

    chosen = routes[0].T
    terms, normed, rows = expert_terms(
        placement,
        in_hbm(hidden[0].T),
        chosen,
        norm_gain[None],
        in_hbm(resident_gate_up[0]),
        in_hbm(resident_down[0].T),
    )
    chunks, terms = lax.optimization_barrier((chunks, terms))
    terms = terms.reshape(SLOTS, SUB, WIDE)
    terms = lax.all_to_all(terms, FSDP, split_axis=0, concat_axis=0, tiled=True)

    across = lax.ppermute(chunks, "yh", ((0, 1), (1, 0)))
    core = lax.ppermute(chunks, "c", ((0, 1), (1, 0)))
    both = lax.ppermute(across, "c", ((0, 1), (1, 0)))
    refreshed = assemble(chunks, across, core, both).T
    router_rows, _ = lax.optimization_barrier((router.T, chunks))
    routers = [router_rows]
    for d in range(1, 4):
        routers.append(lax.ppermute(router_rows, REP, [(r, r ^ d) for r in range(4)]))
    table = weigh(placement, chosen, jnp.stack(routers), normed)
    terms, refreshed, table = lax.optimization_barrier((terms, refreshed, table))
    decoded = finish(table, terms.reshape(SLOTS * SUB, WIDE), rows)
    return (refreshed[None], decoded[None])


def solution(mesh):
    cut = Mesh(mesh.devices.reshape(4, 2, 8, 2, 2), ("x", "yl", "z", "yh", "c"))
    placed = (
        P(None, REP, FSDP),
        P(),
        P(FSDP, None, None),
        P(FSDP, None, None),
        P(REP, None, None),
        P(REP, None, None),
        P(),
        P(REP, None),
    )
    return jax.shard_map(
        on_device,
        mesh=cut,
        in_specs=placed,
        out_specs=(P(FSDP, None, None), P(REP, FSDP, None)),
        check_vma=False,
    )
```

time: 72.1 us -> 71.6 us (level)
  starting transfers between devices: 28.9 us -> 24.5 us
  waiting for transfers between devices: 25.6 us -> 29.6 us
  Pallas kernels: 15.6 us -> 16.5 us
  other arithmetic: 0.79 us -> 0.01 us
    all_to_all x2 -> x1, waiting for transfers between devices: 18.8 us -> 2.39 us  [on_device(): terms = lax.all_to_all(terms, FSDP, split_axis=0, concat_axis=0, tiled=True)]
    ppermute x1, waiting for transfers between devices: 0.01 us -> 14.5 us  [on_device(): across = lax.ppermute(chunks, 'yh', ((0, 1), (1, 0)))]
    all_to_all x1, waiting for transfers between devices: 4.35 us -> 8.72 us  [on_device(): lax.all_to_all(chunks, FSDP, split_axis=0, concat_axis=0, tiled=True)]
    all_to_all x2 -> x1, starting transfers between devices: 9.35 us -> 5.28 us  [on_device(): terms = lax.all_to_all(terms, FSDP, split_axis=0, concat_axis=0, tiled=True)]
    ppermute x3, waiting for transfers between devices: 0.69 us -> 3.95 us  [on_device(): lax.ppermute(router_rows, REP, [(r, r ^ d) for r in range(4)])]
    ppermute x1, waiting for transfers between devices: 1.21 us -> 0.01 us  [on_device(): core = lax.ppermute(chunks, 'c', ((0, 1), (1, 0)))]
    pallas_call x3, Pallas kernels: 8.13 us -> 9.12 us  [the longest x1 6.86 us: expert_terms(): pl.pallas_call(expert_kernel, name='expert_terms', out_shape=(jax.ShapeDt...]
  transfers between devices with their start and end apart: 9 -> 8, of which waited for: 6 -> 5; matrix products, arithmetic and copies ran while one was open for 0% -> 0% of each run, Pallas kernels for 14% -> 15%
where the time goes in v4:
time: 71.6 us; the launch traced here: 71.4 us
  waiting for transfers between devices  29.6 us (41%)
  starting transfers between devices  24.5 us (34%)
  Pallas kernels  16.5 us (23%)
  between operations  0.76 us (1%)
    ppermute x1, waiting for transfers between devices, on_device(): across = lax.ppermute(chunks, 'yh', ((0, 1), (1, 0)))  14.5 us
    all_to_all x1, starting transfers between devices, on_device(): lax.all_to_all(chunks, FSDP, split_axis=0, concat_axis=0, tiled=True)  12.6 us
    all_to_all x1, waiting for transfers between devices, on_device(): lax.all_to_all(chunks, FSDP, split_axis=0, concat_axis=0, tiled=True)  8.72 us
    pallas_call x1, Pallas kernels, expert_terms(): pl.pallas_call(expert_kernel, name='expert_terms', out_shape=(jax.ShapeDt...  6.86 us
    all_to_all x1, starting transfers between devices, on_device(): terms = lax.all_to_all(terms, FSDP, split_axis=0, concat_axis=0, tiled=True)  5.28 us
    pallas_call x1, Pallas kernels, encode(): pl.pallas_call(encode_kernel, name='encode', out_shape=jax.ShapeDtypeStru...  5.11 us
    ppermute x3, waiting for transfers between devices, on_device(): lax.ppermute(router_rows, REP, [(r, r ^ d) for r in range(4)])  3.95 us
    ppermute x3, starting transfers between devices, on_device(): lax.ppermute(router_rows, REP, [(r, r ^ d) for r in range(4)])  3.64 us
  transfers between devices with their start and end apart: 8, of which 5 were waited for; matrix products, arithmetic and copies ran while one was open for 0% of the time, Pallas kernels for 15%

profile of v4, /device:TPU:32, one launch (start us, length us, event | category | flops | bytes accessed | tf_op | source)
XLA Modules:
  0.0 71.4 jit_solution(12364601317877480124)
XLA Ops:
  0.6 0.0 copy-start.3
  0.6 0.0 copy-start
  0.7 0.0 copy-start.1
  0.7 5.1 %encode.1 = bf16[64,24,128]{2,1,0:T(8,128)(2,1)} custom-call(s32[64]{0:T(128)} %place_ref.3, f32[45,64,64]{2,1,0:T(8,128)} %bitcast.33), custom_call_target="tpu_custom_call" | custom-call | flops 1000000000 | bytes 4000000 | tf_op jit(solution)/shard_map/encode/pallas_call | solution.py:127
  5.8 12.6 %all-to-all-start = ((bf16[64,24,128]{2,1,0:T(8,128)(2,1)}), bf16[64,24,128]{2,1,0:T(8,128)(2,1)S(1)}, u32[]{:S(2)}, u32[]{:S(2)}) async-start(bf16[64,24,128]{2,1,0:T(8,128)(2,1)} %encode.1), calls=%async_computation | async-start | bytes 786432 | tf_op jit(solution)/shard_map/all_to_all | solution.py:418
  18.4 0.0 copy-done.3
  18.4 0.0 copy-done
  18.4 0.0 copy-done.1
  18.4 6.9 %expert_terms.1 = (bf16[512,1152]{1,0:T(8,128)(2,1)}, bf16[2880,256]{1,0:T(8,128)(2,1)S(1)}, f32[8,2880]{1,0:T(8,128)S(1)}) custom-call(s32[64]{0:T(128)S(1)} %copy-done.1, bf16[2880,256]{1,0:T(8,128)(2,1)} %bitcast.34, s32[4,256]{1,0:T(4,128)S(1)} %bitcast.22, bf16[1,2880]{1,0:T(2,128)(2,1)S(1)} %broadcast_in_dim.9.gain_ref, bf16[2880,512]{1,0:T(8,128)(2,1)} %bitcast.32, ...), custom_call_target="tpu_custom_call" | custom-call | flops 3000000000 | bytes 8000000 | tf_op jit(solution)/shard_map/expert_terms/pallas_call | solution.py:305
  25.3 0.0 copy-start.2
  25.3 8.7 %all-to-all-done.own_ref = bf16[64,24,128]{2,1,0:T(8,128)(2,1)S(1)} async-done(((bf16[64,24,128]{2,1,0:T(8,128)(2,1)}), bf16[64,24,128]{2,1,0:T(8,128)(2,1)S(1)}, u32[]{:S(2)}, u32[]{:S(2)}) %all-to-all-start) | async-done | bytes 393248 | tf_op jit(solution)/shard_map/all_to_all | solution.py:418
  34.0 5.3 %all-to-all-start.1 = ((bf16[64,8,1152]{2,1,0:T(8,128)(2,1)}), bf16[64,8,1152]{2,1,0:T(8,128)(2,1)S(1)}, u32[]{:S(2)}, u32[]{:S(2)}) async-start(bf16[64,8,1152]{2,1,0:T(8,128)(2,1)} %bitcast.8), calls=%async_computation.1 | async-start | bytes 2359296 | tf_op jit(solution)/shard_map/all_to_all | solution.py:431
  39.3 3.0 %collective-permute-start = (bf16[64,24,128]{2,1,0:T(8,128)(2,1)S(1)}, bf16[64,24,128]{2,1,0:T(8,128)(2,1)S(1)}, u32[]{:S(2)}, u32[]{:S(2)}) collective-permute-start(bf16[64,24,128]{2,1,0:T(8,128)(2,1)S(1)} %all-to-all-done.own_ref), channel_id=1, source_target_pairs={{0,2},{2,0},{1,3},{3,1},{4,6},{6,4},{5,7},{7,5},{8,10},{10,8},{9,1... | collective-permute-start | bytes 1179656 | tf_op jit(solution)/shard_map/ppermute | solution.py:433
  42.3 0.0 collective-permute-start.1
  42.3 14.5 %collective-permute-done.across_ref = bf16[64,24,128]{2,1,0:T(8,128)(2,1)S(1)} collective-permute-done((bf16[64,24,128]{2,1,0:T(8,128)(2,1)S(1)}, bf16[64,24,128]{2,1,0:T(8,128)(2,1)S(1)}, u32[]{:S(2)}, u32[]{:S(2)}) %collective-permute-start) | collective-permute-done | bytes 393248 | tf_op jit(solution)/shard_map/ppermute | solution.py:433
  56.8 0.0 collective-permute-start.2
  56.8 0.0 copy-done.2
  56.8 2.2 %collective-permute-start.5 = (bf16[8,720]{1,0:T(8,128)(2,1)S(1)}, bf16[8,720]{1,0:T(8,128)(2,1)S(1)}, u32[]{:S(2)}, u32[]{:S(2)}) collective-permute-start(bf16[8,720]{1,0:T(8,128)(2,1)S(1)} %bitcast.25), channel_id=1, source_target_pairs={{0,3},{1,2},{2,1},{3,0},{4,7},{5,6},{6,5},{7,4},{8,11},{9,10},{10,... | collective-permute-start | bytes 34568 | tf_op jit(solution)/shard_map/ppermute | solution.py:440
  59.0 1.5 %collective-permute-start.4 = (bf16[8,720]{1,0:T(8,128)(2,1)S(1)}, bf16[8,720]{1,0:T(8,128)(2,1)S(1)}, u32[]{:S(2)}, u32[]{:S(2)}) collective-permute-start(bf16[8,720]{1,0:T(8,128)(2,1)S(1)} %bitcast.26), channel_id=1, source_target_pairs={{0,2},{1,3},{2,0},{3,1},{4,6},{5,7},{6,4},{7,5},{8,10},{9,11},{10,... | collective-permute-start | bytes 34568 | tf_op jit(solution)/shard_map/ppermute | solution.py:440
  60.5 0.0 collective-permute-start.3
  60.5 1.0 %collective-permute-done.5 = bf16[8,720]{1,0:T(8,128)(2,1)S(1)} collective-permute-done((bf16[8,720]{1,0:T(8,128)(2,1)S(1)}, bf16[8,720]{1,0:T(8,128)(2,1)S(1)}, u32[]{:S(2)}, u32[]{:S(2)}) %collective-permute-start.5) | collective-permute-done | bytes 11552 | tf_op jit(solution)/shard_map/ppermute | solution.py:440
  61.5 2.9 %collective-permute-done.4 = bf16[8,720]{1,0:T(8,128)(2,1)S(1)} collective-permute-done((bf16[8,720]{1,0:T(8,128)(2,1)S(1)}, bf16[8,720]{1,0:T(8,128)(2,1)S(1)}, u32[]{:S(2)}, u32[]{:S(2)}) %collective-permute-start.4) | collective-permute-done | bytes 11552 | tf_op jit(solution)/shard_map/ppermute | solution.py:440
  64.4 0.0 collective-permute-done.3
  64.4 1.2 %weigh.1.table_ref = bf16[64,512]{1,0:T(8,128)(2,1)S(1)} custom-call(s32[64]{0:T(128)S(1)} %copy-done.1, s32[4,256]{1,0:T(4,128)S(1)} %bitcast.23, bf16[4,8,720]{2,1,0:T(8,128)(2,1)S(1)} %pad_maximum_fusion.router_ref, bf16[2880,256]{1,0:T(8,128)(2,1)S(1)} %get-tuple-element.15.normed_ref), custom_call_target="tpu_custom_call" | custom-call | flops 1000000000 | bytes 2000000 | tf_op jit(solution)/shard_map/weigh/pallas_call | solution.py:378
  65.7 0.0 collective-permute-done.1.core_ref
  65.7 0.0 collective-permute-done.2.both_ref
  65.7 2.3 %assemble.1 = bf16[2880,256]{1,0:T(8,128)(2,1)} custom-call(bf16[64,24,128]{2,1,0:T(8,128)(2,1)S(1)} %all-to-all-done.own_ref, bf16[64,24,128]{2,1,0:T(8,128)(2,1)S(1)} %collective-permute-done.across_ref, bf16[64,24,128]{2,1,0:T(8,128)(2,1)S(1)} %collective-permute-done.1.core_ref, bf16[64,24,128]{2,1,0:T(8,128)(2,1)S(1)} %collective-permute-done.2.both_ref), custom_call_target="tpu_custom_call" | custom-call | flops 1000000000 | bytes 4000000 | tf_op jit(solution)/shard_map/assemble/pallas_call | solution.py:170
  68.0 2.4 %all-to-all-done.1 = bf16[64,8,1152]{2,1,0:T(8,128)(2,1)S(1)} async-done(((bf16[64,8,1152]{2,1,0:T(8,128)(2,1)}), bf16[64,8,1152]{2,1,0:T(8,128)(2,1)S(1)}, u32[]{:S(2)}, u32[]{:S(2)}) %all-to-all-start.1) | async-done | bytes 1179680 | tf_op jit(solution)/shard_map/all_to_all | solution.py:431
  70.4 1.0 %finish.1 = bf16[4,2880]{1,0:T(4,128)(2,1)} custom-call(bf16[64,512]{1,0:T(8,128)(2,1)S(1)} %weigh.1.table_ref, bf16[512,1152]{1,0:T(8,128)(2,1)S(1)} %bitcast.21, f32[8,2880]{1,0:T(8,128)S(1)} %get-tuple-element.19.rows_ref), custom_call_target="tpu_custom_call" | custom-call | flops 100000000 | bytes 1000000 | tf_op jit(solution)/shard_map/finish/pallas_call | solution.py:403
  (2 shorter events, 0.0 us)
Async XLA Ops:
  0.6 17.8 %copy-start.3 = (bf16[2880]{0:T(1024)(128)(2,1)S(1)}, bf16[2880]{0:T(1024)(128)(2,1)}, u32[]{:S(2)}) copy-start(bf16[2880]{0:T(1024)(128)(2,1)} %param.14) | copy-start | bytes 17284
  0.6 17.8 %copy-start = (s32[1,256,4]{1,2,0:T(4,128)S(1)}, s32[1,256,4]{1,2,0:T(4,128)}, u32[]{:S(2)}) copy-start(s32[1,256,4]{1,2,0:T(4,128)} %param.13) | copy-start | bytes 12292
  0.7 17.8 %copy-start.1 = (s32[64]{0:T(128)S(1)}, s32[64]{0:T(128)}, u32[]{:S(2)}) copy-start(s32[64]{0:T(128)} %place_ref.3) | copy-start | bytes 772
  5.8 28.3 %all-to-all-start = ((bf16[64,24,128]{2,1,0:T(8,128)(2,1)}), bf16[64,24,128]{2,1,0:T(8,128)(2,1)S(1)}, u32[]{:S(2)}, u32[]{:S(2)}) async-start(bf16[64,24,128]{2,1,0:T(8,128)(2,1)} %encode.1), calls=%async_computation | async-start | bytes 786432 | tf_op jit(solution)/shard_map/all_to_all | solution.py:418
  25.3 31.5 %copy-start.2 = (bf16[720,8]{0,1:T(8,128)(2,1)S(1)}, bf16[720,8]{0,1:T(8,128)(2,1)}, u32[]{:S(2)}) copy-start(bf16[720,8]{0,1:T(8,128)(2,1)} %param.15) | copy-start | bytes 34564
  34.0 36.3 %all-to-all-start.1 = ((bf16[64,8,1152]{2,1,0:T(8,128)(2,1)}), bf16[64,8,1152]{2,1,0:T(8,128)(2,1)S(1)}, u32[]{:S(2)}, u32[]{:S(2)}) async-start(bf16[64,8,1152]{2,1,0:T(8,128)(2,1)} %bitcast.8), calls=%async_computation.1 | async-start | bytes 2359296 | tf_op jit(solution)/shard_map/all_to_all | solution.py:431
  39.3 17.5 %collective-permute-start = (bf16[64,24,128]{2,1,0:T(8,128)(2,1)S(1)}, bf16[64,24,128]{2,1,0:T(8,128)(2,1)S(1)}, u32[]{:S(2)}, u32[]{:S(2)}) collective-permute-start(bf16[64,24,128]{2,1,0:T(8,128)(2,1)S(1)} %all-to-all-done.own_ref), channel_id=1, source_target_pairs={{0,2},{2,0},{1,3},{3,1},{4,6},{6,4},{5,7},{7,5},{8,10},{10,8},{9,1... | collective-permute-start | bytes 1179656 | tf_op jit(solution)/shard_map/ppermute | solution.py:433
  42.3 23.4 %collective-permute-start.1 = (bf16[64,24,128]{2,1,0:T(8,128)(2,1)S(1)}, bf16[64,24,128]{2,1,0:T(8,128)(2,1)S(1)}, u32[]{:S(2)}, u32[]{:S(2)}) collective-permute-start(bf16[64,24,128]{2,1,0:T(8,128)(2,1)S(1)} %all-to-all-done.own_ref), channel_id=1, source_target_pairs={{0,1},{1,0},{2,3},{3,2},{4,5},{5,4},{6,7},{7,6},{8,9},{9,8},{10,11... | collective-permute-start | bytes 1179656 | tf_op jit(solution)/shard_map/ppermute | solution.py:434
  56.8 8.9 %collective-permute-start.2 = (bf16[64,24,128]{2,1,0:T(8,128)(2,1)S(1)}, bf16[64,24,128]{2,1,0:T(8,128)(2,1)S(1)}, u32[]{:S(2)}, u32[]{:S(2)}) collective-permute-start(bf16[64,24,128]{2,1,0:T(8,128)(2,1)S(1)} %collective-permute-done.across_ref), channel_id=1, source_target_pairs={{0,1},{1,0},{2,3},{3,2},{4,5},{5,4},{6,7},{7,6},{8,9},{9,8},{10,11... | collective-permute-start | bytes 1179656 | tf_op jit(solution)/shard_map/ppermute | solution.py:435
  56.8 4.7 %collective-permute-start.5 = (bf16[8,720]{1,0:T(8,128)(2,1)S(1)}, bf16[8,720]{1,0:T(8,128)(2,1)S(1)}, u32[]{:S(2)}, u32[]{:S(2)}) collective-permute-start(bf16[8,720]{1,0:T(8,128)(2,1)S(1)} %bitcast.25), channel_id=1, source_target_pairs={{0,3},{1,2},{2,1},{3,0},{4,7},{5,6},{6,5},{7,4},{8,11},{9,10},{10,... | collective-permute-start | bytes 34568 | tf_op jit(solution)/shard_map/ppermute | solution.py:440
  59.0 5.4 %collective-permute-start.4 = (bf16[8,720]{1,0:T(8,128)(2,1)S(1)}, bf16[8,720]{1,0:T(8,128)(2,1)S(1)}, u32[]{:S(2)}, u32[]{:S(2)}) collective-permute-start(bf16[8,720]{1,0:T(8,128)(2,1)S(1)} %bitcast.26), channel_id=1, source_target_pairs={{0,2},{1,3},{2,0},{3,1},{4,6},{5,7},{6,4},{7,5},{8,10},{9,11},{10,... | collective-permute-start | bytes 34568 | tf_op jit(solution)/shard_map/ppermute | solution.py:440
  60.5 4.0 %collective-permute-start.3 = (bf16[8,720]{1,0:T(8,128)(2,1)S(1)}, bf16[8,720]{1,0:T(8,128)(2,1)S(1)}, u32[]{:S(2)}, u32[]{:S(2)}) collective-permute-start(bf16[8,720]{1,0:T(8,128)(2,1)S(1)} %bitcast.27), channel_id=1, source_target_pairs={{0,1},{1,0},{2,3},{3,2},{4,5},{5,4},{6,7},{7,6},{8,9},{9,8},{10,11... | collective-permute-start | bytes 34568 | tf_op jit(solution)/shard_map/ppermute | solution.py:440

commit v5 on v4

--- a/solution.py
+++ b/solution.py
@@ -415,6 +415,7 @@
     master, placement, resident_gate_up, resident_down, hidden, routes, norm_gain, router
 ):
     chunks = encode(in_hbm(placement), in_hbm(jnp.transpose(master, (2, 0, 1))))
+    router_rows, chunks = lax.optimization_barrier((router.T, chunks))
     chunks = lax.all_to_all(chunks, FSDP, split_axis=0, concat_axis=0, tiled=True)
 
     chosen = routes[0].T
@@ -426,7 +427,11 @@
         in_hbm(resident_gate_up[0]),
         in_hbm(resident_down[0].T),
     )
-    chunks, terms = lax.optimization_barrier((chunks, terms))
+    routers = [router_rows]
+    for d in range(1, 4):
+        routers.append(lax.ppermute(router_rows, REP, [(r, r ^ d) for r in range(4)]))
+    table = weigh(placement, chosen, jnp.stack(routers), normed)
+    chunks, terms, table = lax.optimization_barrier((chunks, terms, table))
     terms = terms.reshape(SLOTS, SUB, WIDE)
     terms = lax.all_to_all(terms, FSDP, split_axis=0, concat_axis=0, tiled=True)
 
@@ -434,12 +439,7 @@
     core = lax.ppermute(chunks, "c", ((0, 1), (1, 0)))
     both = lax.ppermute(across, "c", ((0, 1), (1, 0)))
     refreshed = assemble(chunks, across, core, both).T
-    router_rows, _ = lax.optimization_barrier((router.T, chunks))
-    routers = [router_rows]
-    for d in range(1, 4):
-        routers.append(lax.ppermute(router_rows, REP, [(r, r ^ d) for r in range(4)]))
-    table = weigh(placement, chosen, jnp.stack(routers), normed)
-    terms, refreshed, table = lax.optimization_barrier((terms, refreshed, table))
+    terms, refreshed = lax.optimization_barrier((terms, refreshed))
     decoded = finish(table, terms.reshape(SLOTS * SUB, WIDE), rows)
     return (refreshed[None], decoded[None])
 

time: 71.6 us -> 75 us (1.047)
  starting transfers between devices: 24.5 us -> 26.4 us
  waiting for transfers between devices: 29.6 us -> 30.7 us
    all_to_all x1, waiting for transfers between devices: 2.39 us -> 9.46 us  [on_device(): terms = lax.all_to_all(terms, FSDP, split_axis=0, concat_axis=0, tiled=True)]
    all_to_all x1, waiting for transfers between devices: 8.72 us -> 3.98 us  [on_device(): lax.all_to_all(chunks, FSDP, split_axis=0, concat_axis=0, tiled=True)]
    ppermute x3, waiting for transfers between devices: 3.95 us -> 0.01 us  [on_device(): lax.ppermute(router_rows, REP, [(r, r ^ d) for r in range(4)])]
    all_to_all x1, starting transfers between devices: 5.28 us -> 7.3 us  [on_device(): terms = lax.all_to_all(terms, FSDP, split_axis=0, concat_axis=0, tiled=True)]
    ppermute x1, waiting for transfers between devices: 0.01 us -> 1.72 us  [on_device(): both = lax.ppermute(across, 'c', ((0, 1), (1, 0)))]
    ppermute x1, waiting for transfers between devices: 14.5 us -> 15.6 us  [on_device(): across = lax.ppermute(chunks, 'yh', ((0, 1), (1, 0)))]
  transfers between devices with their start and end apart: 8 -> 8, of which waited for: 5 -> 4; matrix products, arithmetic and copies ran while one was open for 0% -> 0% of each run, Pallas kernels for 15% -> 14%
where the time goes in v5:
time: 75 us; the launch traced here: 74.4 us
  waiting for transfers between devices  30.7 us (41%)
  starting transfers between devices  26.4 us (35%)
  Pallas kernels  16.5 us (22%)
  between operations  0.77 us (1%)
    ppermute x1, waiting for transfers between devices, on_device(): across = lax.ppermute(chunks, 'yh', ((0, 1), (1, 0)))  15.6 us
    all_to_all x1, starting transfers between devices, on_device(): lax.all_to_all(chunks, FSDP, split_axis=0, concat_axis=0, tiled=True)  12.6 us
    all_to_all x1, waiting for transfers between devices, on_device(): terms = lax.all_to_all(terms, FSDP, split_axis=0, concat_axis=0, tiled=True)  9.46 us
    all_to_all x1, starting transfers between devices, on_device(): terms = lax.all_to_all(terms, FSDP, split_axis=0, concat_axis=0, tiled=True)  7.3 us
    pallas_call x1, Pallas kernels, expert_terms(): pl.pallas_call(expert_kernel, name='expert_terms', out_shape=(jax.ShapeDt...  6.87 us
    pallas_call x1, Pallas kernels, encode(): pl.pallas_call(encode_kernel, name='encode', out_shape=jax.ShapeDtypeStru...  5.11 us
    all_to_all x1, waiting for transfers between devices, on_device(): lax.all_to_all(chunks, FSDP, split_axis=0, concat_axis=0, tiled=True)  3.98 us
    ppermute x3, starting transfers between devices, on_device(): lax.ppermute(router_rows, REP, [(r, r ^ d) for r in range(4)])  3.45 us
  transfers between devices with their start and end apart: 8, of which 4 were waited for; matrix products, arithmetic and copies ran while one was open for 0% of the time, Pallas kernels for 14%

profile of v5, /device:TPU:32, one launch (start us, length us, event | category | flops | bytes accessed | tf_op | source)
XLA Modules:
  0.0 74.4 jit_solution(11837314959791533954)
XLA Ops:
  0.6 0.0 copy-start.2
  0.6 0.0 copy-start.3
  0.7 0.0 copy-start
  0.7 0.0 copy-start.1
  0.7 5.1 %encode.1 = bf16[64,24,128]{2,1,0:T(8,128)(2,1)} custom-call(s32[64]{0:T(128)} %place_ref.3, f32[45,64,64]{2,1,0:T(8,128)} %bitcast.33), custom_call_target="tpu_custom_call" | custom-call | flops 1000000000 | bytes 4000000 | tf_op jit(solution)/shard_map/encode/pallas_call | solution.py:127
  5.8 12.6 %all-to-all-start = ((bf16[64,24,128]{2,1,0:T(8,128)(2,1)}), bf16[64,24,128]{2,1,0:T(8,128)(2,1)S(1)}, u32[]{:S(2)}, u32[]{:S(2)}) async-start(bf16[64,24,128]{2,1,0:T(8,128)(2,1)} %encode.1), calls=%async_computation | async-start | bytes 786432 | tf_op jit(solution)/shard_map/all_to_all | solution.py:419
  18.4 0.0 copy-done.2
  18.4 1.9 %collective-permute-start.2 = (bf16[8,720]{1,0:T(8,128)(2,1)S(1)}, bf16[8,720]{1,0:T(8,128)(2,1)S(1)}, u32[]{:S(2)}, u32[]{:S(2)}) collective-permute-start(bf16[8,720]{1,0:T(8,128)(2,1)S(1)} %bitcast.25), channel_id=1, source_target_pairs={{0,3},{1,2},{2,1},{3,0},{4,7},{5,6},{6,5},{7,4},{8,11},{9,10},{10,... | collective-permute-start | bytes 34568 | tf_op jit(solution)/shard_map/ppermute | solution.py:432
  20.3 1.2 %collective-permute-start.1 = (bf16[8,720]{1,0:T(8,128)(2,1)S(1)}, bf16[8,720]{1,0:T(8,128)(2,1)S(1)}, u32[]{:S(2)}, u32[]{:S(2)}) collective-permute-start(bf16[8,720]{1,0:T(8,128)(2,1)S(1)} %bitcast.26), channel_id=1, source_target_pairs={{0,2},{1,3},{2,0},{3,1},{4,6},{5,7},{6,4},{7,5},{8,10},{9,11},{10,... | collective-permute-start | bytes 34568 | tf_op jit(solution)/shard_map/ppermute | solution.py:432
  21.5 0.4 collective-permute-start
  21.9 0.0 copy-done.3
  21.9 0.0 copy-done
  21.9 0.0 copy-done.1
  21.9 6.9 %expert_terms.1 = (bf16[512,1152]{1,0:T(8,128)(2,1)}, bf16[2880,256]{1,0:T(8,128)(2,1)S(1)}, f32[8,2880]{1,0:T(8,128)S(1)}) custom-call(s32[64]{0:T(128)S(1)} %copy-done.1, bf16[2880,256]{1,0:T(8,128)(2,1)} %bitcast.34, s32[4,256]{1,0:T(4,128)S(1)} %bitcast.22, bf16[1,2880]{1,0:T(2,128)(2,1)S(1)} %broadcast_in_dim.9.gain_ref, bf16[2880,512]{1,0:T(8,128)(2,1)} %bitcast.32, ...), custom_call_target="tpu_custom_call" | custom-call | flops 3000000000 | bytes 8000000 | tf_op jit(solution)/shard_map/expert_terms/pallas_call | solution.py:305
  28.8 0.0 collective-permute-done.2
  28.8 0.0 collective-permute-done.1
  28.8 0.0 collective-permute-done
  28.8 1.2 %weigh.1.table_ref = bf16[64,512]{1,0:T(8,128)(2,1)S(1)} custom-call(s32[64]{0:T(128)S(1)} %copy-done.1, s32[4,256]{1,0:T(4,128)S(1)} %bitcast.23, bf16[4,8,720]{2,1,0:T(8,128)(2,1)S(1)} %pad_maximum_fusion.router_ref, bf16[2880,256]{1,0:T(8,128)(2,1)S(1)} %get-tuple-element.15.normed_ref), custom_call_target="tpu_custom_call" | custom-call | flops 1000000000 | bytes 2000000 | tf_op jit(solution)/shard_map/weigh/pallas_call | solution.py:378
  30.1 4.0 %all-to-all-done.own_ref = bf16[64,24,128]{2,1,0:T(8,128)(2,1)S(1)} async-done(((bf16[64,24,128]{2,1,0:T(8,128)(2,1)}), bf16[64,24,128]{2,1,0:T(8,128)(2,1)S(1)}, u32[]{:S(2)}, u32[]{:S(2)}) %all-to-all-start) | async-done | bytes 393248 | tf_op jit(solution)/shard_map/all_to_all | solution.py:419
  34.1 7.3 %all-to-all-start.1 = ((bf16[64,8,1152]{2,1,0:T(8,128)(2,1)}), bf16[64,8,1152]{2,1,0:T(8,128)(2,1)S(1)}, u32[]{:S(2)}, u32[]{:S(2)}) async-start(bf16[64,8,1152]{2,1,0:T(8,128)(2,1)} %bitcast.14), calls=%async_computation.1 | async-start | bytes 2359296 | tf_op jit(solution)/shard_map/all_to_all | solution.py:436
  41.4 3.0 %collective-permute-start.3 = (bf16[64,24,128]{2,1,0:T(8,128)(2,1)S(1)}, bf16[64,24,128]{2,1,0:T(8,128)(2,1)S(1)}, u32[]{:S(2)}, u32[]{:S(2)}) collective-permute-start(bf16[64,24,128]{2,1,0:T(8,128)(2,1)S(1)} %all-to-all-done.own_ref), channel_id=1, source_target_pairs={{0,2},{2,0},{1,3},{3,1},{4,6},{6,4},{5,7},{7,5},{8,10},{10,8},{9,1... | collective-permute-start | bytes 1179656 | tf_op jit(solution)/shard_map/ppermute | solution.py:438
  44.4 0.0 collective-permute-start.4
  44.4 15.6 %collective-permute-done.3.across_ref = bf16[64,24,128]{2,1,0:T(8,128)(2,1)S(1)} collective-permute-done((bf16[64,24,128]{2,1,0:T(8,128)(2,1)S(1)}, bf16[64,24,128]{2,1,0:T(8,128)(2,1)S(1)}, u32[]{:S(2)}, u32[]{:S(2)}) %collective-permute-start.3) | collective-permute-done | bytes 393248 | tf_op jit(solution)/shard_map/ppermute | solution.py:438
  59.9 0.0 collective-permute-start.5
  59.9 0.0 collective-permute-done.4.core_ref
  59.9 1.7 %collective-permute-done.5.both_ref = bf16[64,24,128]{2,1,0:T(8,128)(2,1)S(1)} collective-permute-done((bf16[64,24,128]{2,1,0:T(8,128)(2,1)S(1)}, bf16[64,24,128]{2,1,0:T(8,128)(2,1)S(1)}, u32[]{:S(2)}, u32[]{:S(2)}) %collective-permute-start.5) | collective-permute-done | bytes 393248 | tf_op jit(solution)/shard_map/ppermute | solution.py:440
  61.7 2.2 %assemble.1 = bf16[2880,256]{1,0:T(8,128)(2,1)} custom-call(bf16[64,24,128]{2,1,0:T(8,128)(2,1)S(1)} %all-to-all-done.own_ref, bf16[64,24,128]{2,1,0:T(8,128)(2,1)S(1)} %collective-permute-done.3.across_ref, bf16[64,24,128]{2,1,0:T(8,128)(2,1)S(1)} %collective-permute-done.4.core_ref, bf16[64,24,128]{2,1,0:T(8,128)(2,1)S(1)} %collective-permute-done.5.both_ref), custom_call_target="tpu_custom_call" | custom-call | flops 1000000000 | bytes 4000000 | tf_op jit(solution)/shard_map/assemble/pallas_call | solution.py:170
  63.9 9.5 %all-to-all-done.1 = bf16[64,8,1152]{2,1,0:T(8,128)(2,1)S(1)} async-done(((bf16[64,8,1152]{2,1,0:T(8,128)(2,1)}), bf16[64,8,1152]{2,1,0:T(8,128)(2,1)S(1)}, u32[]{:S(2)}, u32[]{:S(2)}) %all-to-all-start.1) | async-done | bytes 1179680 | tf_op jit(solution)/shard_map/all_to_all | solution.py:436
  73.4 1.0 %finish.1 = bf16[4,2880]{1,0:T(4,128)(2,1)} custom-call(bf16[64,512]{1,0:T(8,128)(2,1)S(1)} %weigh.1.table_ref, bf16[512,1152]{1,0:T(8,128)(2,1)S(1)} %bitcast.21, f32[8,2880]{1,0:T(8,128)S(1)} %get-tuple-element.21.rows_ref), custom_call_target="tpu_custom_call" | custom-call | flops 100000000 | bytes 1000000 | tf_op jit(solution)/shard_map/finish/pallas_call | solution.py:403
  (2 shorter events, 0.0 us)
Async XLA Ops:
  0.6 17.8 %copy-start.2 = (bf16[720,8]{0,1:T(8,128)(2,1)S(1)}, bf16[720,8]{0,1:T(8,128)(2,1)}, u32[]{:S(2)}) copy-start(bf16[720,8]{0,1:T(8,128)(2,1)} %param.15) | copy-start | bytes 34564
  0.6 21.2 %copy-start.3 = (bf16[2880]{0:T(1024)(128)(2,1)S(1)}, bf16[2880]{0:T(1024)(128)(2,1)}, u32[]{:S(2)}) copy-start(bf16[2880]{0:T(1024)(128)(2,1)} %param.14) | copy-start | bytes 17284
  0.7 21.2 %copy-start = (s32[1,256,4]{1,2,0:T(4,128)S(1)}, s32[1,256,4]{1,2,0:T(4,128)}, u32[]{:S(2)}) copy-start(s32[1,256,4]{1,2,0:T(4,128)} %param.13) | copy-start | bytes 12292
  0.7 21.2 %copy-start.1 = (s32[64]{0:T(128)S(1)}, s32[64]{0:T(128)}, u32[]{:S(2)}) copy-start(s32[64]{0:T(128)} %place_ref.3) | copy-start | bytes 772
  5.8 28.3 %all-to-all-start = ((bf16[64,24,128]{2,1,0:T(8,128)(2,1)}), bf16[64,24,128]{2,1,0:T(8,128)(2,1)S(1)}, u32[]{:S(2)}, u32[]{:S(2)}) async-start(bf16[64,24,128]{2,1,0:T(8,128)(2,1)} %encode.1), calls=%async_computation | async-start | bytes 786432 | tf_op jit(solution)/shard_map/all_to_all | solution.py:419
  18.4 10.4 %collective-permute-start.2 = (bf16[8,720]{1,0:T(8,128)(2,1)S(1)}, bf16[8,720]{1,0:T(8,128)(2,1)S(1)}, u32[]{:S(2)}, u32[]{:S(2)}) collective-permute-start(bf16[8,720]{1,0:T(8,128)(2,1)S(1)} %bitcast.25), channel_id=1, source_target_pairs={{0,3},{1,2},{2,1},{3,0},{4,7},{5,6},{6,5},{7,4},{8,11},{9,10},{10,... | collective-permute-start | bytes 34568 | tf_op jit(solution)/shard_map/ppermute | solution.py:432
  20.3 8.5 %collective-permute-start.1 = (bf16[8,720]{1,0:T(8,128)(2,1)S(1)}, bf16[8,720]{1,0:T(8,128)(2,1)S(1)}, u32[]{:S(2)}, u32[]{:S(2)}) collective-permute-start(bf16[8,720]{1,0:T(8,128)(2,1)S(1)} %bitcast.26), channel_id=1, source_target_pairs={{0,2},{1,3},{2,0},{3,1},{4,6},{5,7},{6,4},{7,5},{8,10},{9,11},{10,... | collective-permute-start | bytes 34568 | tf_op jit(solution)/shard_map/ppermute | solution.py:432
  21.5 7.3 %collective-permute-start = (bf16[8,720]{1,0:T(8,128)(2,1)S(1)}, bf16[8,720]{1,0:T(8,128)(2,1)S(1)}, u32[]{:S(2)}, u32[]{:S(2)}) collective-permute-start(bf16[8,720]{1,0:T(8,128)(2,1)S(1)} %bitcast.27), channel_id=1, source_target_pairs={{0,1},{1,0},{2,3},{3,2},{4,5},{5,4},{6,7},{7,6},{8,9},{9,8},{10,11... | collective-permute-start | bytes 34568 | tf_op jit(solution)/shard_map/ppermute | solution.py:432
  34.1 39.3 %all-to-all-start.1 = ((bf16[64,8,1152]{2,1,0:T(8,128)(2,1)}), bf16[64,8,1152]{2,1,0:T(8,128)(2,1)S(1)}, u32[]{:S(2)}, u32[]{:S(2)}) async-start(bf16[64,8,1152]{2,1,0:T(8,128)(2,1)} %bitcast.14), calls=%async_computation.1 | async-start | bytes 2359296 | tf_op jit(solution)/shard_map/all_to_all | solution.py:436
  41.4 18.6 %collective-permute-start.3 = (bf16[64,24,128]{2,1,0:T(8,128)(2,1)S(1)}, bf16[64,24,128]{2,1,0:T(8,128)(2,1)S(1)}, u32[]{:S(2)}, u32[]{:S(2)}) collective-permute-start(bf16[64,24,128]{2,1,0:T(8,128)(2,1)S(1)} %all-to-all-done.own_ref), channel_id=1, source_target_pairs={{0,2},{2,0},{1,3},{3,1},{4,6},{6,4},{5,7},{7,5},{8,10},{10,8},{9,1... | collective-permute-start | bytes 1179656 | tf_op jit(solution)/shard_map/ppermute | solution.py:438
  44.4 15.6 %collective-permute-start.4 = (bf16[64,24,128]{2,1,0:T(8,128)(2,1)S(1)}, bf16[64,24,128]{2,1,0:T(8,128)(2,1)S(1)}, u32[]{:S(2)}, u32[]{:S(2)}) collective-permute-start(bf16[64,24,128]{2,1,0:T(8,128)(2,1)S(1)} %all-to-all-done.own_ref), channel_id=1, source_target_pairs={{0,1},{1,0},{2,3},{3,2},{4,5},{5,4},{6,7},{7,6},{8,9},{9,8},{10,11... | collective-permute-start | bytes 1179656 | tf_op jit(solution)/shard_map/ppermute | solution.py:439
  59.9 1.7 %collective-permute-start.5 = (bf16[64,24,128]{2,1,0:T(8,128)(2,1)S(1)}, bf16[64,24,128]{2,1,0:T(8,128)(2,1)S(1)}, u32[]{:S(2)}, u32[]{:S(2)}) collective-permute-start(bf16[64,24,128]{2,1,0:T(8,128)(2,1)S(1)} %collective-permute-done.3.across_ref), channel_id=1, source_target_pairs={{0,1},{1,0},{2,3},{3,2},{4,5},{5,4},{6,7},{7,6},{8,9},{9,8},{10,11... | collective-permute-start | bytes 1179656 | tf_op jit(solution)/shard_map/ppermute | solution.py:440

commit v6 on v5

--- a/solution.py
+++ b/solution.py
@@ -14,11 +14,13 @@
 TOK = 256
 HID = 256
 CAP = 3
+SIDE = 4
 DEPTH = 8
+INNER = 16
 PIECES = 5
 PIECE = D // PIECES
-SUB = 8
-WIDE = 1152
+PACKED = TOK // 4 * CAP
+SIDE_ROWS = PACKED // SIDE
 
 VMEM = pltpu.VMEM
 SMEM = pltpu.SMEM
@@ -139,7 +141,7 @@
             pltpu.SemaphoreType.DMA(()),
         ],
         compiler_params=params(16),
-        cost_estimate=pl.CostEstimate(flops=10**9, bytes_accessed=4 * 10**6, transcendentals=0),
+        cost_estimate=pl.CostEstimate(flops=1, bytes_accessed=1, transcendentals=0),
     )(placement, master)
 
 
@@ -200,21 +202,6 @@
     return jnp.sum(jnp.where(iota((8, TOK), 0) == expert, table, 0.0), axis=0, keepdims=True)
 
 
-def pack_rows(my_turn, wanted, valid):
-    row = iota((SLOTS * SUB, TOK), 0)
-    inside = (iota((SLOTS * SUB, TOK), 1) // 4) == row // SUB
-    here = jnp.broadcast_to(my_turn, (SLOTS * SUB, TOK)) == wanted(row % SUB).astype(F32)
-    return (inside & here & valid(row % SUB)).astype(F32).astype(BF)
-
-
-PLACES = (
-    (lambda s: s, lambda s: s < 3),
-    (lambda s: s - 3, lambda s: (s >= 3) & (s < 6)),
-    (lambda s: (s - 6) * 2, lambda s: s >= 6),
-    (lambda s: s * 0 + 1, lambda s: s == 6),
-)
-
-
 def expert_kernel(
     place_ref,
     hidden_hbm,
@@ -222,7 +209,10 @@
     gain_ref,
     gate_up_hbm,
     down_hbm,
-    out_ref,
+    out0_ref,
+    out1_ref,
+    out2_ref,
+    out3_ref,
     normed_ref,
     rows_ref,
     slot_ref,
@@ -240,11 +230,18 @@
             copy = pltpu.make_async_copy(hbm.at[part], ref.at[part], sems.at[m * PIECES + n])
             copy.start()
             copies.append(copy)
-    down_ref[D:, :] = jnp.zeros((64, HID), BF)
     invert(place_ref, slot_ref)
-    owner = (lax.axis_index("x") * 2 + lax.axis_index("yl")) * DEPTH + lax.axis_index("z")
+    side = lax.axis_index("x")
+    owner = side * INNER + lax.axis_index("yl") * DEPTH + lax.axis_index("z")
     mine = slot_ref[owner] // DEPTH
+
     my_turn = row_of(turns(choices(routes_ref)), mine)
+    packed = iota((PACKED, TOK), 0)
+    block = ((packed // SIDE_ROWS) ^ side) * INNER + (packed % SIDE_ROWS) // CAP
+    pack = (
+        ((iota((PACKED, TOK), 1) // 4) == block)
+        & (jnp.broadcast_to(my_turn, (PACKED, TOK)) == (packed % CAP).astype(F32))
+    ).astype(F32).astype(BF)
 
     total = jnp.zeros((1, TOK), F32)
     for n in range(PIECES):
@@ -271,45 +268,29 @@
     gate = projected[:, :HID]
     up = projected[:, HID:]
     activated = (gate * jax.nn.sigmoid(1.702 * gate) * (up + 1.0)).astype(BF)
-    first, second, third, fourth = (
-        nn(pack_rows(my_turn, *place), activated).astype(BF) for place in PLACES
-    )
-    near = jnp.concatenate([first, second, third], axis=1)
-    far = jnp.concatenate([first, second, fourth], axis=1)
+    activated = nn(pack, activated).astype(BF)
     for n in range(PIECES):
         copies[2 * PIECES + n].wait()
-
-    def terms(lhs, at, size, last):
-        parts = [down_ref[b : b + size, :] for b in (at, WIDE + at, last)]
-        return nt(lhs, jnp.concatenate(parts, axis=1))
-
-    end = 2 * WIDE
-    for at in range(0, 512, 256):
-        out_ref[:, at : at + 256] = terms(near, at, 256, end + at).astype(BF)
-    out_ref[:, 512:640] = jnp.where(
-        iota((SLOTS * SUB, 128), 1) < 64,
-        terms(near, 512, 128, end + 512),
-        terms(far, 512, 128, end - 64),
-    ).astype(BF)
-    for at in range(640, WIDE, 256):
-        out_ref[:, at : at + 256] = terms(far, at, 256, end + at - 576).astype(BF)
+    for at in range(0, D, 640):
+        size = min(640, D - at)
+        terms = nt(activated, down_ref[at : at + size, :]).astype(BF)
+        for d, out_ref in enumerate((out0_ref, out1_ref, out2_ref, out3_ref)):
+            out_ref[:, at : at + size] = terms[d * SIDE_ROWS : (d + 1) * SIDE_ROWS]
 
     own = (iota((8, TOK), 1) == iota((8, TOK), 0) + owner * 4).astype(F32).astype(BF)
     for at in range(0, D, 640):
         size = min(640, D - at)
-        rows_ref[:, at : at + size] = nt(own, hidden_ref[at : at + size, :])
+        rows_ref[:, at : at + size] = nt(own, hidden_ref[at : at + size, :])[:4]
 
 
 def expert_terms(placement, hidden, routes, gain, gate_up, down):
     whole = pl.BlockSpec(memory_space=VMEM)
+    out = jax.ShapeDtypeStruct((SIDE_ROWS, D), BF)
     return pl.pallas_call(
         expert_kernel,
         name="expert_terms",
-        out_shape=(
-            jax.ShapeDtypeStruct((SLOTS * SUB, WIDE), BF),
-            jax.ShapeDtypeStruct((D, TOK), BF),
-            jax.ShapeDtypeStruct((8, D), F32),
-        ),
+        out_shape=(out,) * 4
+        + (jax.ShapeDtypeStruct((D, TOK), BF), jax.ShapeDtypeStruct((4, D), F32)),
         in_specs=[
             pl.BlockSpec(memory_space=SMEM),
             pl.BlockSpec(memory_space=pl.ANY),
@@ -318,12 +299,12 @@
             pl.BlockSpec(memory_space=pl.ANY),
             pl.BlockSpec(memory_space=pl.ANY),
         ],
-        out_specs=(whole,) * 3,
+        out_specs=(whole,) * 6,
         scratch_shapes=[
             pltpu.SMEM((SLOTS,), jnp.int32),
             VMEM((D, TOK), BF),
             VMEM((D, 2 * HID), BF),
-            VMEM((D + 64, HID), BF),
+            VMEM((D, HID), BF),
             pltpu.SemaphoreType.DMA((3 * PIECES,)),
         ],
         compiler_params=params(32),
@@ -331,9 +312,10 @@
     )(placement, hidden, routes, gain, gate_up, down)
 
 
-def weigh_kernel(place_ref, routes_ref, router_ref, normed_ref, out_ref, slot_ref):
+def weigh_kernel(place_ref, routes_ref, router_ref, normed_ref, out_ref, slot_ref, held_ref):
     invert(place_ref, slot_ref)
-    owner = (lax.axis_index("x") * 2 + lax.axis_index("yl")) * DEPTH + lax.axis_index("z")
+    side = lax.axis_index("x")
+    inner = lax.axis_index("yl") * DEPTH + lax.axis_index("z")
 
     rep = lax.axis_index("yh") * 2 + lax.axis_index("c")
     logits = jnp.zeros((8, TOK), F32)
@@ -345,81 +327,65 @@
     weights = powered / jnp.sum(powered, axis=0, keepdims=True)
     turn = turns(chosen)
 
-    lanes = SLOTS * SUB
-    source = iota((8, lanes), 1) // SUB
-    sub = iota((8, lanes), 1) % SUB
-    expert = jnp.zeros((8, lanes), jnp.int32)
-    for o in range(SLOTS):
-        expert = jnp.where(source == o, slot_ref[o] // DEPTH, expert)
-    match = expert == iota((8, lanes), 0)
-    their_turn = jnp.zeros((8, lanes), F32)
-    their_weight = jnp.zeros((8, lanes), F32)
-    for i in range(4):
-        mine = iota((8, TOK), 1) == owner * 4 + i
-        token = iota((8, lanes), 0) == i
-        for table, kind in ((turn, 0), (weights, 1)):
-            column = jnp.sum(jnp.where(mine, table, 0.0), axis=1, keepdims=True)
-            row = jnp.sum(jnp.where(match, column, 0.0), axis=0, keepdims=True)
-            row = jnp.broadcast_to(row, (8, lanes))
-            if kind == 0:
-                their_turn = jnp.where(token, row, their_turn)
-            else:
-                their_weight = jnp.where(token, row, their_weight)
-    their_weight = jnp.where(iota((8, lanes), 0) < 4, their_weight, 0.0)
-    for n, (wanted, valid) in enumerate(PLACES):
-        here = valid(sub) & (their_turn == wanted(sub).astype(F32))
-        table = jnp.where(here, their_weight, 0.0)
-        upper = table.astype(BF).astype(F32)
-        both = jnp.concatenate([upper, table - upper], axis=0)
-        out_ref[16 * n : 16 * n + 16, :] = both.astype(BF)
+    packed = iota((SIDE_ROWS, TOK), 0)
+    inside = (iota((SIDE_ROWS, TOK), 1) // 4) == side * INNER + packed // CAP
+    parts = []
+    for d in range(SIDE):
+        expert = slot_ref[(side ^ d) * INNER + inner] // DEPTH
+        here = jnp.broadcast_to(row_of(turn, expert), (SIDE_ROWS, TOK)) == (packed % CAP).astype(F32)
+        weight = jnp.broadcast_to(row_of(weights, expert), (SIDE_ROWS, TOK))
+        parts.append(jnp.where(inside & here, weight, 0.0))
+    held_ref[...] = jnp.transpose(jnp.concatenate(parts, axis=0))
+    local = 4 * INNER
+    table = held_ref[pl.ds(pl.multiple_of(side * local, local), local), :]
+    upper = table.astype(BF)
+    out_ref[:local, :] = upper
+    out_ref[local:, :] = (table - upper.astype(F32)).astype(BF)
 
 
 def weigh(placement, routes, router, normed):
     return pl.pallas_call(
         weigh_kernel,
         name="weigh",
-        out_shape=jax.ShapeDtypeStruct((64, SLOTS * SUB), BF),
+        out_shape=jax.ShapeDtypeStruct((8 * INNER, PACKED), BF),
         in_specs=[pl.BlockSpec(memory_space=SMEM)] + [pl.BlockSpec(memory_space=VMEM)] * 3,
         out_specs=pl.BlockSpec(memory_space=VMEM),
-        scratch_shapes=[pltpu.SMEM((SLOTS,), jnp.int32)],
+        scratch_shapes=[pltpu.SMEM((SLOTS,), jnp.int32), VMEM((TOK, PACKED), F32)],
         compiler_params=params(16),
-        cost_estimate=pl.CostEstimate(flops=10**9, bytes_accessed=2 * 10**6, transcendentals=0),
+        cost_estimate=pl.CostEstimate(flops=1, bytes_accessed=1, transcendentals=0),
     )(placement, routes, router, normed)
 
 
-def finish_kernel(table_ref, got_ref, rows_ref, out_ref):
-    mixed = []
-    both = nn(table_ref[...], got_ref[...])
-    for n in range(4):
-        mixed.append(both[16 * n : 16 * n + 8] + both[16 * n + 8 : 16 * n + 16])
-    rest = mixed[2] + pltpu.roll(mixed[3], WIDE // 2, 1)
-    for at, part in ((0, mixed[0]), (WIDE, mixed[1]), (2 * WIDE, rest)):
-        size = min(WIDE, D - at)
-        out = rows_ref[:, at : at + size] + part[:, :size]
-        out_ref[:, at : at + size] = out[:4].astype(BF)
-
-
-def finish(table, got, rows):
+def merge_kernel(table_ref, got0_ref, got1_ref, got2_ref, got3_ref, out_ref):
+    local = 4 * INNER
+    for at in range(0, D, 640):
+        size = min(640, D - at)
+        got = jnp.concatenate(
+            [ref[:, at : at + size] for ref in (got0_ref, got1_ref, got2_ref, got3_ref)], axis=0
+        )
+        both = nn(table_ref[...], got)
+        part = (both[:local] + both[local:]).astype(BF)
+        for n in range(INNER):
+            out_ref[n, :, at : at + size] = part[4 * n : 4 * n + 4]
+
+
+def merge_side(table, got):
     return pl.pallas_call(
-        finish_kernel,
-        name="finish",
-        out_shape=jax.ShapeDtypeStruct((4, D), BF),
-        in_specs=[pl.BlockSpec(memory_space=VMEM)] * 3,
+        merge_kernel,
+        name="merge_side",
+        out_shape=jax.ShapeDtypeStruct((INNER, 4, D), BF),
+        in_specs=[pl.BlockSpec(memory_space=VMEM)] * 5,
         out_specs=pl.BlockSpec(memory_space=VMEM),
         compiler_params=params(16),
         cost_estimate=pl.CostEstimate(flops=10**8, bytes_accessed=10**6, transcendentals=0),
-    )(table, got, rows)
+    )(table, *got)
 
 
 def on_device(
     master, placement, resident_gate_up, resident_down, hidden, routes, norm_gain, router
 ):
-    chunks = encode(in_hbm(placement), in_hbm(jnp.transpose(master, (2, 0, 1))))
-    router_rows, chunks = lax.optimization_barrier((router.T, chunks))
-    chunks = lax.all_to_all(chunks, FSDP, split_axis=0, concat_axis=0, tiled=True)
-
     chosen = routes[0].T
-    terms, normed, rows = expert_terms(
+    *terms, normed, rows = expert_terms(
         placement,
         in_hbm(hidden[0].T),
         chosen,
@@ -427,20 +393,28 @@
         in_hbm(resident_gate_up[0]),
         in_hbm(resident_down[0].T),
     )
+    got = [terms[0]]
+    for d in range(1, SIDE):
+        got.append(lax.ppermute(terms[d], "x", [(x, x ^ d) for x in range(SIDE)]))
+
+    master, _ = lax.optimization_barrier((master, terms[0]))
+    chunks = encode(in_hbm(placement), in_hbm(jnp.transpose(master, (2, 0, 1))))
+    router_rows, _ = lax.optimization_barrier((router.T, chunks))
     routers = [router_rows]
     for d in range(1, 4):
         routers.append(lax.ppermute(router_rows, REP, [(r, r ^ d) for r in range(4)]))
+    chunks = lax.all_to_all(chunks, FSDP, split_axis=0, concat_axis=0, tiled=True)
     table = weigh(placement, chosen, jnp.stack(routers), normed)
-    chunks, terms, table = lax.optimization_barrier((chunks, terms, table))
-    terms = terms.reshape(SLOTS, SUB, WIDE)
-    terms = lax.all_to_all(terms, FSDP, split_axis=0, concat_axis=0, tiled=True)
+    terms = merge_side(table, got)
+    chunks, terms = lax.optimization_barrier((chunks, terms))
 
     across = lax.ppermute(chunks, "yh", ((0, 1), (1, 0)))
     core = lax.ppermute(chunks, "c", ((0, 1), (1, 0)))
     both = lax.ppermute(across, "c", ((0, 1), (1, 0)))
+    terms = lax.all_to_all(terms, ("yl", "z"), split_axis=0, concat_axis=0, tiled=True)
     refreshed = assemble(chunks, across, core, both).T
     terms, refreshed = lax.optimization_barrier((terms, refreshed))
-    decoded = finish(table, terms.reshape(SLOTS * SUB, WIDE), rows)
+    decoded = (rows + jnp.sum(terms.astype(F32), axis=0)).astype(BF)
     return (refreshed[None], decoded[None])
 
 

time: 75 us -> 69.7 us (0.929)
  waiting for transfers between devices: 30.7 us -> 20.8 us
  starting transfers between devices: 26.4 us -> 30 us
  local copies, waits for them, and re-layouts: 0.03 us -> 2.06 us
  Pallas kernels: 16.5 us -> 14.9 us
  other arithmetic: 0.01 us -> 0.79 us
    ppermute x1, waiting for transfers between devices: 15.6 us -> 2.89 us  [on_device(): across = lax.ppermute(chunks, 'yh', ((0, 1), (1, 0)))]
    ppermute x0 -> x3, waiting for transfers between devices: none -> 9.16 us  [on_device(): got.append(lax.ppermute(terms[d], 'x', [(x, x ^ d) for x in range(SIDE)]))]
    all_to_all x1, waiting for transfers between devices: 9.46 us -> 3.52 us  [on_device(): lax.all_to_all(terms, ('yl', 'z'), split_axis=0, concat_axis=0, tiled=True)]
    ppermute x0 -> x3, starting transfers between devices: none -> 4.79 us  [on_device(): got.append(lax.ppermute(terms[d], 'x', [(x, x ^ d) for x in range(SIDE)]))]
    all_to_all x1, waiting for transfers between devices: 3.98 us -> 0.01 us  [on_device(): lax.all_to_all(chunks, FSDP, split_axis=0, concat_axis=0, tiled=True)]
    ppermute x3, waiting for transfers between devices: 0.01 us -> 3.51 us  [on_device(): lax.ppermute(router_rows, REP, [(r, r ^ d) for r in range(4)])]
    pallas_call x2, Pallas kernels: 7.88 us -> 6.34 us  [the longest x1 5.19 us: expert_terms(): pl.pallas_call(expert_kernel, name='expert_terms', out_shape=(out,) * 4 +...]
    unnamed x8 -> x10, local copies, waits for them, and re-layouts: 0.02 us -> 1.35 us
  transfers between devices with their start and end apart: 8 -> 11, of which waited for: 4 -> 8; matrix products, arithmetic and copies ran while one was open for 0% -> 0% of each run, Pallas kernels for 14% -> 7%
where the time goes in v6:
time: 69.7 us; the launch traced here: 69.2 us
  starting transfers between devices  30 us (43%)
  waiting for transfers between devices  20.8 us (30%)
  Pallas kernels  14.9 us (21%)
  local copies, waits for them, and re-layouts  2.06 us (3%)
  other arithmetic  0.79 us (1%)
  between operations  0.73 us (1%)
    all_to_all x1, starting transfers between devices, on_device(): lax.all_to_all(chunks, FSDP, split_axis=0, concat_axis=0, tiled=True)  12.6 us
    ppermute x3, waiting for transfers between devices, on_device(): got.append(lax.ppermute(terms[d], 'x', [(x, x ^ d) for x in range(SIDE)]))  9.16 us
    all_to_all x1, starting transfers between devices, on_device(): lax.all_to_all(terms, ('yl', 'z'), split_axis=0, concat_axis=0, tiled=True)  6.69 us
    pallas_call x1, Pallas kernels, expert_terms(): pl.pallas_call(expert_kernel, name='expert_terms', out_shape=(out,) * 4 +...  5.19 us
    pallas_call x1, Pallas kernels, encode(): pl.pallas_call(encode_kernel, name='encode', out_shape=jax.ShapeDtypeStru...  5.1 us
    ppermute x3, starting transfers between devices, on_device(): got.append(lax.ppermute(terms[d], 'x', [(x, x ^ d) for x in range(SIDE)]))  4.79 us
    all_to_all x1, waiting for transfers between devices, on_device(): lax.all_to_all(terms, ('yl', 'z'), split_axis=0, concat_axis=0, tiled=True)  3.52 us
    ppermute x3, waiting for transfers between devices, on_device(): lax.ppermute(router_rows, REP, [(r, r ^ d) for r in range(4)])  3.51 us
  transfers between devices with their start and end apart: 11, of which 8 were waited for; matrix products, arithmetic and copies ran while one was open for 0% of the time, Pallas kernels for 7%

profile of v6, /device:TPU:32, one launch (start us, length us, event | category | flops | bytes accessed | tf_op | source)
XLA Modules:
  0.0 69.2 jit_solution(1526498505120295825)
XLA Ops:
  0.6 0.7 %broadcast_in_dim.9.gain_ref = bf16[1,2880]{1,0:T(2,128)(2,1)S(1)} reshape(bf16[2880]{0:T(1024)(128)(2,1)} %param.14) | data formatting | bytes 11520 | tf_op jit(solution)/shard_map/broadcast_in_dim | solution.py:392
  1.3 0.0 copy-start
  1.3 0.7 copy-done
  2.0 0.0 copy-start.2
  2.0 0.7 copy-done.2
  2.7 5.2 %expert_terms.1 = (bf16[48,2880]{1,0:T(8,128)(2,1)S(1)}, bf16[48,2880]{1,0:T(8,128)(2,1)S(1)}, bf16[48,2880]{1,0:T(8,128)(2,1)S(1)}, bf16[48,2880]{1,0:T(8,128)(...) custom-call(s32[64]{0:T(128)S(1)} %copy-done.2, bf16[2880,256]{1,0:T(8,128)(2,1)} %bitcast.31, ...), custom_call_target="tpu_custom_call" | custom-call | flops 3000000000 | bytes 8000000 | tf_op jit(solution)/shard_map/expert_terms/pallas_call | solution.py:289
  7.9 0.0 copy-start.4
  7.9 0.0 copy-start.1
  7.9 0.0 copy-start.3
  7.9 5.1 %encode.1 = bf16[64,24,128]{2,1,0:T(8,128)(2,1)} custom-call(s32[64]{0:T(128)} %place_ref.3, f32[45,64,64]{2,1,0:T(8,128)} %bitcast.22), custom_call_target="tpu_custom_call" | custom-call | flops 1 | bytes 1 | tf_op jit(solution)/shard_map/encode/pallas_call | solution.py:129
  13.0 12.6 %all-to-all-start = ((bf16[64,24,128]{2,1,0:T(8,128)(2,1)}), bf16[64,24,128]{2,1,0:T(8,128)(2,1)S(1)}, u32[]{:S(2)}, u32[]{:S(2)}) async-start(bf16[64,24,128]{2,1,0:T(8,128)(2,1)} %encode.1), calls=%async_computation | async-start | bytes 786432 | tf_op jit(solution)/shard_map/all_to_all | solution.py:406
  25.6 1.6 %collective-permute-start.3 = (bf16[48,2880]{1,0:T(8,128)(2,1)S(1)}, bf16[48,2880]{1,0:T(8,128)(2,1)S(1)}, u32[]{:S(2)}, u32[]{:S(2)}) collective-permute-start(bf16[48,2880]{1,0:T(8,128)(2,1)S(1)} %get-tuple-element.18), channel_id=1, source_target_pairs={{0,64},{64,0},{128,192},{192,128},{1,65},{65,1},{129,193},{193,129... | collective-permute-start | bytes 829448 | tf_op jit(solution)/shard_map/ppermute | solution.py:398
  27.2 2.9 %collective-permute-start.4 = (bf16[48,2880]{1,0:T(8,128)(2,1)S(1)}, bf16[48,2880]{1,0:T(8,128)(2,1)S(1)}, u32[]{:S(2)}, u32[]{:S(2)}) collective-permute-start(bf16[48,2880]{1,0:T(8,128)(2,1)S(1)} %get-tuple-element.19), channel_id=1, source_target_pairs={{0,128},{64,192},{128,0},{192,64},{1,129},{65,193},{129,1},{193,65... | collective-permute-start | bytes 829448 | tf_op jit(solution)/shard_map/ppermute | solution.py:398
  30.1 0.3 collective-permute-start.5
  30.4 0.0 copy-done.4
  30.4 0.9 %collective-permute-start.2 = (bf16[8,720]{1,0:T(8,128)(2,1)S(1)}, bf16[8,720]{1,0:T(8,128)(2,1)S(1)}, u32[]{:S(2)}, u32[]{:S(2)}) collective-permute-start(bf16[8,720]{1,0:T(8,128)(2,1)S(1)} %bitcast.23), channel_id=1, source_target_pairs={{0,3},{1,2},{2,1},{3,0},{4,7},{5,6},{6,5},{7,4},{8,11},{9,10},{10,... | collective-permute-start | bytes 34568 | tf_op jit(solution)/shard_map/ppermute | solution.py:405
  31.4 2.0 %collective-permute-start.1 = (bf16[8,720]{1,0:T(8,128)(2,1)S(1)}, bf16[8,720]{1,0:T(8,128)(2,1)S(1)}, u32[]{:S(2)}, u32[]{:S(2)}) collective-permute-start(bf16[8,720]{1,0:T(8,128)(2,1)S(1)} %bitcast.24), channel_id=1, source_target_pairs={{0,2},{1,3},{2,0},{3,1},{4,6},{5,7},{6,4},{7,5},{8,10},{9,11},{10,... | collective-permute-start | bytes 34568 | tf_op jit(solution)/shard_map/ppermute | solution.py:405
  33.4 1.8 %collective-permute-done.2 = bf16[8,720]{1,0:T(8,128)(2,1)S(1)} collective-permute-done((bf16[8,720]{1,0:T(8,128)(2,1)S(1)}, bf16[8,720]{1,0:T(8,128)(2,1)S(1)}, u32[]{:S(2)}, u32[]{:S(2)}) %collective-permute-start.2) | collective-permute-done | bytes 11552 | tf_op jit(solution)/shard_map/ppermute | solution.py:405
  35.2 0.1 collective-permute-start
  35.2 1.7 %collective-permute-done.1 = bf16[8,720]{1,0:T(8,128)(2,1)S(1)} collective-permute-done((bf16[8,720]{1,0:T(8,128)(2,1)S(1)}, bf16[8,720]{1,0:T(8,128)(2,1)S(1)}, u32[]{:S(2)}, u32[]{:S(2)}) %collective-permute-start.1) | collective-permute-done | bytes 11552 | tf_op jit(solution)/shard_map/ppermute | solution.py:405
  36.9 0.0 collective-permute-done
  37.0 0.0 copy-done.1
  37.0 0.0 copy-done.3
  37.0 1.2 %weigh.1.table_ref = bf16[128,192]{1,0:T(8,128)(2,1)S(1)} custom-call(s32[64]{0:T(128)S(1)} %copy-done.3, s32[4,256]{1,0:T(4,128)S(1)} %bitcast.21, bf16[4,8,720]{2,1,0:T(8,128)(2,1)S(1)} %pad_maximum_fusion.router_ref, bf16[2880,256]{1,0:T(8,128)(2,1)S(1)} %get-tuple-element.17.normed_ref), custom_call_target="tpu_custom_call" | custom-call | flops 1 | bytes 1 | tf_op jit(solution)/shard_map/weigh/pallas_call | solution.py:347
  38.2 0.4 collective-permute-done.3.got1_ref
  38.5 7.4 %collective-permute-done.4.got2_ref = bf16[48,2880]{1,0:T(8,128)(2,1)S(1)} collective-permute-done((bf16[48,2880]{1,0:T(8,128)(2,1)S(1)}, bf16[48,2880]{1,0:T(8,128)(2,1)S(1)}, u32[]{:S(2)}, u32[]{:S(2)}) %collective-permute-start.4) | collective-permute-done | bytes 276512 | tf_op jit(solution)/shard_map/ppermute | solution.py:398
  45.9 1.4 %collective-permute-done.5.got3_ref = bf16[48,2880]{1,0:T(8,128)(2,1)S(1)} collective-permute-done((bf16[48,2880]{1,0:T(8,128)(2,1)S(1)}, bf16[48,2880]{1,0:T(8,128)(2,1)S(1)}, u32[]{:S(2)}, u32[]{:S(2)}) %collective-permute-start.5) | collective-permute-done | bytes 276512 | tf_op jit(solution)/shard_map/ppermute | solution.py:398
  47.3 1.1 %merge_side.1 = bf16[16,4,2880]{2,1,0:T(4,128)(2,1)} custom-call(bf16[128,192]{1,0:T(8,128)(2,1)S(1)} %weigh.1.table_ref, bf16[48,2880]{1,0:T(8,128)(2,1)S(1)} %get-tuple-element.14.got0_ref, bf16[48,2880]{1,0:T(8,128)(2,1)S(1)} %collective-permute-done.3.got1_ref, bf16[48,2880]{1,0:T(8,128)(2,1)S(1)} %collective-permute-done.4.got2_ref, ...), custom_call_target="tpu_custom_call" | custom-call | flops 100000000 | bytes 1000000 | tf_op jit(solution)/shard_map/merge_side/pallas_call | solution.py:373
  48.5 0.0 all-to-all-done.own_ref
  48.5 2.9 %collective-permute-start.6 = (bf16[64,24,128]{2,1,0:T(8,128)(2,1)S(1)}, bf16[64,24,128]{2,1,0:T(8,128)(2,1)S(1)}, u32[]{:S(2)}, u32[]{:S(2)}) collective-permute-start(bf16[64,24,128]{2,1,0:T(8,128)(2,1)S(1)} %all-to-all-done.own_ref), channel_id=1, source_target_pairs={{0,2},{2,0},{1,3},{3,1},{4,6},{6,4},{5,7},{7,5},{8,10},{10,8},{9,1... | collective-permute-start | bytes 1179656 | tf_op jit(solution)/shard_map/ppermute | solution.py:411
  51.4 6.7 %all-to-all-start.1 = ((bf16[16,4,2880]{2,1,0:T(4,128)(2,1)}), bf16[16,4,2880]{2,1,0:T(4,128)(2,1)S(1)}, u32[]{:S(2)}, u32[]{:S(2)}) async-start(bf16[16,4,2880]{2,1,0:T(4,128)(2,1)} %merge_side.1), calls=%async_computation.1 | async-start | bytes 753664 | tf_op jit(solution)/shard_map/all_to_all | solution.py:414
  58.1 0.0 collective-permute-start.7
  58.1 2.9 %collective-permute-done.6.across_ref = bf16[64,24,128]{2,1,0:T(8,128)(2,1)S(1)} collective-permute-done((bf16[64,24,128]{2,1,0:T(8,128)(2,1)S(1)}, bf16[64,24,128]{2,1,0:T(8,128)(2,1)S(1)}, u32[]{:S(2)}, u32[]{:S(2)}) %collective-permute-start.6) | collective-permute-done | bytes 393248 | tf_op jit(solution)/shard_map/ppermute | solution.py:411
  61.0 0.0 collective-permute-start.8
  61.0 0.0 collective-permute-done.7.core_ref
  61.0 1.7 %collective-permute-done.8.both_ref = bf16[64,24,128]{2,1,0:T(8,128)(2,1)S(1)} collective-permute-done((bf16[64,24,128]{2,1,0:T(8,128)(2,1)S(1)}, bf16[64,24,128]{2,1,0:T(8,128)(2,1)S(1)}, u32[]{:S(2)}, u32[]{:S(2)}) %collective-permute-start.8) | collective-permute-done | bytes 393248 | tf_op jit(solution)/shard_map/ppermute | solution.py:413
  62.7 2.2 %assemble.1 = bf16[2880,256]{1,0:T(8,128)(2,1)} custom-call(bf16[64,24,128]{2,1,0:T(8,128)(2,1)S(1)} %all-to-all-done.own_ref, bf16[64,24,128]{2,1,0:T(8,128)(2,1)S(1)} %collective-permute-done.6.across_ref, bf16[64,24,128]{2,1,0:T(8,128)(2,1)S(1)} %collective-permute-done.7.core_ref, bf16[64,24,128]{2,1,0:T(8,128)(2,1)S(1)} %collective-permute-done.8.both_ref), custom_call_target="tpu_custom_call" | custom-call | flops 1000000000 | bytes 4000000 | tf_op jit(solution)/shard_map/assemble/pallas_call | solution.py:172
  64.9 3.5 %all-to-all-done.1 = bf16[16,4,2880]{2,1,0:T(4,128)(2,1)S(1)} async-done(((bf16[16,4,2880]{2,1,0:T(4,128)(2,1)}), bf16[16,4,2880]{2,1,0:T(4,128)(2,1)S(1)}, u32[]{:S(2)}, u32[]{:S(2)}) %all-to-all-start.1) | async-done | bytes 368672 | tf_op jit(solution)/shard_map/all_to_all | solution.py:414
  68.4 0.2 convert_reduce_fusion
  68.6 0.6 fusion
  (1 shorter events, 0.0 us)
Async XLA Ops:
  1.3 0.7 copy-start
  2.0 0.7 copy-start.2
  7.9 22.6 %copy-start.4 = (bf16[720,8]{0,1:T(8,128)(2,1)S(1)}, bf16[720,8]{0,1:T(8,128)(2,1)}, u32[]{:S(2)}) copy-start(bf16[720,8]{0,1:T(8,128)(2,1)} %param.15) | copy-start | bytes 34564
  7.9 29.1 %copy-start.1 = (s32[1,256,4]{1,2,0:T(4,128)S(1)}, s32[1,256,4]{1,2,0:T(4,128)}, u32[]{:S(2)}) copy-start(s32[1,256,4]{1,2,0:T(4,128)} %param.13) | copy-start | bytes 12292
  7.9 29.1 %copy-start.3 = (s32[64]{0:T(128)S(1)}, s32[64]{0:T(128)}, u32[]{:S(2)}) copy-start(s32[64]{0:T(128)} %place_ref.3) | copy-start | bytes 772
  13.0 35.5 %all-to-all-start = ((bf16[64,24,128]{2,1,0:T(8,128)(2,1)}), bf16[64,24,128]{2,1,0:T(8,128)(2,1)S(1)}, u32[]{:S(2)}, u32[]{:S(2)}) async-start(bf16[64,24,128]{2,1,0:T(8,128)(2,1)} %encode.1), calls=%async_computation | async-start | bytes 786432 | tf_op jit(solution)/shard_map/all_to_all | solution.py:406
  25.6 12.9 %collective-permute-start.3 = (bf16[48,2880]{1,0:T(8,128)(2,1)S(1)}, bf16[48,2880]{1,0:T(8,128)(2,1)S(1)}, u32[]{:S(2)}, u32[]{:S(2)}) collective-permute-start(bf16[48,2880]{1,0:T(8,128)(2,1)S(1)} %get-tuple-element.18), channel_id=1, source_target_pairs={{0,64},{64,0},{128,192},{192,128},{1,65},{65,1},{129,193},{193,129... | collective-permute-start | bytes 829448 | tf_op jit(solution)/shard_map/ppermute | solution.py:398
  27.2 18.7 %collective-permute-start.4 = (bf16[48,2880]{1,0:T(8,128)(2,1)S(1)}, bf16[48,2880]{1,0:T(8,128)(2,1)S(1)}, u32[]{:S(2)}, u32[]{:S(2)}) collective-permute-start(bf16[48,2880]{1,0:T(8,128)(2,1)S(1)} %get-tuple-element.19), channel_id=1, source_target_pairs={{0,128},{64,192},{128,0},{192,64},{1,129},{65,193},{129,1},{193,65... | collective-permute-start | bytes 829448 | tf_op jit(solution)/shard_map/ppermute | solution.py:398
  30.1 17.2 %collective-permute-start.5 = (bf16[48,2880]{1,0:T(8,128)(2,1)S(1)}, bf16[48,2880]{1,0:T(8,128)(2,1)S(1)}, u32[]{:S(2)}, u32[]{:S(2)}) collective-permute-start(bf16[48,2880]{1,0:T(8,128)(2,1)S(1)} %get-tuple-element.20), channel_id=1, source_target_pairs={{0,192},{64,128},{128,64},{192,0},{1,193},{65,129},{129,65},{193,1... | collective-permute-start | bytes 829448 | tf_op jit(solution)/shard_map/ppermute | solution.py:398
  30.4 4.7 %collective-permute-start.2 = (bf16[8,720]{1,0:T(8,128)(2,1)S(1)}, bf16[8,720]{1,0:T(8,128)(2,1)S(1)}, u32[]{:S(2)}, u32[]{:S(2)}) collective-permute-start(bf16[8,720]{1,0:T(8,128)(2,1)S(1)} %bitcast.23), channel_id=1, source_target_pairs={{0,3},{1,2},{2,1},{3,0},{4,7},{5,6},{6,5},{7,4},{8,11},{9,10},{10,... | collective-permute-start | bytes 34568 | tf_op jit(solution)/shard_map/ppermute | solution.py:405
  31.4 5.6 %collective-permute-start.1 = (bf16[8,720]{1,0:T(8,128)(2,1)S(1)}, bf16[8,720]{1,0:T(8,128)(2,1)S(1)}, u32[]{:S(2)}, u32[]{:S(2)}) collective-permute-start(bf16[8,720]{1,0:T(8,128)(2,1)S(1)} %bitcast.24), channel_id=1, source_target_pairs={{0,2},{1,3},{2,0},{3,1},{4,6},{5,7},{6,4},{7,5},{8,10},{9,11},{10,... | collective-permute-start | bytes 34568 | tf_op jit(solution)/shard_map/ppermute | solution.py:405
  35.2 1.8 %collective-permute-start = (bf16[8,720]{1,0:T(8,128)(2,1)S(1)}, bf16[8,720]{1,0:T(8,128)(2,1)S(1)}, u32[]{:S(2)}, u32[]{:S(2)}) collective-permute-start(bf16[8,720]{1,0:T(8,128)(2,1)S(1)} %bitcast.25), channel_id=1, source_target_pairs={{0,1},{1,0},{2,3},{3,2},{4,5},{5,4},{6,7},{7,6},{8,9},{9,8},{10,11... | collective-permute-start | bytes 34568 | tf_op jit(solution)/shard_map/ppermute | solution.py:405
  48.5 12.5 %collective-permute-start.6 = (bf16[64,24,128]{2,1,0:T(8,128)(2,1)S(1)}, bf16[64,24,128]{2,1,0:T(8,128)(2,1)S(1)}, u32[]{:S(2)}, u32[]{:S(2)}) collective-permute-start(bf16[64,24,128]{2,1,0:T(8,128)(2,1)S(1)} %all-to-all-done.own_ref), channel_id=1, source_target_pairs={{0,2},{2,0},{1,3},{3,1},{4,6},{6,4},{5,7},{7,5},{8,10},{10,8},{9,1... | collective-permute-start | bytes 1179656 | tf_op jit(solution)/shard_map/ppermute | solution.py:411
  51.4 17.1 %all-to-all-start.1 = ((bf16[16,4,2880]{2,1,0:T(4,128)(2,1)}), bf16[16,4,2880]{2,1,0:T(4,128)(2,1)S(1)}, u32[]{:S(2)}, u32[]{:S(2)}) async-start(bf16[16,4,2880]{2,1,0:T(4,128)(2,1)} %merge_side.1), calls=%async_computation.1 | async-start | bytes 753664 | tf_op jit(solution)/shard_map/all_to_all | solution.py:414
  58.1 2.9 %collective-permute-start.7 = (bf16[64,24,128]{2,1,0:T(8,128)(2,1)S(1)}, bf16[64,24,128]{2,1,0:T(8,128)(2,1)S(1)}, u32[]{:S(2)}, u32[]{:S(2)}) collective-permute-start(bf16[64,24,128]{2,1,0:T(8,128)(2,1)S(1)} %all-to-all-done.own_ref), channel_id=1, source_target_pairs={{0,1},{1,0},{2,3},{3,2},{4,5},{5,4},{6,7},{7,6},{8,9},{9,8},{10,11... | collective-permute-start | bytes 1179656 | tf_op jit(solution)/shard_map/ppermute | solution.py:412
  61.0 1.7 %collective-permute-start.8 = (bf16[64,24,128]{2,1,0:T(8,128)(2,1)S(1)}, bf16[64,24,128]{2,1,0:T(8,128)(2,1)S(1)}, u32[]{:S(2)}, u32[]{:S(2)}) collective-permute-start(bf16[64,24,128]{2,1,0:T(8,128)(2,1)S(1)} %collective-permute-done.6.across_ref), channel_id=1, source_target_pairs={{0,1},{1,0},{2,3},{3,2},{4,5},{5,4},{6,7},{7,6},{8,9},{9,8},{10,11... | collective-permute-start | bytes 1179656 | tf_op jit(solution)/shard_map/ppermute | solution.py:413

commit v7 on v6

--- a/solution.py
+++ b/solution.py
@@ -204,7 +204,7 @@
 
 def expert_kernel(
     place_ref,
-    hidden_hbm,
+    hidden_ref,
     routes_ref,
     gain_ref,
     gate_up_hbm,
@@ -216,15 +216,12 @@
     normed_ref,
     rows_ref,
     slot_ref,
-    hidden_ref,
     gate_up_ref,
     down_ref,
     sems,
 ):
     copies = []
-    for m, (hbm, ref) in enumerate(
-        ((hidden_hbm, hidden_ref), (gate_up_hbm, gate_up_ref), (down_hbm, down_ref))
-    ):
+    for m, (hbm, ref) in enumerate(((gate_up_hbm, gate_up_ref), (down_hbm, down_ref))):
         for n in range(PIECES):
             part = pl.ds(n * PIECE, PIECE)
             copy = pltpu.make_async_copy(hbm.at[part], ref.at[part], sems.at[m * PIECES + n])
@@ -245,7 +242,6 @@
 
     total = jnp.zeros((1, TOK), F32)
     for n in range(PIECES):
-        copies[n].wait()
         part = hidden_ref[n * PIECE : (n + 1) * PIECE, :].astype(F32)
         total = total + jnp.sum(part * part, axis=0, keepdims=True)
     factor = lax.rsqrt(total * (1.0 / D) + 1e-05)
@@ -262,7 +258,7 @@
 
     projected = jnp.zeros((TOK, 2 * HID), F32)
     for n in range(PIECES):
-        copies[PIECES + n].wait()
+        copies[n].wait()
         part = slice(n * PIECE, (n + 1) * PIECE)
         projected = projected + tn(normed_ref[part, :], gate_up_ref[part, :])
     gate = projected[:, :HID]
@@ -270,7 +266,7 @@
     activated = (gate * jax.nn.sigmoid(1.702 * gate) * (up + 1.0)).astype(BF)
     activated = nn(pack, activated).astype(BF)
     for n in range(PIECES):
-        copies[2 * PIECES + n].wait()
+        copies[PIECES + n].wait()
     for at in range(0, D, 640):
         size = min(640, D - at)
         terms = nt(activated, down_ref[at : at + size, :]).astype(BF)
@@ -293,7 +289,7 @@
         + (jax.ShapeDtypeStruct((D, TOK), BF), jax.ShapeDtypeStruct((4, D), F32)),
         in_specs=[
             pl.BlockSpec(memory_space=SMEM),
-            pl.BlockSpec(memory_space=pl.ANY),
+            whole,
             whole,
             whole,
             pl.BlockSpec(memory_space=pl.ANY),
@@ -302,10 +298,9 @@
         out_specs=(whole,) * 6,
         scratch_shapes=[
             pltpu.SMEM((SLOTS,), jnp.int32),
-            VMEM((D, TOK), BF),
             VMEM((D, 2 * HID), BF),
             VMEM((D, HID), BF),
-            pltpu.SemaphoreType.DMA((3 * PIECES,)),
+            pltpu.SemaphoreType.DMA((2 * PIECES,)),
         ],
         compiler_params=params(32),
         cost_estimate=pl.CostEstimate(flops=3 * 10**9, bytes_accessed=8 * 10**6, transcendentals=0),
@@ -377,33 +372,33 @@
         in_specs=[pl.BlockSpec(memory_space=VMEM)] * 5,
         out_specs=pl.BlockSpec(memory_space=VMEM),
         compiler_params=params(16),
-        cost_estimate=pl.CostEstimate(flops=10**8, bytes_accessed=10**6, transcendentals=0),
+        cost_estimate=pl.CostEstimate(flops=4 * 10**9, bytes_accessed=1, transcendentals=0),
     )(table, *got)
 
 
 def on_device(
     master, placement, resident_gate_up, resident_down, hidden, routes, norm_gain, router
 ):
+    chunks = encode(in_hbm(placement), in_hbm(jnp.transpose(master, (2, 0, 1))))
     chosen = routes[0].T
+    norm_gain, chunks = lax.optimization_barrier((norm_gain, chunks))
     *terms, normed, rows = expert_terms(
         placement,
-        in_hbm(hidden[0].T),
+        hidden[0].T,
         chosen,
         norm_gain[None],
         in_hbm(resident_gate_up[0]),
         in_hbm(resident_down[0].T),
     )
     got = [terms[0]]
+    chunks, *terms = lax.optimization_barrier((chunks, *terms))
     for d in range(1, SIDE):
         got.append(lax.ppermute(terms[d], "x", [(x, x ^ d) for x in range(SIDE)]))
-
-    master, _ = lax.optimization_barrier((master, terms[0]))
-    chunks = encode(in_hbm(placement), in_hbm(jnp.transpose(master, (2, 0, 1))))
-    router_rows, _ = lax.optimization_barrier((router.T, chunks))
+    chunks = lax.all_to_all(chunks, FSDP, split_axis=0, concat_axis=0, tiled=True)
+    router_rows, *_ = lax.optimization_barrier((router.T, *got[1:]))
     routers = [router_rows]
     for d in range(1, 4):
         routers.append(lax.ppermute(router_rows, REP, [(r, r ^ d) for r in range(4)]))
-    chunks = lax.all_to_all(chunks, FSDP, split_axis=0, concat_axis=0, tiled=True)
     table = weigh(placement, chosen, jnp.stack(routers), normed)
     terms = merge_side(table, got)
     chunks, terms = lax.optimization_barrier((chunks, terms))

time: 69.7 us -> 66.3 us (0.951)
  waiting for transfers between devices: 20.8 us -> 18.9 us
  local copies, waits for them, and re-layouts: 2.06 us -> 0.76 us
    ppermute x3, waiting for transfers between devices: 9.16 us -> 2.67 us  [on_device(): got.append(lax.ppermute(terms[d], 'x', [(x, x ^ d) for x in range(SIDE)]))]
    all_to_all x1, waiting for transfers between devices: 0.01 us -> 3.66 us  [on_device(): lax.all_to_all(chunks, FSDP, split_axis=0, concat_axis=0, tiled=True)]
    all_to_all x1, waiting for transfers between devices: 3.52 us -> 6.4 us  [on_device(): lax.all_to_all(terms, ('yl', 'z'), split_axis=0, concat_axis=0, tiled=True)]
    ppermute x1, waiting for transfers between devices: 2.89 us -> 1.79 us  [on_device(): across = lax.ppermute(chunks, 'yh', ((0, 1), (1, 0)))]
    ppermute x3, waiting for transfers between devices: 3.51 us -> 2.66 us  [on_device(): lax.ppermute(router_rows, REP, [(r, r ^ d) for r in range(4)])]
  transfers between devices with their start and end apart: 11 -> 11, of which waited for: 8 -> 7; matrix products, arithmetic and copies ran while one was open for 0% -> 0% of each run, Pallas kernels for 7% -> 7%
where the time goes in v7:
time: 66.3 us; the launch traced here: 65.7 us
  starting transfers between devices  29.6 us (45%)
  waiting for transfers between devices  18.9 us (29%)
  Pallas kernels  14.8 us (22%)
  between operations  0.8 us (1%)
  other arithmetic  0.79 us (1%)
  local copies, waits for them, and re-layouts  0.76 us (1%)
    all_to_all x1, starting transfers between devices, on_device(): lax.all_to_all(chunks, FSDP, split_axis=0, concat_axis=0, tiled=True)  12.3 us
    all_to_all x1, waiting for transfers between devices, on_device(): lax.all_to_all(terms, ('yl', 'z'), split_axis=0, concat_axis=0, tiled=True)  6.4 us
    all_to_all x1, starting transfers between devices, on_device(): lax.all_to_all(terms, ('yl', 'z'), split_axis=0, concat_axis=0, tiled=True)  6.31 us
    pallas_call x1, Pallas kernels, encode(): pl.pallas_call(encode_kernel, name='encode', out_shape=jax.ShapeDtypeStru...  5.21 us
    pallas_call x1, Pallas kernels, expert_terms(): pl.pallas_call(expert_kernel, name='expert_terms', out_shape=(out,) * 4 +...  4.98 us
    ppermute x3, starting transfers between devices, on_device(): got.append(lax.ppermute(terms[d], 'x', [(x, x ^ d) for x in range(SIDE)]))  4.7 us
    all_to_all x1, waiting for transfers between devices, on_device(): lax.all_to_all(chunks, FSDP, split_axis=0, concat_axis=0, tiled=True)  3.66 us
    ppermute x3, starting transfers between devices, on_device(): lax.ppermute(router_rows, REP, [(r, r ^ d) for r in range(4)])  3.4 us
  transfers between devices with their start and end apart: 11, of which 7 were waited for; matrix products, arithmetic and copies ran while one was open for 0% of the time, Pallas kernels for 7%

profile of v7, /device:TPU:32, one launch (start us, length us, event | category | flops | bytes accessed | tf_op | source)
XLA Modules:
  0.0 65.7 jit_solution(9111878066980739276)
XLA Ops:
  0.6 0.0 copy-start.1
  0.6 0.0 copy-start.6
  0.7 0.0 copy-start
  0.7 0.0 copy-start.2
  0.7 5.2 %encode.1 = bf16[64,24,128]{2,1,0:T(8,128)(2,1)} custom-call(s32[64]{0:T(128)} %place_ref.3, f32[45,64,64]{2,1,0:T(8,128)} %bitcast.23), custom_call_target="tpu_custom_call" | custom-call | flops 1 | bytes 1 | tf_op jit(solution)/shard_map/encode/pallas_call | solution.py:129
  5.9 0.0 copy-done.6
  5.9 0.0 copy-done.1
  5.9 0.0 copy-done
  5.9 0.0 copy-done.2
  5.9 0.0 copy-start.5
  6.0 5.0 %expert_terms.1 = (bf16[48,2880]{1,0:T(8,128)(2,1)S(1)}, bf16[48,2880]{1,0:T(8,128)(2,1)}, bf16[48,2880]{1,0:T(8,128)(2,1)S(1)}, bf16[48,2880]{1,0:T(8,128)(2,1)...) custom-call(s32[64]{0:T(128)S(1)} %copy-done.1, bf16[2880,256]{1,0:T(8,128)(2,1)S(1)} %bitcast.22, ...), custom_call_target="tpu_custom_call" | custom-call | flops 3000000000 | bytes 8000000 | tf_op jit(solution)/shard_map/expert_terms/pallas_call | solution.py:285
  10.9 0.0 copy-start.3
  10.9 0.7 %copy-done.3 = bf16[48,2880]{1,0:T(8,128)(2,1)} copy-done((bf16[48,2880]{1,0:T(8,128)(2,1)}, bf16[48,2880]{1,0:T(8,128)(2,1)S(1)}, u32[]{:S(2)}) %copy-start.3) | copy-done | bytes 276504
  11.7 1.5 %collective-permute-start = (bf16[48,2880]{1,0:T(8,128)(2,1)}, bf16[48,2880]{1,0:T(8,128)(2,1)S(1)}, u32[]{:S(2)}, u32[]{:S(2)}) collective-permute-start(bf16[48,2880]{1,0:T(8,128)(2,1)} %get-tuple-element.26), channel_id=1, source_target_pairs={{0,64},{64,0},{128,192},{192,128},{1,65},{65,1},{129,193},{193,129... | collective-permute-start | bytes 829448 | tf_op jit(solution)/shard_map/ppermute | solution.py:396
  13.2 2.7 %collective-permute-start.1 = (bf16[48,2880]{1,0:T(8,128)(2,1)S(1)}, bf16[48,2880]{1,0:T(8,128)(2,1)S(1)}, u32[]{:S(2)}, u32[]{:S(2)}) collective-permute-start(bf16[48,2880]{1,0:T(8,128)(2,1)S(1)} %get-tuple-element.27), channel_id=1, source_target_pairs={{0,128},{64,192},{128,0},{192,64},{1,129},{65,193},{129,1},{193,65... | collective-permute-start | bytes 829448 | tf_op jit(solution)/shard_map/ppermute | solution.py:396
  15.9 0.5 collective-permute-start.2
  16.4 12.3 %all-to-all-start = ((bf16[64,24,128]{2,1,0:T(8,128)(2,1)}), bf16[64,24,128]{2,1,0:T(8,128)(2,1)S(1)}, u32[]{:S(2)}, u32[]{:S(2)}) async-start(bf16[64,24,128]{2,1,0:T(8,128)(2,1)} %encode.1), calls=%async_computation | async-start | bytes 786432 | tf_op jit(solution)/shard_map/all_to_all | solution.py:397
  28.7 0.0 copy-start.4
  28.7 0.0 collective-permute-done.got1_ref
  28.7 0.0 collective-permute-done.1.got2_ref
  28.7 2.7 %collective-permute-done.2.got3_ref = bf16[48,2880]{1,0:T(8,128)(2,1)S(1)} collective-permute-done((bf16[48,2880]{1,0:T(8,128)(2,1)S(1)}, bf16[48,2880]{1,0:T(8,128)(2,1)S(1)}, u32[]{:S(2)}, u32[]{:S(2)}) %collective-permute-start.2) | collective-permute-done | bytes 276512 | tf_op jit(solution)/shard_map/ppermute | solution.py:396
  31.4 0.0 copy-done.5
  31.4 0.8 %collective-permute-start.5 = (bf16[8,720]{1,0:T(8,128)(2,1)S(1)}, bf16[8,720]{1,0:T(8,128)(2,1)S(1)}, u32[]{:S(2)}, u32[]{:S(2)}) collective-permute-start(bf16[8,720]{1,0:T(8,128)(2,1)S(1)} %bitcast.24), channel_id=1, source_target_pairs={{0,3},{1,2},{2,1},{3,0},{4,7},{5,6},{6,5},{7,4},{8,11},{9,10},{10,... | collective-permute-start | bytes 34568 | tf_op jit(solution)/shard_map/ppermute | solution.py:401
  32.2 2.5 %collective-permute-start.4 = (bf16[8,720]{1,0:T(8,128)(2,1)S(1)}, bf16[8,720]{1,0:T(8,128)(2,1)S(1)}, u32[]{:S(2)}, u32[]{:S(2)}) collective-permute-start(bf16[8,720]{1,0:T(8,128)(2,1)S(1)} %bitcast.25), channel_id=1, source_target_pairs={{0,2},{1,3},{2,0},{3,1},{4,6},{5,7},{6,4},{7,5},{8,10},{9,11},{10,... | collective-permute-start | bytes 34568 | tf_op jit(solution)/shard_map/ppermute | solution.py:401
  34.7 0.1 collective-permute-start.3
  34.8 1.2 %collective-permute-done.5 = bf16[8,720]{1,0:T(8,128)(2,1)S(1)} collective-permute-done((bf16[8,720]{1,0:T(8,128)(2,1)S(1)}, bf16[8,720]{1,0:T(8,128)(2,1)S(1)}, u32[]{:S(2)}, u32[]{:S(2)}) %collective-permute-start.5) | collective-permute-done | bytes 11552 | tf_op jit(solution)/shard_map/ppermute | solution.py:401
  36.0 1.4 %collective-permute-done.4 = bf16[8,720]{1,0:T(8,128)(2,1)S(1)} collective-permute-done((bf16[8,720]{1,0:T(8,128)(2,1)S(1)}, bf16[8,720]{1,0:T(8,128)(2,1)S(1)}, u32[]{:S(2)}, u32[]{:S(2)}) %collective-permute-start.4) | collective-permute-done | bytes 11552 | tf_op jit(solution)/shard_map/ppermute | solution.py:401
  37.5 0.0 collective-permute-done.3
  37.5 1.2 %weigh.1.table_ref = bf16[128,192]{1,0:T(8,128)(2,1)S(1)} custom-call(s32[64]{0:T(128)S(1)} %copy-done.1, s32[4,256]{1,0:T(4,128)S(1)} %bitcast.21, bf16[4,8,720]{2,1,0:T(8,128)(2,1)S(1)} %pad_maximum_fusion.router_ref, bf16[2880,256]{1,0:T(8,128)(2,1)S(1)} %get-tuple-element.30.normed_ref), custom_call_target="tpu_custom_call" | custom-call | flops 1 | bytes 1 | tf_op jit(solution)/shard_map/weigh/pallas_call | solution.py:342
  38.7 0.0 copy-done.4
  38.7 1.2 %merge_side.1 = bf16[16,4,2880]{2,1,0:T(4,128)(2,1)} custom-call(bf16[128,192]{1,0:T(8,128)(2,1)S(1)} %weigh.1.table_ref, bf16[48,2880]{1,0:T(8,128)(2,1)S(1)} %copy-done.4, bf16[48,2880]{1,0:T(8,128)(2,1)S(1)} %collective-permute-done.got1_ref, bf16[48,2880]{1,0:T(8,128)(2,1)S(1)} %collective-permute-done.1.got2_ref, ...), custom_call_target="tpu_custom_call" | custom-call | flops 4000000000 | bytes 1 | tf_op jit(solution)/shard_map/merge_side/pallas_call | solution.py:368
  39.9 3.7 %all-to-all-done.own_ref = bf16[64,24,128]{2,1,0:T(8,128)(2,1)S(1)} async-done(((bf16[64,24,128]{2,1,0:T(8,128)(2,1)}), bf16[64,24,128]{2,1,0:T(8,128)(2,1)S(1)}, u32[]{:S(2)}, u32[]{:S(2)}) %all-to-all-start) | async-done | bytes 393248 | tf_op jit(solution)/shard_map/all_to_all | solution.py:397
  43.5 2.9 %collective-permute-start.6 = (bf16[64,24,128]{2,1,0:T(8,128)(2,1)S(1)}, bf16[64,24,128]{2,1,0:T(8,128)(2,1)S(1)}, u32[]{:S(2)}, u32[]{:S(2)}) collective-permute-start(bf16[64,24,128]{2,1,0:T(8,128)(2,1)S(1)} %all-to-all-done.own_ref), channel_id=1, source_target_pairs={{0,2},{2,0},{1,3},{3,1},{4,6},{6,4},{5,7},{7,5},{8,10},{10,8},{9,1... | collective-permute-start | bytes 1179656 | tf_op jit(solution)/shard_map/ppermute | solution.py:406
  46.4 6.3 %all-to-all-start.1 = ((bf16[16,4,2880]{2,1,0:T(4,128)(2,1)}), bf16[16,4,2880]{2,1,0:T(4,128)(2,1)S(1)}, u32[]{:S(2)}, u32[]{:S(2)}) async-start(bf16[16,4,2880]{2,1,0:T(4,128)(2,1)} %merge_side.1), calls=%async_computation.1 | async-start | bytes 753664 | tf_op jit(solution)/shard_map/all_to_all | solution.py:409
  52.7 0.0 collective-permute-start.7
  52.7 1.8 %collective-permute-done.6.across_ref = bf16[64,24,128]{2,1,0:T(8,128)(2,1)S(1)} collective-permute-done((bf16[64,24,128]{2,1,0:T(8,128)(2,1)S(1)}, bf16[64,24,128]{2,1,0:T(8,128)(2,1)S(1)}, u32[]{:S(2)}, u32[]{:S(2)}) %collective-permute-start.6) | collective-permute-done | bytes 393248 | tf_op jit(solution)/shard_map/ppermute | solution.py:406
  54.5 0.0 collective-permute-start.8
  54.5 0.0 collective-permute-done.7.core_ref
  54.5 1.7 %collective-permute-done.8.both_ref = bf16[64,24,128]{2,1,0:T(8,128)(2,1)S(1)} collective-permute-done((bf16[64,24,128]{2,1,0:T(8,128)(2,1)S(1)}, bf16[64,24,128]{2,1,0:T(8,128)(2,1)S(1)}, u32[]{:S(2)}, u32[]{:S(2)}) %collective-permute-start.8) | collective-permute-done | bytes 393248 | tf_op jit(solution)/shard_map/ppermute | solution.py:408
  56.2 2.2 %assemble.1 = bf16[2880,256]{1,0:T(8,128)(2,1)} custom-call(bf16[64,24,128]{2,1,0:T(8,128)(2,1)S(1)} %all-to-all-done.own_ref, bf16[64,24,128]{2,1,0:T(8,128)(2,1)S(1)} %collective-permute-done.6.across_ref, bf16[64,24,128]{2,1,0:T(8,128)(2,1)S(1)} %collective-permute-done.7.core_ref, bf16[64,24,128]{2,1,0:T(8,128)(2,1)S(1)} %collective-permute-done.8.both_ref), custom_call_target="tpu_custom_call" | custom-call | flops 1000000000 | bytes 4000000 | tf_op jit(solution)/shard_map/assemble/pallas_call | solution.py:172
  58.5 6.4 %all-to-all-done.1 = bf16[16,4,2880]{2,1,0:T(4,128)(2,1)S(1)} async-done(((bf16[16,4,2880]{2,1,0:T(4,128)(2,1)}), bf16[16,4,2880]{2,1,0:T(4,128)(2,1)S(1)}, u32[]{:S(2)}, u32[]{:S(2)}) %all-to-all-start.1) | async-done | bytes 368672 | tf_op jit(solution)/shard_map/all_to_all | solution.py:409
  64.9 0.2 convert_reduce_fusion
  65.1 0.6 fusion
  (2 shorter events, 0.0 us)
Async XLA Ops:
  0.6 5.3 %copy-start.1 = (s32[64]{0:T(128)S(1)}, s32[64]{0:T(128)}, u32[]{:S(2)}) copy-start(s32[64]{0:T(128)} %place_ref.3) | copy-start | bytes 772
  0.6 5.2 %copy-start.6 = (bf16[2880]{0:T(1024)(128)(2,1)S(1)}, bf16[2880]{0:T(1024)(128)(2,1)}, u32[]{:S(2)}) copy-start(bf16[2880]{0:T(1024)(128)(2,1)} %param.14) | copy-start | bytes 17284
  0.7 5.3 %copy-start = (s32[1,256,4]{1,2,0:T(4,128)S(1)}, s32[1,256,4]{1,2,0:T(4,128)}, u32[]{:S(2)}) copy-start(s32[1,256,4]{1,2,0:T(4,128)} %param.13) | copy-start | bytes 12292
  0.7 5.3 %copy-start.2 = (bf16[1,256,2880]{1,2,0:T(8,128)(2,1)S(1)}, bf16[1,256,2880]{1,2,0:T(8,128)(2,1)}, u32[]{:S(2)}) copy-start(bf16[1,256,2880]{1,2,0:T(8,128)(2,1)} %param.12) | copy-start | bytes 4423684
  5.9 25.5 %copy-start.5 = (bf16[720,8]{0,1:T(8,128)(2,1)S(1)}, bf16[720,8]{0,1:T(8,128)(2,1)}, u32[]{:S(2)}) copy-start(bf16[720,8]{0,1:T(8,128)(2,1)} %param.15) | copy-start | bytes 34564
  10.9 0.7 %copy-start.3 = (bf16[48,2880]{1,0:T(8,128)(2,1)}, bf16[48,2880]{1,0:T(8,128)(2,1)S(1)}, u32[]{:S(2)}) copy-start(bf16[48,2880]{1,0:T(8,128)(2,1)S(1)} %get-tuple-element.21.got0_ref) | copy-start | bytes 829444
  11.7 17.1 %collective-permute-start = (bf16[48,2880]{1,0:T(8,128)(2,1)}, bf16[48,2880]{1,0:T(8,128)(2,1)S(1)}, u32[]{:S(2)}, u32[]{:S(2)}) collective-permute-start(bf16[48,2880]{1,0:T(8,128)(2,1)} %get-tuple-element.26), channel_id=1, source_target_pairs={{0,64},{64,0},{128,192},{192,128},{1,65},{65,1},{129,193},{193,129... | collective-permute-start | bytes 829448 | tf_op jit(solution)/shard_map/ppermute | solution.py:396
  13.2 15.6 %collective-permute-start.1 = (bf16[48,2880]{1,0:T(8,128)(2,1)S(1)}, bf16[48,2880]{1,0:T(8,128)(2,1)S(1)}, u32[]{:S(2)}, u32[]{:S(2)}) collective-permute-start(bf16[48,2880]{1,0:T(8,128)(2,1)S(1)} %get-tuple-element.27), channel_id=1, source_target_pairs={{0,128},{64,192},{128,0},{192,64},{1,129},{65,193},{129,1},{193,65... | collective-permute-start | bytes 829448 | tf_op jit(solution)/shard_map/ppermute | solution.py:396
  15.9 15.5 %collective-permute-start.2 = (bf16[48,2880]{1,0:T(8,128)(2,1)S(1)}, bf16[48,2880]{1,0:T(8,128)(2,1)S(1)}, u32[]{:S(2)}, u32[]{:S(2)}) collective-permute-start(bf16[48,2880]{1,0:T(8,128)(2,1)S(1)} %get-tuple-element.28), channel_id=1, source_target_pairs={{0,192},{64,128},{128,64},{192,0},{1,193},{65,129},{129,65},{193,1... | collective-permute-start | bytes 829448 | tf_op jit(solution)/shard_map/ppermute | solution.py:396
  16.4 27.2 %all-to-all-start = ((bf16[64,24,128]{2,1,0:T(8,128)(2,1)}), bf16[64,24,128]{2,1,0:T(8,128)(2,1)S(1)}, u32[]{:S(2)}, u32[]{:S(2)}) async-start(bf16[64,24,128]{2,1,0:T(8,128)(2,1)} %encode.1), calls=%async_computation | async-start | bytes 786432 | tf_op jit(solution)/shard_map/all_to_all | solution.py:397
  28.7 10.0 %copy-start.4 = (bf16[48,2880]{1,0:T(8,128)(2,1)S(1)}, bf16[48,2880]{1,0:T(8,128)(2,1)}, u32[]{:S(2)}) copy-start(bf16[48,2880]{1,0:T(8,128)(2,1)} %copy-done.3) | copy-start | bytes 829444
  31.4 4.6 %collective-permute-start.5 = (bf16[8,720]{1,0:T(8,128)(2,1)S(1)}, bf16[8,720]{1,0:T(8,128)(2,1)S(1)}, u32[]{:S(2)}, u32[]{:S(2)}) collective-permute-start(bf16[8,720]{1,0:T(8,128)(2,1)S(1)} %bitcast.24), channel_id=1, source_target_pairs={{0,3},{1,2},{2,1},{3,0},{4,7},{5,6},{6,5},{7,4},{8,11},{9,10},{10,... | collective-permute-start | bytes 34568 | tf_op jit(solution)/shard_map/ppermute | solution.py:401
  32.2 5.2 %collective-permute-start.4 = (bf16[8,720]{1,0:T(8,128)(2,1)S(1)}, bf16[8,720]{1,0:T(8,128)(2,1)S(1)}, u32[]{:S(2)}, u32[]{:S(2)}) collective-permute-start(bf16[8,720]{1,0:T(8,128)(2,1)S(1)} %bitcast.25), channel_id=1, source_target_pairs={{0,2},{1,3},{2,0},{3,1},{4,6},{5,7},{6,4},{7,5},{8,10},{9,11},{10,... | collective-permute-start | bytes 34568 | tf_op jit(solution)/shard_map/ppermute | solution.py:401
  34.7 2.8 %collective-permute-start.3 = (bf16[8,720]{1,0:T(8,128)(2,1)S(1)}, bf16[8,720]{1,0:T(8,128)(2,1)S(1)}, u32[]{:S(2)}, u32[]{:S(2)}) collective-permute-start(bf16[8,720]{1,0:T(8,128)(2,1)S(1)} %bitcast.26), channel_id=1, source_target_pairs={{0,1},{1,0},{2,3},{3,2},{4,5},{5,4},{6,7},{7,6},{8,9},{9,8},{10,11... | collective-permute-start | bytes 34568 | tf_op jit(solution)/shard_map/ppermute | solution.py:401
  43.5 11.0 %collective-permute-start.6 = (bf16[64,24,128]{2,1,0:T(8,128)(2,1)S(1)}, bf16[64,24,128]{2,1,0:T(8,128)(2,1)S(1)}, u32[]{:S(2)}, u32[]{:S(2)}) collective-permute-start(bf16[64,24,128]{2,1,0:T(8,128)(2,1)S(1)} %all-to-all-done.own_ref), channel_id=1, source_target_pairs={{0,2},{2,0},{1,3},{3,1},{4,6},{6,4},{5,7},{7,5},{8,10},{10,8},{9,1... | collective-permute-start | bytes 1179656 | tf_op jit(solution)/shard_map/ppermute | solution.py:406
  46.4 18.5 %all-to-all-start.1 = ((bf16[16,4,2880]{2,1,0:T(4,128)(2,1)}), bf16[16,4,2880]{2,1,0:T(4,128)(2,1)S(1)}, u32[]{:S(2)}, u32[]{:S(2)}) async-start(bf16[16,4,2880]{2,1,0:T(4,128)(2,1)} %merge_side.1), calls=%async_computation.1 | async-start | bytes 753664 | tf_op jit(solution)/shard_map/all_to_all | solution.py:409
  52.7 1.8 %collective-permute-start.7 = (bf16[64,24,128]{2,1,0:T(8,128)(2,1)S(1)}, bf16[64,24,128]{2,1,0:T(8,128)(2,1)S(1)}, u32[]{:S(2)}, u32[]{:S(2)}) collective-permute-start(bf16[64,24,128]{2,1,0:T(8,128)(2,1)S(1)} %all-to-all-done.own_ref), channel_id=1, source_target_pairs={{0,1},{1,0},{2,3},{3,2},{4,5},{5,4},{6,7},{7,6},{8,9},{9,8},{10,11... | collective-permute-start | bytes 1179656 | tf_op jit(solution)/shard_map/ppermute | solution.py:407
  54.5 1.7 %collective-permute-start.8 = (bf16[64,24,128]{2,1,0:T(8,128)(2,1)S(1)}, bf16[64,24,128]{2,1,0:T(8,128)(2,1)S(1)}, u32[]{:S(2)}, u32[]{:S(2)}) collective-permute-start(bf16[64,24,128]{2,1,0:T(8,128)(2,1)S(1)} %collective-permute-done.6.across_ref), channel_id=1, source_target_pairs={{0,1},{1,0},{2,3},{3,2},{4,5},{5,4},{6,7},{7,6},{8,9},{9,8},{10,11... | collective-permute-start | bytes 1179656 | tf_op jit(solution)/shard_map/ppermute | solution.py:408

commit v8 on v7

--- a/solution.py
+++ b/solution.py
@@ -86,20 +86,22 @@
     return jnp.where(values < 0, -out, out)
 
 
-def encode_kernel(
-    place_hbm, master_ref, out_ref, place_ref, slot_ref, held_ref, raw_ref, sems, place_sem
-):
-    place_copy = pltpu.make_async_copy(place_hbm, place_ref, place_sem)
-    place_copy.start()
+def fetch(pairs, sems):
     copies = []
-    for g in range(HALF // PAIRS):
-        at = g * PAIRS
-        wide = min(PAIRS, COLS - HALF - at)
-        for n, (start, size) in enumerate(((at, PAIRS), (HALF + at, wide))):
-            part = pl.ds(start, size)
-            copy = pltpu.make_async_copy(master_ref.at[part], raw_ref.at[part], sems.at[2 * g + n])
-            copy.start()
-            copies.append(copy)
+    for n, (source, target) in enumerate(pairs):
+        copy = pltpu.make_async_copy(source, target, sems.at[n])
+        copy.start()
+        copies.append(copy)
+    return copies
+
+
+def master_parts():
+    for at in range(0, HALF, PAIRS):
+        yield at, PAIRS
+        yield HALF + at, min(PAIRS, COLS - HALF - at)
+
+
+def encode(copies, raw_ref, held_ref):
     spread = (iota((128, 128), 0) == (iota((128, 128), 1) // 32) * 32 + 31).astype(F32).astype(BF)
     for g in range(HALF // PAIRS):
         at = g * PAIRS
@@ -114,35 +116,6 @@
         high = high.reshape(PAIRS * SLOTS, ROWS)
         values = jnp.concatenate([low, high], axis=1)
         held_ref[at * SLOTS : (at + PAIRS) * SLOTS, :] = round_blocks(values, spread)
-
-    place_copy.wait()
-    invert(place_ref, slot_ref)
-
-    def deal(o, _):
-        out_ref[o] = held_ref[pl.ds(slot_ref[o], HALF, stride=SLOTS), :].astype(BF)
-        return 0
-
-    lax.fori_loop(0, SLOTS, deal, 0, unroll=8)
-
-
-def encode(placement, master):
-    return pl.pallas_call(
-        encode_kernel,
-        name="encode",
-        out_shape=jax.ShapeDtypeStruct((SLOTS, HALF, 128), BF),
-        in_specs=[pl.BlockSpec(memory_space=pl.ANY)] * 2,
-        out_specs=pl.BlockSpec(memory_space=VMEM),
-        scratch_shapes=[
-            pltpu.SMEM((SLOTS,), jnp.int32),
-            pltpu.SMEM((SLOTS,), jnp.int32),
-            VMEM((HALF * SLOTS, 128), F32),
-            VMEM((COLS, SLOTS, ROWS), F32),
-            pltpu.SemaphoreType.DMA((2 * HALF // PAIRS,)),
-            pltpu.SemaphoreType.DMA(()),
-        ],
-        compiler_params=params(16),
-        cost_estimate=pl.CostEstimate(flops=1, bytes_accessed=1, transcendentals=0),
-    )(placement, master)
 
 
 GROUP = 16
@@ -202,32 +175,53 @@
     return jnp.sum(jnp.where(iota((8, TOK), 0) == expert, table, 0.0), axis=0, keepdims=True)
 
 
-def expert_kernel(
-    place_ref,
-    hidden_ref,
-    routes_ref,
-    gain_ref,
+def prepare_kernel(
+    place_hbm,
+    master_hbm,
+    hidden_hbm,
+    routes_hbm,
+    gain_hbm,
     gate_up_hbm,
     down_hbm,
+    chunks_ref,
     out0_ref,
     out1_ref,
     out2_ref,
     out3_ref,
     normed_ref,
     rows_ref,
+    place_ref,
     slot_ref,
+    routes_ref,
+    gain_ref,
+    raw_ref,
+    held_ref,
+    hidden_ref,
     gate_up_ref,
     down_ref,
     sems,
 ):
-    copies = []
-    for m, (hbm, ref) in enumerate(((gate_up_hbm, gate_up_ref), (down_hbm, down_ref))):
-        for n in range(PIECES):
-            part = pl.ds(n * PIECE, PIECE)
-            copy = pltpu.make_async_copy(hbm.at[part], ref.at[part], sems.at[m * PIECES + n])
-            copy.start()
-            copies.append(copy)
+    pieces = [pl.ds(n * PIECE, PIECE) for n in range(PIECES)]
+    masters = [pl.ds(*part) for part in master_parts()]
+    copies = fetch(
+        [(master_hbm.at[part], raw_ref.at[part]) for part in masters]
+        + [(place_hbm, place_ref), (routes_hbm, routes_ref), (gain_hbm, gain_ref)]
+        + [(hidden_hbm.at[part], hidden_ref.at[part]) for part in pieces]
+        + [(gate_up_hbm.at[part], gate_up_ref.at[part]) for part in pieces]
+        + [(down_hbm.at[part], down_ref.at[part]) for part in pieces],
+        sems,
+    )
+    encode(copies, raw_ref, held_ref)
+    for copy in copies[len(masters) :]:
+        copy.wait()
     invert(place_ref, slot_ref)
+
+    def deal(o, _):
+        chunks_ref[o] = held_ref[pl.ds(slot_ref[o], HALF, stride=SLOTS), :].astype(BF)
+        return 0
+
+    lax.fori_loop(0, SLOTS, deal, 0, unroll=8)
+
     side = lax.axis_index("x")
     owner = side * INNER + lax.axis_index("yl") * DEPTH + lax.axis_index("z")
     mine = slot_ref[owner] // DEPTH
@@ -248,7 +242,7 @@
     ones = jnp.ones((128, TOK), BF)
     for at in range(0, D, 128):
         size = min(128, D - at)
-        gain = gain_ref[:, at : at + size].astype(F32)
+        gain = gain_ref[at : at + size].astype(F32)
         diagonal = jnp.where(
             iota((size, size), 0) == iota((size, size), 1), jnp.broadcast_to(gain, (size, size)), 0.0
         ).astype(BF)
@@ -258,15 +252,12 @@
 
     projected = jnp.zeros((TOK, 2 * HID), F32)
     for n in range(PIECES):
-        copies[n].wait()
         part = slice(n * PIECE, (n + 1) * PIECE)
         projected = projected + tn(normed_ref[part, :], gate_up_ref[part, :])
     gate = projected[:, :HID]
     up = projected[:, HID:]
     activated = (gate * jax.nn.sigmoid(1.702 * gate) * (up + 1.0)).astype(BF)
     activated = nn(pack, activated).astype(BF)
-    for n in range(PIECES):
-        copies[PIECES + n].wait()
     for at in range(0, D, 640):
         size = min(640, D - at)
         terms = nt(activated, down_ref[at : at + size, :]).astype(BF)
@@ -279,35 +270,40 @@
         rows_ref[:, at : at + size] = nt(own, hidden_ref[at : at + size, :])[:4]
 
 
-def expert_terms(placement, hidden, routes, gain, gate_up, down):
+def prepare(placement, master, hidden, routes, gain, gate_up, down):
     whole = pl.BlockSpec(memory_space=VMEM)
+    apart = pl.BlockSpec(memory_space=pl.ANY)
     out = jax.ShapeDtypeStruct((SIDE_ROWS, D), BF)
     return pl.pallas_call(
-        expert_kernel,
-        name="expert_terms",
-        out_shape=(out,) * 4
+        prepare_kernel,
+        name="prepare",
+        out_shape=(jax.ShapeDtypeStruct((SLOTS, HALF, 128), BF),)
+        + (out,) * 4
         + (jax.ShapeDtypeStruct((D, TOK), BF), jax.ShapeDtypeStruct((4, D), F32)),
-        in_specs=[
-            pl.BlockSpec(memory_space=SMEM),
-            whole,
-            whole,
-            whole,
-            pl.BlockSpec(memory_space=pl.ANY),
-            pl.BlockSpec(memory_space=pl.ANY),
-        ],
-        out_specs=(whole,) * 6,
+        in_specs=[apart] * 7,
+        out_specs=(whole,) * 7,
         scratch_shapes=[
             pltpu.SMEM((SLOTS,), jnp.int32),
+            pltpu.SMEM((SLOTS,), jnp.int32),
+            VMEM((4, TOK), jnp.int32),
+            VMEM((D,), BF),
+            VMEM((COLS, SLOTS, ROWS), F32),
+            VMEM((HALF * SLOTS, 128), F32),
+            VMEM((D, TOK), BF),
             VMEM((D, 2 * HID), BF),
             VMEM((D, HID), BF),
-            pltpu.SemaphoreType.DMA((2 * PIECES,)),
+            pltpu.SemaphoreType.DMA((2 * HALF // PAIRS + 3 + 3 * PIECES,)),
         ],
         compiler_params=params(32),
-        cost_estimate=pl.CostEstimate(flops=3 * 10**9, bytes_accessed=8 * 10**6, transcendentals=0),
-    )(placement, hidden, routes, gain, gate_up, down)
-
-
-def weigh_kernel(place_ref, routes_ref, router_ref, normed_ref, out_ref, slot_ref, held_ref):
+        cost_estimate=pl.CostEstimate(flops=8 * 10**9, bytes_accessed=10**7, transcendentals=0),
+    )(
+        *map(in_hbm, (placement, master, hidden, routes, gain, gate_up, down))
+    )
+
+
+def weigh_kernel(
+    place_ref, routes_ref, near_ref, far_ref, normed_ref, out_ref, slot_ref, held_ref
+):
     invert(place_ref, slot_ref)
     side = lax.axis_index("x")
     inner = lax.axis_index("yl") * DEPTH + lax.axis_index("z")
@@ -316,7 +312,8 @@
     logits = jnp.zeros((8, TOK), F32)
     for d in range(4):
         start = pl.multiple_of((rep ^ d) * 720, 720)
-        logits = logits + nn(router_ref[d], normed_ref[pl.ds(start, 720), :])
+        router = (near_ref if d < 2 else far_ref)[d % 2]
+        logits = logits + nn(router, normed_ref[pl.ds(start, 720), :])
     chosen = choices(routes_ref)
     powered = jnp.where(chosen > 0, jnp.exp(logits), 0.0)
     weights = powered / jnp.sum(powered, axis=0, keepdims=True)
@@ -338,17 +335,17 @@
     out_ref[local:, :] = (table - upper.astype(F32)).astype(BF)
 
 
-def weigh(placement, routes, router, normed):
+def weigh(placement, routes, near, far, normed):
     return pl.pallas_call(
         weigh_kernel,
         name="weigh",
         out_shape=jax.ShapeDtypeStruct((8 * INNER, PACKED), BF),
-        in_specs=[pl.BlockSpec(memory_space=SMEM)] + [pl.BlockSpec(memory_space=VMEM)] * 3,
+        in_specs=[pl.BlockSpec(memory_space=SMEM)] + [pl.BlockSpec(memory_space=VMEM)] * 4,
         out_specs=pl.BlockSpec(memory_space=VMEM),
         scratch_shapes=[pltpu.SMEM((SLOTS,), jnp.int32), VMEM((TOK, PACKED), F32)],
         compiler_params=params(16),
         cost_estimate=pl.CostEstimate(flops=1, bytes_accessed=1, transcendentals=0),
-    )(placement, routes, router, normed)
+    )(placement, routes, near, far, normed)
 
 
 def merge_kernel(table_ref, got0_ref, got1_ref, got2_ref, got3_ref, out_ref):
@@ -376,40 +373,62 @@
     )(table, *got)
 
 
+def finish_kernel(got_ref, rows_ref, out_ref):
+    total = rows_ref[...]
+    for n in range(INNER):
+        total = total + got_ref[n].astype(F32)
+    out_ref[...] = total.astype(BF)
+
+
+def finish(got, rows):
+    whole = pl.BlockSpec(memory_space=VMEM)
+    return pl.pallas_call(
+        finish_kernel,
+        name="finish",
+        out_shape=jax.ShapeDtypeStruct((4, D), BF),
+        in_specs=[whole] * 2,
+        out_specs=whole,
+        compiler_params=params(16),
+        cost_estimate=pl.CostEstimate(flops=10**6, bytes_accessed=10**6, transcendentals=0),
+    )(got, rows)
+
+
 def on_device(
     master, placement, resident_gate_up, resident_down, hidden, routes, norm_gain, router
 ):
-    chunks = encode(in_hbm(placement), in_hbm(jnp.transpose(master, (2, 0, 1))))
+    swap = ((0, 1), (1, 0))
+    router_rows = router.T
+    router_core = lax.ppermute(router_rows, "c", swap)
     chosen = routes[0].T
-    norm_gain, chunks = lax.optimization_barrier((norm_gain, chunks))
-    *terms, normed, rows = expert_terms(
+    chunks, *terms, normed, rows = prepare(
         placement,
+        jnp.transpose(master, (2, 0, 1)),
         hidden[0].T,
         chosen,
-        norm_gain[None],
-        in_hbm(resident_gate_up[0]),
-        in_hbm(resident_down[0].T),
+        norm_gain,
+        resident_gate_up[0],
+        resident_down[0].T,
     )
-    got = [terms[0]]
-    chunks, *terms = lax.optimization_barrier((chunks, *terms))
+    chunks, router_core, *terms = lax.optimization_barrier((chunks, router_core, *terms))
+    got = [in_hbm(terms[0])]
     for d in range(1, SIDE):
         got.append(lax.ppermute(terms[d], "x", [(x, x ^ d) for x in range(SIDE)]))
     chunks = lax.all_to_all(chunks, FSDP, split_axis=0, concat_axis=0, tiled=True)
-    router_rows, *_ = lax.optimization_barrier((router.T, *got[1:]))
-    routers = [router_rows]
-    for d in range(1, 4):
-        routers.append(lax.ppermute(router_rows, REP, [(r, r ^ d) for r in range(4)]))
-    table = weigh(placement, chosen, jnp.stack(routers), normed)
+
+    router_core, *_ = lax.optimization_barrier((router_core, *got[1:]))
+    near = jnp.stack([router_rows, router_core])
+    far = lax.ppermute(near, "yh", swap)
+    table = weigh(placement, chosen, near, far, normed)
     terms = merge_side(table, got)
     chunks, terms = lax.optimization_barrier((chunks, terms))
 
-    across = lax.ppermute(chunks, "yh", ((0, 1), (1, 0)))
-    core = lax.ppermute(chunks, "c", ((0, 1), (1, 0)))
-    both = lax.ppermute(across, "c", ((0, 1), (1, 0)))
+    core = lax.ppermute(chunks, "c", swap)
+    across = lax.ppermute(chunks, "yh", swap)
+    both = lax.ppermute(across, "c", swap)
     terms = lax.all_to_all(terms, ("yl", "z"), split_axis=0, concat_axis=0, tiled=True)
     refreshed = assemble(chunks, across, core, both).T
     terms, refreshed = lax.optimization_barrier((terms, refreshed))
-    decoded = (rows + jnp.sum(terms.astype(F32), axis=0)).astype(BF)
+    decoded = finish(terms, rows)
     return (refreshed[None], decoded[None])
 
 

time: 66.3 us -> 62.7 us (0.946)
  waiting for transfers between devices: 18.9 us -> 16.4 us
  starting transfers between devices: 29.6 us -> 30.7 us
  Pallas kernels: 14.8 us -> 13.8 us
  other arithmetic: 0.79 us -> 0.01 us
    pallas_call x2, Pallas kernels: 10.2 us -> 8.31 us  [the longest x1 7.63 us: prepare(): pl.pallas_call(prepare_kernel, name='prepare', out_shape=(jax.ShapeDtypeS...]
    all_to_all x1, waiting for transfers between devices: 6.4 us -> 4.87 us  [on_device(): lax.all_to_all(terms, ('yl', 'z'), split_axis=0, concat_axis=0, tiled=True)]
    ppermute x6 -> x5, waiting for transfers between devices: 6.17 us -> 4.97 us  [the longest x1 2.2 us: on_device(): far = lax.ppermute(near, 'yh', swap)]
    all_to_all x1, starting transfers between devices: 6.31 us -> 7.26 us  [on_device(): lax.all_to_all(terms, ('yl', 'z'), split_axis=0, concat_axis=0, tiled=True)]
    pallas_call x1, Pallas kernels: 1.16 us -> 2.1 us  [merge_side(): pl.pallas_call(merge_kernel, name='merge_side', out_shape=jax.ShapeDtypeS...]
    ppermute x3, waiting for transfers between devices: 2.67 us -> 3.35 us  [on_device(): got.append(lax.ppermute(terms[d], 'x', [(x, x ^ d) for x in range(SIDE)]))]
    ppermute x6 -> x5, starting transfers between devices: 6.31 us -> 6.37 us  [the longest x1 3.35 us: on_device(): far = lax.ppermute(near, 'yh', swap)]
  transfers between devices with their start and end apart: 11 -> 10, of which waited for: 7 -> 8; matrix products, arithmetic and copies ran while one was open for 0% -> 0% of each run, Pallas kernels for 7% -> 21%
where the time goes in v8:
time: 62.7 us; the launch traced here: 62.4 us
  starting transfers between devices  30.7 us (49%)
  waiting for transfers between devices  16.4 us (26%)
  Pallas kernels  13.8 us (22%)
  local copies, waits for them, and re-layouts  0.72 us (1%)
  between operations  0.72 us (1%)
    all_to_all x1, starting transfers between devices, on_device(): lax.all_to_all(chunks, FSDP, split_axis=0, concat_axis=0, tiled=True)  12.3 us
    pallas_call x1, Pallas kernels, prepare(): pl.pallas_call(prepare_kernel, name='prepare', out_shape=(jax.ShapeDtypeS...  7.63 us
    all_to_all x1, starting transfers between devices, on_device(): lax.all_to_all(terms, ('yl', 'z'), split_axis=0, concat_axis=0, tiled=True)  7.26 us
    all_to_all x1, waiting for transfers between devices, on_device(): lax.all_to_all(terms, ('yl', 'z'), split_axis=0, concat_axis=0, tiled=True)  4.87 us
    ppermute x3, starting transfers between devices, on_device(): got.append(lax.ppermute(terms[d], 'x', [(x, x ^ d) for x in range(SIDE)]))  4.7 us
    ppermute x3, waiting for transfers between devices, on_device(): got.append(lax.ppermute(terms[d], 'x', [(x, x ^ d) for x in range(SIDE)]))  3.35 us
    ppermute x1, starting transfers between devices, on_device(): far = lax.ppermute(near, 'yh', swap)  3.35 us
    all_to_all x1, waiting for transfers between devices, on_device(): lax.all_to_all(chunks, FSDP, split_axis=0, concat_axis=0, tiled=True)  3.26 us
  transfers between devices with their start and end apart: 10, of which 8 were waited for; matrix products, arithmetic and copies ran while one was open for 0% of the time, Pallas kernels for 21%

profile of v8, /device:TPU:32, one launch (start us, length us, event | category | flops | bytes accessed | tf_op | source)
XLA Modules:
  0.0 62.4 jit_solution(2598306024086443251)
XLA Ops:
  0.6 0.1 collective-permute-start
  0.7 0.0 copy-start.3
  0.7 0.0 copy-start
  0.8 0.0 copy-start.1
  0.8 7.6 %prepare.1 = (bf16[64,24,128]{2,1,0:T(8,128)(2,1)}, bf16[48,2880]{1,0:T(8,128)(2,1)S(1)}, bf16[48,2880]{1,0:T(8,128)(2,1)}, bf16[48,2880]{1,0:T(8,128)(2,1)S(1)}...) custom-call(s32[64]{0:T(128)} %place_ref.1, f32[45,64,64]{2,1,0:T(8,128)} %bitcast.25, ...), custom_call_target="tpu_custom_call" | custom-call | flops 8000000000 | bytes 10000000 | tf_op jit(solution)/shard_map/prepare/pallas_call | solution.py:277
  8.4 0.0 copy-start.2
  8.4 0.7 %copy-done.2 = bf16[48,2880]{1,0:T(8,128)(2,1)} copy-done((bf16[48,2880]{1,0:T(8,128)(2,1)}, bf16[48,2880]{1,0:T(8,128)(2,1)S(1)}, u32[]{:S(2)}) %copy-start.2) | copy-done | bytes 276504
  9.1 0.0 collective-permute-done
  9.1 1.5 %collective-permute-start.1 = (bf16[48,2880]{1,0:T(8,128)(2,1)}, bf16[48,2880]{1,0:T(8,128)(2,1)S(1)}, u32[]{:S(2)}, u32[]{:S(2)}) collective-permute-start(bf16[48,2880]{1,0:T(8,128)(2,1)} %get-tuple-element.27), channel_id=1, source_target_pairs={{0,64},{64,0},{128,192},{192,128},{1,65},{65,1},{129,193},{193,129... | collective-permute-start | bytes 829448 | tf_op jit(solution)/shard_map/ppermute | solution.py:415
  10.6 2.7 %collective-permute-start.2 = (bf16[48,2880]{1,0:T(8,128)(2,1)S(1)}, bf16[48,2880]{1,0:T(8,128)(2,1)S(1)}, u32[]{:S(2)}, u32[]{:S(2)}) collective-permute-start(bf16[48,2880]{1,0:T(8,128)(2,1)S(1)} %get-tuple-element.28), channel_id=1, source_target_pairs={{0,128},{64,192},{128,0},{192,64},{1,129},{65,193},{129,1},{193,65... | collective-permute-start | bytes 829448 | tf_op jit(solution)/shard_map/ppermute | solution.py:415
  13.3 0.5 collective-permute-start.3
  13.8 12.3 %all-to-all-start = ((bf16[64,24,128]{2,1,0:T(8,128)(2,1)}), bf16[64,24,128]{2,1,0:T(8,128)(2,1)S(1)}, u32[]{:S(2)}, u32[]{:S(2)}) async-start(bf16[64,24,128]{2,1,0:T(8,128)(2,1)} %get-tuple-element.25), calls=%async_computation | async-start | bytes 786432 | tf_op jit(solution)/shard_map/all_to_all | solution.py:416
  26.2 0.0 collective-permute-done.1.got1_ref
  26.2 0.7 %collective-permute-done.2.got2_ref = bf16[48,2880]{1,0:T(8,128)(2,1)S(1)} collective-permute-done((bf16[48,2880]{1,0:T(8,128)(2,1)S(1)}, bf16[48,2880]{1,0:T(8,128)(2,1)S(1)}, u32[]{:S(2)}, u32[]{:S(2)}) %collective-permute-start.2) | collective-permute-done | bytes 276512 | tf_op jit(solution)/shard_map/ppermute | solution.py:415
  26.8 2.7 %collective-permute-done.3.got3_ref = bf16[48,2880]{1,0:T(8,128)(2,1)S(1)} collective-permute-done((bf16[48,2880]{1,0:T(8,128)(2,1)S(1)}, bf16[48,2880]{1,0:T(8,128)(2,1)S(1)}, u32[]{:S(2)}, u32[]{:S(2)}) %collective-permute-start.3) | collective-permute-done | bytes 276512 | tf_op jit(solution)/shard_map/ppermute | solution.py:415
  29.5 0.0 copy-done.3
  29.5 3.3 %collective-permute-start.4 = (bf16[2,8,720]{2,1,0:T(8,128)(2,1)S(1)}, bf16[2,8,720]{2,1,0:T(8,128)(2,1)S(1)}, u32[]{:S(2)}, u32[]{:S(2)}) collective-permute-start(bf16[2,8,720]{2,1,0:T(8,128)(2,1)S(1)} %pad_maximum_fusion.near_ref), channel_id=1, source_target_pairs={{0,2},{2,0},{1,3},{3,1},{4,6},{6,4},{5,7},{7,5},{8,10},{10,8},{9,1... | collective-permute-start | bytes 69128 | tf_op jit(solution)/shard_map/ppermute | solution.py:420
  32.9 2.2 %collective-permute-done.4.far_ref = bf16[2,8,720]{2,1,0:T(8,128)(2,1)S(1)} collective-permute-done((bf16[2,8,720]{2,1,0:T(8,128)(2,1)S(1)}, bf16[2,8,720]{2,1,0:T(8,128)(2,1)S(1)}, u32[]{:S(2)}, u32[]{:S(2)}) %collective-permute-start.4) | collective-permute-done | bytes 23072 | tf_op jit(solution)/shard_map/ppermute | solution.py:420
  35.1 0.0 copy-done
  35.1 0.0 copy-done.1
  35.1 1.2 %weigh.1.table_ref = bf16[128,192]{1,0:T(8,128)(2,1)S(1)} custom-call(s32[64]{0:T(128)S(1)} %copy-done.1, s32[4,256]{1,0:T(4,128)S(1)} %bitcast.19, bf16[2,8,720]{2,1,0:T(8,128)(2,1)S(1)} %pad_maximum_fusion.near_ref, bf16[2,8,720]{2,1,0:T(8,128)(2,1)S(1)} %collective-permute-done.4.far_ref, bf16[2880,256]{1,0:T(8,128)(2,1)S(1)} %get-tuple-element.31.normed_ref), custom_call_target="tpu_custom_call" | custom-call | flops 1 | bytes 1 | tf_op jit(solution)/shard_map/weigh/pallas_call | solution.py:339
  36.3 2.1 %merge_side.1 = bf16[16,4,2880]{2,1,0:T(4,128)(2,1)} custom-call(bf16[128,192]{1,0:T(8,128)(2,1)S(1)} %weigh.1.table_ref, bf16[48,2880]{1,0:T(8,128)(2,1)} %copy-done.2, bf16[48,2880]{1,0:T(8,128)(2,1)S(1)} %collective-permute-done.1.got1_ref, bf16[48,2880]{1,0:T(8,128)(2,1)S(1)} %collective-permute-done.2.got2_ref, ...), custom_call_target="tpu_custom_call" | custom-call | flops 4000000000 | bytes 1 | tf_op jit(solution)/shard_map/merge_side/pallas_call | solution.py:365
  38.4 3.3 %all-to-all-done.own_ref = bf16[64,24,128]{2,1,0:T(8,128)(2,1)S(1)} async-done(((bf16[64,24,128]{2,1,0:T(8,128)(2,1)}), bf16[64,24,128]{2,1,0:T(8,128)(2,1)S(1)}, u32[]{:S(2)}, u32[]{:S(2)}) %all-to-all-start) | async-done | bytes 393248 | tf_op jit(solution)/shard_map/all_to_all | solution.py:416
  41.6 2.9 %collective-permute-start.5 = (bf16[64,24,128]{2,1,0:T(8,128)(2,1)S(1)}, bf16[64,24,128]{2,1,0:T(8,128)(2,1)S(1)}, u32[]{:S(2)}, u32[]{:S(2)}) collective-permute-start(bf16[64,24,128]{2,1,0:T(8,128)(2,1)S(1)} %all-to-all-done.own_ref), channel_id=1, source_target_pairs={{0,2},{2,0},{1,3},{3,1},{4,6},{6,4},{5,7},{7,5},{8,10},{10,8},{9,1... | collective-permute-start | bytes 1179656 | tf_op jit(solution)/shard_map/ppermute | solution.py:426
  44.6 7.3 %all-to-all-start.1 = ((bf16[16,4,2880]{2,1,0:T(4,128)(2,1)}), bf16[16,4,2880]{2,1,0:T(4,128)(2,1)S(1)}, u32[]{:S(2)}, u32[]{:S(2)}) async-start(bf16[16,4,2880]{2,1,0:T(4,128)(2,1)} %merge_side.1), calls=%async_computation.1 | async-start | bytes 753664 | tf_op jit(solution)/shard_map/all_to_all | solution.py:428
  51.8 0.0 collective-permute-start.6
  51.8 1.1 %collective-permute-done.5.across_ref = bf16[64,24,128]{2,1,0:T(8,128)(2,1)S(1)} collective-permute-done((bf16[64,24,128]{2,1,0:T(8,128)(2,1)S(1)}, bf16[64,24,128]{2,1,0:T(8,128)(2,1)S(1)}, u32[]{:S(2)}, u32[]{:S(2)}) %collective-permute-start.5) | collective-permute-done | bytes 393248 | tf_op jit(solution)/shard_map/ppermute | solution.py:426
  52.9 0.0 collective-permute-start.7
  52.9 0.7 %collective-permute-done.6.core_ref = bf16[64,24,128]{2,1,0:T(8,128)(2,1)S(1)} collective-permute-done((bf16[64,24,128]{2,1,0:T(8,128)(2,1)S(1)}, bf16[64,24,128]{2,1,0:T(8,128)(2,1)S(1)}, u32[]{:S(2)}, u32[]{:S(2)}) %collective-permute-start.6) | collective-permute-done | bytes 393248 | tf_op jit(solution)/shard_map/ppermute | solution.py:425
  53.5 1.1 %collective-permute-done.7.both_ref = bf16[64,24,128]{2,1,0:T(8,128)(2,1)S(1)} collective-permute-done((bf16[64,24,128]{2,1,0:T(8,128)(2,1)S(1)}, bf16[64,24,128]{2,1,0:T(8,128)(2,1)S(1)}, u32[]{:S(2)}, u32[]{:S(2)}) %collective-permute-start.7) | collective-permute-done | bytes 393248 | tf_op jit(solution)/shard_map/ppermute | solution.py:427
  54.6 2.2 %assemble.1 = bf16[2880,256]{1,0:T(8,128)(2,1)} custom-call(bf16[64,24,128]{2,1,0:T(8,128)(2,1)S(1)} %all-to-all-done.own_ref, bf16[64,24,128]{2,1,0:T(8,128)(2,1)S(1)} %collective-permute-done.5.across_ref, bf16[64,24,128]{2,1,0:T(8,128)(2,1)S(1)} %collective-permute-done.6.core_ref, bf16[64,24,128]{2,1,0:T(8,128)(2,1)S(1)} %collective-permute-done.7.both_ref), custom_call_target="tpu_custom_call" | custom-call | flops 1000000000 | bytes 4000000 | tf_op jit(solution)/shard_map/assemble/pallas_call | solution.py:145
  56.8 4.9 %all-to-all-done.1.got_ref = bf16[16,4,2880]{2,1,0:T(4,128)(2,1)S(1)} async-done(((bf16[16,4,2880]{2,1,0:T(4,128)(2,1)}), bf16[16,4,2880]{2,1,0:T(4,128)(2,1)S(1)}, u32[]{:S(2)}, u32[]{:S(2)}) %all-to-all-start.1) | async-done | bytes 368672 | tf_op jit(solution)/shard_map/all_to_all | solution.py:428
  61.7 0.7 %finish.1 = bf16[4,2880]{1,0:T(4,128)(2,1)} custom-call(bf16[16,4,2880]{2,1,0:T(4,128)(2,1)S(1)} %all-to-all-done.1.got_ref, f32[4,2880]{1,0:T(4,128)S(1)} %get-tuple-element.37.rows_ref), custom_call_target="tpu_custom_call" | custom-call | flops 1000000 | bytes 1000000 | tf_op jit(solution)/shard_map/finish/pallas_call | solution.py:385
  (1 shorter events, 0.0 us)
Async XLA Ops:
  0.6 8.5 %collective-permute-start = (bf16[8,720]{1,0:T(8,128)(2,1)}, bf16[8,720]{1,0:T(8,128)(2,1)S(1)}, u32[]{:S(2)}, u32[]{:S(2)}) collective-permute-start(bf16[8,720]{1,0:T(8,128)(2,1)} %bitcast.21), channel_id=1, source_target_pairs={{0,1},{1,0},{2,3},{3,2},{4,5},{5,4},{6,7},{7,6},{8,9},{9,8},{10,11... | collective-permute-start | bytes 34568 | tf_op jit(solution)/shard_map/ppermute | solution.py:401
  0.7 28.8 %copy-start.3 = (bf16[720,8]{0,1:T(8,128)(2,1)S(1)}, bf16[720,8]{0,1:T(8,128)(2,1)}, u32[]{:S(2)}) copy-start(bf16[720,8]{0,1:T(8,128)(2,1)} %param.15) | copy-start | bytes 34564
  0.7 34.3 %copy-start = (s32[1,256,4]{1,2,0:T(4,128)S(1)}, s32[1,256,4]{1,2,0:T(4,128)}, u32[]{:S(2)}) copy-start(s32[1,256,4]{1,2,0:T(4,128)} %param.13) | copy-start | bytes 12292
  0.8 34.3 %copy-start.1 = (s32[64]{0:T(128)S(1)}, s32[64]{0:T(128)}, u32[]{:S(2)}) copy-start(s32[64]{0:T(128)} %place_ref.1) | copy-start | bytes 772
  8.4 0.7 %copy-start.2 = (bf16[48,2880]{1,0:T(8,128)(2,1)}, bf16[48,2880]{1,0:T(8,128)(2,1)S(1)}, u32[]{:S(2)}) copy-start(bf16[48,2880]{1,0:T(8,128)(2,1)S(1)} %get-tuple-element.32.got0_ref) | copy-start | bytes 829444
  9.1 17.0 %collective-permute-start.1 = (bf16[48,2880]{1,0:T(8,128)(2,1)}, bf16[48,2880]{1,0:T(8,128)(2,1)S(1)}, u32[]{:S(2)}, u32[]{:S(2)}) collective-permute-start(bf16[48,2880]{1,0:T(8,128)(2,1)} %get-tuple-element.27), channel_id=1, source_target_pairs={{0,64},{64,0},{128,192},{192,128},{1,65},{65,1},{129,193},{193,129... | collective-permute-start | bytes 829448 | tf_op jit(solution)/shard_map/ppermute | solution.py:415
  10.6 16.2 %collective-permute-start.2 = (bf16[48,2880]{1,0:T(8,128)(2,1)S(1)}, bf16[48,2880]{1,0:T(8,128)(2,1)S(1)}, u32[]{:S(2)}, u32[]{:S(2)}) collective-permute-start(bf16[48,2880]{1,0:T(8,128)(2,1)S(1)} %get-tuple-element.28), channel_id=1, source_target_pairs={{0,128},{64,192},{128,0},{192,64},{1,129},{65,193},{129,1},{193,65... | collective-permute-start | bytes 829448 | tf_op jit(solution)/shard_map/ppermute | solution.py:415
  13.3 16.2 %collective-permute-start.3 = (bf16[48,2880]{1,0:T(8,128)(2,1)S(1)}, bf16[48,2880]{1,0:T(8,128)(2,1)S(1)}, u32[]{:S(2)}, u32[]{:S(2)}) collective-permute-start(bf16[48,2880]{1,0:T(8,128)(2,1)S(1)} %get-tuple-element.29), channel_id=1, source_target_pairs={{0,192},{64,128},{128,64},{192,0},{1,193},{65,129},{129,65},{193,1... | collective-permute-start | bytes 829448 | tf_op jit(solution)/shard_map/ppermute | solution.py:415
  13.8 27.8 %all-to-all-start = ((bf16[64,24,128]{2,1,0:T(8,128)(2,1)}), bf16[64,24,128]{2,1,0:T(8,128)(2,1)S(1)}, u32[]{:S(2)}, u32[]{:S(2)}) async-start(bf16[64,24,128]{2,1,0:T(8,128)(2,1)} %get-tuple-element.25), calls=%async_computation | async-start | bytes 786432 | tf_op jit(solution)/shard_map/all_to_all | solution.py:416
  29.5 5.5 %collective-permute-start.4 = (bf16[2,8,720]{2,1,0:T(8,128)(2,1)S(1)}, bf16[2,8,720]{2,1,0:T(8,128)(2,1)S(1)}, u32[]{:S(2)}, u32[]{:S(2)}) collective-permute-start(bf16[2,8,720]{2,1,0:T(8,128)(2,1)S(1)} %pad_maximum_fusion.near_ref), channel_id=1, source_target_pairs={{0,2},{2,0},{1,3},{3,1},{4,6},{6,4},{5,7},{7,5},{8,10},{10,8},{9,1... | collective-permute-start | bytes 69128 | tf_op jit(solution)/shard_map/ppermute | solution.py:420
  41.6 11.2 %collective-permute-start.5 = (bf16[64,24,128]{2,1,0:T(8,128)(2,1)S(1)}, bf16[64,24,128]{2,1,0:T(8,128)(2,1)S(1)}, u32[]{:S(2)}, u32[]{:S(2)}) collective-permute-start(bf16[64,24,128]{2,1,0:T(8,128)(2,1)S(1)} %all-to-all-done.own_ref), channel_id=1, source_target_pairs={{0,2},{2,0},{1,3},{3,1},{4,6},{6,4},{5,7},{7,5},{8,10},{10,8},{9,1... | collective-permute-start | bytes 1179656 | tf_op jit(solution)/shard_map/ppermute | solution.py:426
  44.6 17.2 %all-to-all-start.1 = ((bf16[16,4,2880]{2,1,0:T(4,128)(2,1)}), bf16[16,4,2880]{2,1,0:T(4,128)(2,1)S(1)}, u32[]{:S(2)}, u32[]{:S(2)}) async-start(bf16[16,4,2880]{2,1,0:T(4,128)(2,1)} %merge_side.1), calls=%async_computation.1 | async-start | bytes 753664 | tf_op jit(solution)/shard_map/all_to_all | solution.py:428
  51.8 1.7 %collective-permute-start.6 = (bf16[64,24,128]{2,1,0:T(8,128)(2,1)S(1)}, bf16[64,24,128]{2,1,0:T(8,128)(2,1)S(1)}, u32[]{:S(2)}, u32[]{:S(2)}) collective-permute-start(bf16[64,24,128]{2,1,0:T(8,128)(2,1)S(1)} %all-to-all-done.own_ref), channel_id=1, source_target_pairs={{0,1},{1,0},{2,3},{3,2},{4,5},{5,4},{6,7},{7,6},{8,9},{9,8},{10,11... | collective-permute-start | bytes 1179656 | tf_op jit(solution)/shard_map/ppermute | solution.py:425
  52.9 1.7 %collective-permute-start.7 = (bf16[64,24,128]{2,1,0:T(8,128)(2,1)S(1)}, bf16[64,24,128]{2,1,0:T(8,128)(2,1)S(1)}, u32[]{:S(2)}, u32[]{:S(2)}) collective-permute-start(bf16[64,24,128]{2,1,0:T(8,128)(2,1)S(1)} %collective-permute-done.5.across_ref), channel_id=1, source_target_pairs={{0,1},{1,0},{2,3},{3,2},{4,5},{5,4},{6,7},{7,6},{8,9},{9,8},{10,11... | collective-permute-start | bytes 1179656 | tf_op jit(solution)/shard_map/ppermute | solution.py:427

commit v9 on v8

--- a/solution.py
+++ b/solution.py
@@ -121,23 +121,33 @@
 GROUP = 16
 
 
-def assemble_kernel(own_ref, across_ref, core_ref, both_ref, out_ref, held_ref):
+def assemble_kernel(own_ref, across_ref, core_ref, both_ref, out_hbm, held_ref, out_ref, sems):
     low = iota((HALF, 128), 1) < ROWS
     half = lax.axis_index("yh")
     core = lax.axis_index("c")
-    for i in range(GROUP):
-        here = (own_ref[i].astype(F32), core_ref[i].astype(F32))
-        there = (across_ref[i].astype(F32), both_ref[i].astype(F32))
-        for h in range(2):
-            mine, other = (jnp.where(half == h, a, b) for a, b in zip(here, there))
-            first = jnp.where(core == 0, mine, other)
-            second = jnp.where(core == 0, other, mine)
-            upper = jnp.where(low, first, pltpu.roll(second, ROWS, 1))
-            lower = jnp.where(low, pltpu.roll(first, ROWS, 1), second)
-            lanes = slice(128 * h, 128 * h + 128)
-            held_ref[COLS * i : COLS * i + HALF, lanes] = upper
-            held_ref[COLS * i + HALF : COLS * (i + 1), lanes] = lower[: COLS - HALF]
-    out_ref[...] = held_ref[...].astype(BF)
+    rows = GROUP * COLS
+    copies = []
+    for g in range(SLOTS // GROUP):
+        for i in range(GROUP):
+            n = g * GROUP + i
+            here = (own_ref[n].astype(F32), core_ref[n].astype(F32))
+            there = (across_ref[n].astype(F32), both_ref[n].astype(F32))
+            for h in range(2):
+                mine, other = (jnp.where(half == h, a, b) for a, b in zip(here, there))
+                first = jnp.where(core == 0, mine, other)
+                second = jnp.where(core == 0, other, mine)
+                upper = jnp.where(low, first, pltpu.roll(second, ROWS, 1))
+                lower = jnp.where(low, pltpu.roll(first, ROWS, 1), second)
+                lanes = slice(128 * h, 128 * h + 128)
+                held_ref[COLS * i : COLS * i + HALF, lanes] = upper
+                held_ref[COLS * i + HALF : COLS * (i + 1), lanes] = lower[: COLS - HALF]
+        part = pl.ds(g * rows, rows)
+        out_ref[part, :] = held_ref[...].astype(BF)
+        copy = pltpu.make_async_copy(out_ref.at[part], out_hbm.at[part], sems.at[g])
+        copy.start()
+        copies.append(copy)
+    for copy in copies:
+        copy.wait()
 
 
 def assemble(own, across, core, both):
@@ -145,11 +155,14 @@
     return pl.pallas_call(
         assemble_kernel,
         name="assemble",
-        grid=(SLOTS // GROUP,),
         out_shape=jax.ShapeDtypeStruct((D, 4 * ROWS), BF),
-        in_specs=[pl.BlockSpec((GROUP, HALF, 128), lambda g: (g, 0, 0))] * 4,
-        out_specs=pl.BlockSpec((rows, 4 * ROWS), lambda g: (g, 0)),
-        scratch_shapes=[VMEM((rows, 4 * ROWS), F32)],
+        in_specs=[pl.BlockSpec(memory_space=VMEM)] * 4,
+        out_specs=pl.BlockSpec(memory_space=pl.ANY),
+        scratch_shapes=[
+            VMEM((rows, 4 * ROWS), F32),
+            VMEM((D, 4 * ROWS), BF),
+            pltpu.SemaphoreType.DMA((SLOTS // GROUP,)),
+        ],
         compiler_params=params(24),
         cost_estimate=pl.CostEstimate(flops=10**9, bytes_accessed=4 * 10**6, transcendentals=0),
     )(own, across, core, both)
@@ -409,13 +422,13 @@
         resident_gate_up[0],
         resident_down[0].T,
     )
-    chunks, router_core, *terms = lax.optimization_barrier((chunks, router_core, *terms))
-    got = [in_hbm(terms[0])]
+    chunks, router_core, *terms[1:] = lax.optimization_barrier((chunks, router_core, *terms[1:]))
+    got = [terms[0]]
     for d in range(1, SIDE):
         got.append(lax.ppermute(terms[d], "x", [(x, x ^ d) for x in range(SIDE)]))
     chunks = lax.all_to_all(chunks, FSDP, split_axis=0, concat_axis=0, tiled=True)
 
-    router_core, *_ = lax.optimization_barrier((router_core, *got[1:]))
+    router_core, _ = lax.optimization_barrier((router_core, got[2]))
     near = jnp.stack([router_rows, router_core])
     far = lax.ppermute(near, "yh", swap)
     table = weigh(placement, chosen, near, far, normed)

time: 62.7 us -> 59.6 us (0.951)
  Pallas kernels: 13.8 us -> 12 us
  local copies, waits for them, and re-layouts: 0.72 us -> 0.01 us
    all_to_all x1, waiting for transfers between devices: 3.26 us -> 0.67 us  [on_device(): lax.all_to_all(chunks, FSDP, split_axis=0, concat_axis=0, tiled=True)]
    ppermute x3, starting transfers between devices: 4.7 us -> 6.84 us  [on_device(): got.append(lax.ppermute(terms[d], 'x', [(x, x ^ d) for x in range(SIDE)]))]
    all_to_all x1, starting transfers between devices: 12.3 us -> 10.7 us  [on_device(): lax.all_to_all(chunks, FSDP, split_axis=0, concat_axis=0, tiled=True)]
    ppermute x1, waiting for transfers between devices: 1.05 us -> 2.04 us  [on_device(): across = lax.ppermute(chunks, 'yh', swap)]
    all_to_all x1, waiting for transfers between devices: 4.87 us -> 5.82 us  [on_device(): lax.all_to_all(terms, ('yl', 'z'), split_axis=0, concat_axis=0, tiled=True)]
    pallas_call x1, Pallas kernels: 2.1 us -> 1.14 us  [merge_side(): pl.pallas_call(merge_kernel, name='merge_side', out_shape=jax.ShapeDtypeS...]
    unnamed x8 -> x6, local copies, waits for them, and re-layouts: 0.72 us -> 0.01 us
    all_to_all x1, starting transfers between devices: 7.26 us -> 6.56 us  [on_device(): lax.all_to_all(terms, ('yl', 'z'), split_axis=0, concat_axis=0, tiled=True)]
  transfers between devices with their start and end apart: 10 -> 10, of which waited for: 8 -> 7; matrix products, arithmetic and copies ran while one was open for 0% -> 0% of each run, Pallas kernels for 21% -> 19%
where the time goes in v9:
time: 59.6 us; the launch traced here: 59.4 us
  starting transfers between devices  30.1 us (51%)
  waiting for transfers between devices  16.6 us (28%)
  Pallas kernels  12 us (20%)
  between operations  0.72 us (1%)
    all_to_all x1, starting transfers between devices, on_device(): lax.all_to_all(chunks, FSDP, split_axis=0, concat_axis=0, tiled=True)  10.7 us
    pallas_call x1, Pallas kernels, prepare(): pl.pallas_call(prepare_kernel, name='prepare', out_shape=(jax.ShapeDtypeS...  7.23 us
    ppermute x3, starting transfers between devices, on_device(): got.append(lax.ppermute(terms[d], 'x', [(x, x ^ d) for x in range(SIDE)]))  6.84 us
    all_to_all x1, starting transfers between devices, on_device(): lax.all_to_all(terms, ('yl', 'z'), split_axis=0, concat_axis=0, tiled=True)  6.56 us
    all_to_all x1, waiting for transfers between devices, on_device(): lax.all_to_all(terms, ('yl', 'z'), split_axis=0, concat_axis=0, tiled=True)  5.82 us
    ppermute x3, waiting for transfers between devices, on_device(): got.append(lax.ppermute(terms[d], 'x', [(x, x ^ d) for x in range(SIDE)]))  3.81 us
    ppermute x1, starting transfers between devices, on_device(): far = lax.ppermute(near, 'yh', swap)  2.99 us
    ppermute x1, starting transfers between devices, on_device(): across = lax.ppermute(chunks, 'yh', swap)  2.9 us
  transfers between devices with their start and end apart: 10, of which 7 were waited for; matrix products, arithmetic and copies ran while one was open for 0% of the time, Pallas kernels for 19%

profile of v9, /device:TPU:32, one launch (start us, length us, event | category | flops | bytes accessed | tf_op | source)
XLA Modules:
  0.0 59.4 jit_solution(14742059437614613720)
XLA Ops:
  0.6 0.1 collective-permute-start
  0.7 0.0 copy-start.2
  0.7 0.0 copy-start
  0.8 0.0 copy-start.1
  0.8 7.2 %prepare.1 = (bf16[64,24,128]{2,1,0:T(8,128)(2,1)}, bf16[48,2880]{1,0:T(8,128)(2,1)S(1)}, bf16[48,2880]{1,0:T(8,128)(2,1)S(1)}, bf16[48,2880]{1,0:T(8,128)(2,1)S...) custom-call(s32[64]{0:T(128)} %place_ref.1, f32[45,64,64]{2,1,0:T(8,128)} %bitcast.25, ...), custom_call_target="tpu_custom_call" | custom-call | flops 8000000000 | bytes 10000000 | tf_op jit(solution)/shard_map/prepare/pallas_call | solution.py:290
  8.0 0.0 collective-permute-done
  8.0 3.1 %collective-permute-start.1 = (bf16[48,2880]{1,0:T(8,128)(2,1)S(1)}, bf16[48,2880]{1,0:T(8,128)(2,1)S(1)}, u32[]{:S(2)}, u32[]{:S(2)}) collective-permute-start(bf16[48,2880]{1,0:T(8,128)(2,1)S(1)} %get-tuple-element.25), channel_id=1, source_target_pairs={{0,128},{64,192},{128,0},{192,64},{1,129},{65,193},{129,1},{193,65... | collective-permute-start | bytes 829448 | tf_op jit(solution)/shard_map/ppermute | solution.py:428
  11.1 10.7 %all-to-all-start = ((bf16[64,24,128]{2,1,0:T(8,128)(2,1)}), bf16[64,24,128]{2,1,0:T(8,128)(2,1)S(1)}, u32[]{:S(2)}, u32[]{:S(2)}) async-start(bf16[64,24,128]{2,1,0:T(8,128)(2,1)} %get-tuple-element.23), calls=%async_computation | async-start | bytes 786432 | tf_op jit(solution)/shard_map/all_to_all | solution.py:429
  21.9 1.6 %collective-permute-start.3 = (bf16[48,2880]{1,0:T(8,128)(2,1)S(1)}, bf16[48,2880]{1,0:T(8,128)(2,1)S(1)}, u32[]{:S(2)}, u32[]{:S(2)}) collective-permute-start(bf16[48,2880]{1,0:T(8,128)(2,1)S(1)} %get-tuple-element.29), channel_id=1, source_target_pairs={{0,64},{64,0},{128,192},{192,128},{1,65},{65,1},{129,193},{193,129... | collective-permute-start | bytes 829448 | tf_op jit(solution)/shard_map/ppermute | solution.py:428
  23.4 2.2 %collective-permute-start.4 = (bf16[48,2880]{1,0:T(8,128)(2,1)S(1)}, bf16[48,2880]{1,0:T(8,128)(2,1)S(1)}, u32[]{:S(2)}, u32[]{:S(2)}) collective-permute-start(bf16[48,2880]{1,0:T(8,128)(2,1)S(1)} %get-tuple-element.30), channel_id=1, source_target_pairs={{0,192},{64,128},{128,64},{192,0},{1,193},{65,129},{129,65},{193,1... | collective-permute-start | bytes 829448 | tf_op jit(solution)/shard_map/ppermute | solution.py:428
  25.6 0.0 collective-permute-done.1.got2_ref
  25.6 0.0 copy-done.2
  25.6 3.0 %collective-permute-start.2 = (bf16[2,8,720]{2,1,0:T(8,128)(2,1)S(1)}, bf16[2,8,720]{2,1,0:T(8,128)(2,1)S(1)}, u32[]{:S(2)}, u32[]{:S(2)}) collective-permute-start(bf16[2,8,720]{2,1,0:T(8,128)(2,1)S(1)} %pad_maximum_fusion.near_ref), channel_id=1, source_target_pairs={{0,2},{2,0},{1,3},{3,1},{4,6},{6,4},{5,7},{7,5},{8,10},{10,8},{9,1... | collective-permute-start | bytes 69128 | tf_op jit(solution)/shard_map/ppermute | solution.py:433
  28.6 2.5 %collective-permute-done.2.far_ref = bf16[2,8,720]{2,1,0:T(8,128)(2,1)S(1)} collective-permute-done((bf16[2,8,720]{2,1,0:T(8,128)(2,1)S(1)}, bf16[2,8,720]{2,1,0:T(8,128)(2,1)S(1)}, u32[]{:S(2)}, u32[]{:S(2)}) %collective-permute-start.2) | collective-permute-done | bytes 23072 | tf_op jit(solution)/shard_map/ppermute | solution.py:433
  31.1 0.0 copy-done
  31.1 0.0 copy-done.1
  31.1 1.2 %weigh.1.table_ref = bf16[128,192]{1,0:T(8,128)(2,1)S(1)} custom-call(s32[64]{0:T(128)S(1)} %copy-done.1, s32[4,256]{1,0:T(4,128)S(1)} %bitcast.19, bf16[2,8,720]{2,1,0:T(8,128)(2,1)S(1)} %pad_maximum_fusion.near_ref, bf16[2,8,720]{2,1,0:T(8,128)(2,1)S(1)} %collective-permute-done.2.far_ref, bf16[2880,256]{1,0:T(8,128)(2,1)S(1)} %get-tuple-element.27.normed_ref), custom_call_target="tpu_custom_call" | custom-call | flops 1 | bytes 1 | tf_op jit(solution)/shard_map/weigh/pallas_call | solution.py:352
  32.3 1.5 %collective-permute-done.3.got1_ref = bf16[48,2880]{1,0:T(8,128)(2,1)S(1)} collective-permute-done((bf16[48,2880]{1,0:T(8,128)(2,1)S(1)}, bf16[48,2880]{1,0:T(8,128)(2,1)S(1)}, u32[]{:S(2)}, u32[]{:S(2)}) %collective-permute-start.3) | collective-permute-done | bytes 276512 | tf_op jit(solution)/shard_map/ppermute | solution.py:428
  33.7 2.4 %collective-permute-done.4.got3_ref = bf16[48,2880]{1,0:T(8,128)(2,1)S(1)} collective-permute-done((bf16[48,2880]{1,0:T(8,128)(2,1)S(1)}, bf16[48,2880]{1,0:T(8,128)(2,1)S(1)}, u32[]{:S(2)}, u32[]{:S(2)}) %collective-permute-start.4) | collective-permute-done | bytes 276512 | tf_op jit(solution)/shard_map/ppermute | solution.py:428
  36.1 1.1 %merge_side.1 = bf16[16,4,2880]{2,1,0:T(4,128)(2,1)} custom-call(bf16[128,192]{1,0:T(8,128)(2,1)S(1)} %weigh.1.table_ref, bf16[48,2880]{1,0:T(8,128)(2,1)S(1)} %get-tuple-element.28.got0_ref, bf16[48,2880]{1,0:T(8,128)(2,1)S(1)} %collective-permute-done.3.got1_ref, bf16[48,2880]{1,0:T(8,128)(2,1)S(1)} %collective-permute-done.1.got2_ref, ...), custom_call_target="tpu_custom_call" | custom-call | flops 4000000000 | bytes 1 | tf_op jit(solution)/shard_map/merge_side/pallas_call | solution.py:378
  37.2 0.7 %all-to-all-done.own_ref = bf16[64,24,128]{2,1,0:T(8,128)(2,1)S(1)} async-done(((bf16[64,24,128]{2,1,0:T(8,128)(2,1)}), bf16[64,24,128]{2,1,0:T(8,128)(2,1)S(1)}, u32[]{:S(2)}, u32[]{:S(2)}) %all-to-all-start) | async-done | bytes 393248 | tf_op jit(solution)/shard_map/all_to_all | solution.py:429
  37.9 2.9 %collective-permute-start.5 = (bf16[64,24,128]{2,1,0:T(8,128)(2,1)S(1)}, bf16[64,24,128]{2,1,0:T(8,128)(2,1)S(1)}, u32[]{:S(2)}, u32[]{:S(2)}) collective-permute-start(bf16[64,24,128]{2,1,0:T(8,128)(2,1)S(1)} %all-to-all-done.own_ref), channel_id=1, source_target_pairs={{0,2},{2,0},{1,3},{3,1},{4,6},{6,4},{5,7},{7,5},{8,10},{10,8},{9,1... | collective-permute-start | bytes 1179656 | tf_op jit(solution)/shard_map/ppermute | solution.py:439
  40.8 6.6 %all-to-all-start.1 = ((bf16[16,4,2880]{2,1,0:T(4,128)(2,1)}), bf16[16,4,2880]{2,1,0:T(4,128)(2,1)S(1)}, u32[]{:S(2)}, u32[]{:S(2)}) async-start(bf16[16,4,2880]{2,1,0:T(4,128)(2,1)} %merge_side.1), calls=%async_computation.1 | async-start | bytes 753664 | tf_op jit(solution)/shard_map/all_to_all | solution.py:441
  47.3 0.0 collective-permute-start.6
  47.4 2.0 %collective-permute-done.5.across_ref = bf16[64,24,128]{2,1,0:T(8,128)(2,1)S(1)} collective-permute-done((bf16[64,24,128]{2,1,0:T(8,128)(2,1)S(1)}, bf16[64,24,128]{2,1,0:T(8,128)(2,1)S(1)}, u32[]{:S(2)}, u32[]{:S(2)}) %collective-permute-start.5) | collective-permute-done | bytes 393248 | tf_op jit(solution)/shard_map/ppermute | solution.py:439
  49.4 0.0 collective-permute-start.7
  49.4 0.0 collective-permute-done.6.core_ref
  49.4 1.7 %collective-permute-done.7.both_ref = bf16[64,24,128]{2,1,0:T(8,128)(2,1)S(1)} collective-permute-done((bf16[64,24,128]{2,1,0:T(8,128)(2,1)S(1)}, bf16[64,24,128]{2,1,0:T(8,128)(2,1)S(1)}, u32[]{:S(2)}, u32[]{:S(2)}) %collective-permute-start.7) | collective-permute-done | bytes 393248 | tf_op jit(solution)/shard_map/ppermute | solution.py:440
  51.1 1.8 %assemble.1 = bf16[2880,256]{1,0:T(8,128)(2,1)} custom-call(bf16[64,24,128]{2,1,0:T(8,128)(2,1)S(1)} %all-to-all-done.own_ref, bf16[64,24,128]{2,1,0:T(8,128)(2,1)S(1)} %collective-permute-done.5.across_ref, bf16[64,24,128]{2,1,0:T(8,128)(2,1)S(1)} %collective-permute-done.6.core_ref, bf16[64,24,128]{2,1,0:T(8,128)(2,1)S(1)} %collective-permute-done.7.both_ref), custom_call_target="tpu_custom_call" | custom-call | flops 1000000000 | bytes 4000000 | tf_op jit(solution)/shard_map/assemble/pallas_call | solution.py:155
  52.9 5.8 %all-to-all-done.1.got_ref = bf16[16,4,2880]{2,1,0:T(4,128)(2,1)S(1)} async-done(((bf16[16,4,2880]{2,1,0:T(4,128)(2,1)}), bf16[16,4,2880]{2,1,0:T(4,128)(2,1)S(1)}, u32[]{:S(2)}, u32[]{:S(2)}) %all-to-all-start.1) | async-done | bytes 368672 | tf_op jit(solution)/shard_map/all_to_all | solution.py:441
  58.7 0.7 %finish.1 = bf16[4,2880]{1,0:T(4,128)(2,1)} custom-call(bf16[16,4,2880]{2,1,0:T(4,128)(2,1)S(1)} %all-to-all-done.1.got_ref, f32[4,2880]{1,0:T(4,128)S(1)} %get-tuple-element.35.rows_ref), custom_call_target="tpu_custom_call" | custom-call | flops 1000000 | bytes 1000000 | tf_op jit(solution)/shard_map/finish/pallas_call | solution.py:398
  (1 shorter events, 0.0 us)
Async XLA Ops:
  0.6 7.4 %collective-permute-start = (bf16[8,720]{1,0:T(8,128)(2,1)}, bf16[8,720]{1,0:T(8,128)(2,1)S(1)}, u32[]{:S(2)}, u32[]{:S(2)}) collective-permute-start(bf16[8,720]{1,0:T(8,128)(2,1)} %bitcast.21), channel_id=1, source_target_pairs={{0,1},{1,0},{2,3},{3,2},{4,5},{5,4},{6,7},{7,6},{8,9},{9,8},{10,11... | collective-permute-start | bytes 34568 | tf_op jit(solution)/shard_map/ppermute | solution.py:414
  0.7 24.8 %copy-start.2 = (bf16[720,8]{0,1:T(8,128)(2,1)S(1)}, bf16[720,8]{0,1:T(8,128)(2,1)}, u32[]{:S(2)}) copy-start(bf16[720,8]{0,1:T(8,128)(2,1)} %param.15) | copy-start | bytes 34564
  0.7 30.3 %copy-start = (s32[1,256,4]{1,2,0:T(4,128)S(1)}, s32[1,256,4]{1,2,0:T(4,128)}, u32[]{:S(2)}) copy-start(s32[1,256,4]{1,2,0:T(4,128)} %param.13) | copy-start | bytes 12292
  0.8 30.3 %copy-start.1 = (s32[64]{0:T(128)S(1)}, s32[64]{0:T(128)}, u32[]{:S(2)}) copy-start(s32[64]{0:T(128)} %place_ref.1) | copy-start | bytes 772
  8.0 17.6 %collective-permute-start.1 = (bf16[48,2880]{1,0:T(8,128)(2,1)S(1)}, bf16[48,2880]{1,0:T(8,128)(2,1)S(1)}, u32[]{:S(2)}, u32[]{:S(2)}) collective-permute-start(bf16[48,2880]{1,0:T(8,128)(2,1)S(1)} %get-tuple-element.25), channel_id=1, source_target_pairs={{0,128},{64,192},{128,0},{192,64},{1,129},{65,193},{129,1},{193,65... | collective-permute-start | bytes 829448 | tf_op jit(solution)/shard_map/ppermute | solution.py:428
  11.1 26.8 %all-to-all-start = ((bf16[64,24,128]{2,1,0:T(8,128)(2,1)}), bf16[64,24,128]{2,1,0:T(8,128)(2,1)S(1)}, u32[]{:S(2)}, u32[]{:S(2)}) async-start(bf16[64,24,128]{2,1,0:T(8,128)(2,1)} %get-tuple-element.23), calls=%async_computation | async-start | bytes 786432 | tf_op jit(solution)/shard_map/all_to_all | solution.py:429
  21.9 11.9 %collective-permute-start.3 = (bf16[48,2880]{1,0:T(8,128)(2,1)S(1)}, bf16[48,2880]{1,0:T(8,128)(2,1)S(1)}, u32[]{:S(2)}, u32[]{:S(2)}) collective-permute-start(bf16[48,2880]{1,0:T(8,128)(2,1)S(1)} %get-tuple-element.29), channel_id=1, source_target_pairs={{0,64},{64,0},{128,192},{192,128},{1,65},{65,1},{129,193},{193,129... | collective-permute-start | bytes 829448 | tf_op jit(solution)/shard_map/ppermute | solution.py:428
  23.4 12.7 %collective-permute-start.4 = (bf16[48,2880]{1,0:T(8,128)(2,1)S(1)}, bf16[48,2880]{1,0:T(8,128)(2,1)S(1)}, u32[]{:S(2)}, u32[]{:S(2)}) collective-permute-start(bf16[48,2880]{1,0:T(8,128)(2,1)S(1)} %get-tuple-element.30), channel_id=1, source_target_pairs={{0,192},{64,128},{128,64},{192,0},{1,193},{65,129},{129,65},{193,1... | collective-permute-start | bytes 829448 | tf_op jit(solution)/shard_map/ppermute | solution.py:428
  25.6 5.5 %collective-permute-start.2 = (bf16[2,8,720]{2,1,0:T(8,128)(2,1)S(1)}, bf16[2,8,720]{2,1,0:T(8,128)(2,1)S(1)}, u32[]{:S(2)}, u32[]{:S(2)}) collective-permute-start(bf16[2,8,720]{2,1,0:T(8,128)(2,1)S(1)} %pad_maximum_fusion.near_ref), channel_id=1, source_target_pairs={{0,2},{2,0},{1,3},{3,1},{4,6},{6,4},{5,7},{7,5},{8,10},{10,8},{9,1... | collective-permute-start | bytes 69128 | tf_op jit(solution)/shard_map/ppermute | solution.py:433
  37.9 11.5 %collective-permute-start.5 = (bf16[64,24,128]{2,1,0:T(8,128)(2,1)S(1)}, bf16[64,24,128]{2,1,0:T(8,128)(2,1)S(1)}, u32[]{:S(2)}, u32[]{:S(2)}) collective-permute-start(bf16[64,24,128]{2,1,0:T(8,128)(2,1)S(1)} %all-to-all-done.own_ref), channel_id=1, source_target_pairs={{0,2},{2,0},{1,3},{3,1},{4,6},{6,4},{5,7},{7,5},{8,10},{10,8},{9,1... | collective-permute-start | bytes 1179656 | tf_op jit(solution)/shard_map/ppermute | solution.py:439
  40.8 17.9 %all-to-all-start.1 = ((bf16[16,4,2880]{2,1,0:T(4,128)(2,1)}), bf16[16,4,2880]{2,1,0:T(4,128)(2,1)S(1)}, u32[]{:S(2)}, u32[]{:S(2)}) async-start(bf16[16,4,2880]{2,1,0:T(4,128)(2,1)} %merge_side.1), calls=%async_computation.1 | async-start | bytes 753664 | tf_op jit(solution)/shard_map/all_to_all | solution.py:441
  47.3 2.1 %collective-permute-start.6 = (bf16[64,24,128]{2,1,0:T(8,128)(2,1)S(1)}, bf16[64,24,128]{2,1,0:T(8,128)(2,1)S(1)}, u32[]{:S(2)}, u32[]{:S(2)}) collective-permute-start(bf16[64,24,128]{2,1,0:T(8,128)(2,1)S(1)} %all-to-all-done.own_ref), channel_id=1, source_target_pairs={{0,1},{1,0},{2,3},{3,2},{4,5},{5,4},{6,7},{7,6},{8,9},{9,8},{10,11... | collective-permute-start | bytes 1179656 | tf_op jit(solution)/shard_map/ppermute | solution.py:438
  49.4 1.7 %collective-permute-start.7 = (bf16[64,24,128]{2,1,0:T(8,128)(2,1)S(1)}, bf16[64,24,128]{2,1,0:T(8,128)(2,1)S(1)}, u32[]{:S(2)}, u32[]{:S(2)}) collective-permute-start(bf16[64,24,128]{2,1,0:T(8,128)(2,1)S(1)} %collective-permute-done.5.across_ref), channel_id=1, source_target_pairs={{0,1},{1,0},{2,3},{3,2},{4,5},{5,4},{6,7},{7,6},{8,9},{9,8},{10,11... | collective-permute-start | bytes 1179656 | tf_op jit(solution)/shard_map/ppermute | solution.py:440

commit v10 on v9

--- a/solution.py
+++ b/solution.py
@@ -64,6 +64,7 @@
 
 
 PAIRS = 12
+STRIDE = 72
 
 
 def round_blocks(values, spread):
@@ -115,7 +116,10 @@
         low = low.reshape(PAIRS * SLOTS, ROWS)
         high = high.reshape(PAIRS * SLOTS, ROWS)
         values = jnp.concatenate([low, high], axis=1)
-        held_ref[at * SLOTS : (at + PAIRS) * SLOTS, :] = round_blocks(values, spread)
+        decoded = round_blocks(values, spread)
+        for k in range(PAIRS):
+            start = (at + k) * STRIDE
+            held_ref[start : start + SLOTS, :] = decoded[k * SLOTS : (k + 1) * SLOTS]
 
 
 GROUP = 16
@@ -188,6 +192,21 @@
     return jnp.sum(jnp.where(iota((8, TOK), 0) == expert, table, 0.0), axis=0, keepdims=True)
 
 
+def norm_into(normed_ref, hidden_ref, gain_ref):
+    total = jnp.zeros((1, TOK), F32)
+    for n in range(PIECES):
+        part = hidden_ref[n * PIECE : (n + 1) * PIECE, :].astype(F32)
+        total = total + jnp.sum(part * part, axis=0, keepdims=True)
+    factor = lax.rsqrt(total * (1.0 / D) + 1e-05)
+    for at in range(0, D, 128):
+        size = min(128, D - at)
+        gain = gain_ref[at : at + size].astype(F32)
+        spread = jnp.transpose(jnp.broadcast_to(gain, (128, size)))
+        spread = jnp.concatenate([spread, spread], axis=1)
+        part = hidden_ref[at : at + size, :].astype(F32)
+        normed_ref[at : at + size, :] = (part * factor * spread).astype(BF)
+
+
 def prepare_kernel(
     place_hbm,
     master_hbm,
@@ -201,8 +220,6 @@
     out1_ref,
     out2_ref,
     out3_ref,
-    normed_ref,
-    rows_ref,
     place_ref,
     slot_ref,
     routes_ref,
@@ -212,6 +229,7 @@
     hidden_ref,
     gate_up_ref,
     down_ref,
+    normed_ref,
     sems,
 ):
     pieces = [pl.ds(n * PIECE, PIECE) for n in range(PIECES)]
@@ -230,7 +248,7 @@
     invert(place_ref, slot_ref)
 
     def deal(o, _):
-        chunks_ref[o] = held_ref[pl.ds(slot_ref[o], HALF, stride=SLOTS), :].astype(BF)
+        chunks_ref[o] = held_ref[pl.ds(slot_ref[o], HALF, stride=STRIDE), :].astype(BF)
         return 0
 
     lax.fori_loop(0, SLOTS, deal, 0, unroll=8)
@@ -247,22 +265,7 @@
         & (jnp.broadcast_to(my_turn, (PACKED, TOK)) == (packed % CAP).astype(F32))
     ).astype(F32).astype(BF)
 
-    total = jnp.zeros((1, TOK), F32)
-    for n in range(PIECES):
-        part = hidden_ref[n * PIECE : (n + 1) * PIECE, :].astype(F32)
-        total = total + jnp.sum(part * part, axis=0, keepdims=True)
-    factor = lax.rsqrt(total * (1.0 / D) + 1e-05)
-    ones = jnp.ones((128, TOK), BF)
-    for at in range(0, D, 128):
-        size = min(128, D - at)
-        gain = gain_ref[at : at + size].astype(F32)
-        diagonal = jnp.where(
-            iota((size, size), 0) == iota((size, size), 1), jnp.broadcast_to(gain, (size, size)), 0.0
-        ).astype(BF)
-        spread = nn(diagonal, ones[:size])
-        part = hidden_ref[at : at + size, :].astype(F32)
-        normed_ref[at : at + size, :] = (part * factor * spread).astype(BF)
-
+    norm_into(normed_ref, hidden_ref, gain_ref)
     projected = jnp.zeros((TOK, 2 * HID), F32)
     for n in range(PIECES):
         part = slice(n * PIECE, (n + 1) * PIECE)
@@ -277,11 +280,6 @@
         for d, out_ref in enumerate((out0_ref, out1_ref, out2_ref, out3_ref)):
             out_ref[:, at : at + size] = terms[d * SIDE_ROWS : (d + 1) * SIDE_ROWS]
 
-    own = (iota((8, TOK), 1) == iota((8, TOK), 0) + owner * 4).astype(F32).astype(BF)
-    for at in range(0, D, 640):
-        size = min(640, D - at)
-        rows_ref[:, at : at + size] = nt(own, hidden_ref[at : at + size, :])[:4]
-
 
 def prepare(placement, master, hidden, routes, gain, gate_up, down):
     whole = pl.BlockSpec(memory_space=VMEM)
@@ -291,20 +289,20 @@
         prepare_kernel,
         name="prepare",
         out_shape=(jax.ShapeDtypeStruct((SLOTS, HALF, 128), BF),)
-        + (out,) * 4
-        + (jax.ShapeDtypeStruct((D, TOK), BF), jax.ShapeDtypeStruct((4, D), F32)),
+        + (out,) * 4,
         in_specs=[apart] * 7,
-        out_specs=(whole,) * 7,
+        out_specs=(whole,) * 5,
         scratch_shapes=[
             pltpu.SMEM((SLOTS,), jnp.int32),
             pltpu.SMEM((SLOTS,), jnp.int32),
             VMEM((4, TOK), jnp.int32),
             VMEM((D,), BF),
             VMEM((COLS, SLOTS, ROWS), F32),
-            VMEM((HALF * SLOTS, 128), F32),
+            VMEM((HALF * STRIDE, 128), F32),
             VMEM((D, TOK), BF),
             VMEM((D, 2 * HID), BF),
             VMEM((D, HID), BF),
+            VMEM((D, TOK), BF),
             pltpu.SemaphoreType.DMA((2 * HALF // PAIRS + 3 + 3 * PIECES,)),
         ],
         compiler_params=params(32),
@@ -315,12 +313,29 @@
 
 
 def weigh_kernel(
-    place_ref, routes_ref, near_ref, far_ref, normed_ref, out_ref, slot_ref, held_ref
+    place_ref,
+    routes_ref,
+    near_ref,
+    far_ref,
+    hidden_ref,
+    gain_ref,
+    out_ref,
+    rows_ref,
+    slot_ref,
+    held_ref,
+    normed_ref,
 ):
     invert(place_ref, slot_ref)
     side = lax.axis_index("x")
     inner = lax.axis_index("yl") * DEPTH + lax.axis_index("z")
 
+    owner = side * INNER + inner
+    own = (iota((8, TOK), 1) == iota((8, TOK), 0) + owner * 4).astype(F32).astype(BF)
+    for at in range(0, D, 640):
+        size = min(640, D - at)
+        rows_ref[:, at : at + size] = nt(own, hidden_ref[at : at + size, :])[:4]
+
+    norm_into(normed_ref, hidden_ref, gain_ref)
     rep = lax.axis_index("yh") * 2 + lax.axis_index("c")
     logits = jnp.zeros((8, TOK), F32)
     for d in range(4):
@@ -348,17 +363,24 @@
     out_ref[local:, :] = (table - upper.astype(F32)).astype(BF)
 
 
-def weigh(placement, routes, near, far, normed):
+def weigh(placement, routes, near, far, hidden, gain):
     return pl.pallas_call(
         weigh_kernel,
         name="weigh",
-        out_shape=jax.ShapeDtypeStruct((8 * INNER, PACKED), BF),
-        in_specs=[pl.BlockSpec(memory_space=SMEM)] + [pl.BlockSpec(memory_space=VMEM)] * 4,
-        out_specs=pl.BlockSpec(memory_space=VMEM),
-        scratch_shapes=[pltpu.SMEM((SLOTS,), jnp.int32), VMEM((TOK, PACKED), F32)],
+        out_shape=(
+            jax.ShapeDtypeStruct((8 * INNER, PACKED), BF),
+            jax.ShapeDtypeStruct((4, D), F32),
+        ),
+        in_specs=[pl.BlockSpec(memory_space=SMEM)] + [pl.BlockSpec(memory_space=VMEM)] * 5,
+        out_specs=(pl.BlockSpec(memory_space=VMEM),) * 2,
+        scratch_shapes=[
+            pltpu.SMEM((SLOTS,), jnp.int32),
+            VMEM((TOK, PACKED), F32),
+            VMEM((D, TOK), BF),
+        ],
         compiler_params=params(16),
         cost_estimate=pl.CostEstimate(flops=1, bytes_accessed=1, transcendentals=0),
-    )(placement, routes, near, far, normed)
+    )(placement, routes, near, far, hidden, gain)
 
 
 def merge_kernel(table_ref, got0_ref, got1_ref, got2_ref, got3_ref, out_ref):
@@ -413,7 +435,7 @@
     router_rows = router.T
     router_core = lax.ppermute(router_rows, "c", swap)
     chosen = routes[0].T
-    chunks, *terms, normed, rows = prepare(
+    chunks, *terms = prepare(
         placement,
         jnp.transpose(master, (2, 0, 1)),
         hidden[0].T,
@@ -431,7 +453,7 @@
     router_core, _ = lax.optimization_barrier((router_core, got[2]))
     near = jnp.stack([router_rows, router_core])
     far = lax.ppermute(near, "yh", swap)
-    table = weigh(placement, chosen, near, far, normed)
+    table, rows = weigh(placement, chosen, near, far, hidden[0].T, norm_gain)
     terms = merge_side(table, got)
     chunks, terms = lax.optimization_barrier((chunks, terms))
 

time: 59.6 us -> 59 us (0.990)
  waiting for transfers between devices: 16.6 us -> 15.8 us
    pallas_call x1, Pallas kernels: 1.18 us -> 1.84 us  [weigh(): pl.pallas_call(weigh_kernel, name='weigh', out_shape=(jax.ShapeDtypeStruc...]
    pallas_call x1, Pallas kernels: 7.23 us -> 6.57 us  [prepare(): pl.pallas_call(prepare_kernel, name='prepare', out_shape=(jax.ShapeDtypeS...]
    ppermute x3, waiting for transfers between devices: 3.81 us -> 3.16 us  [on_device(): got.append(lax.ppermute(terms[d], 'x', [(x, x ^ d) for x in range(SIDE)]))]
where the time goes in v10:
time: 59 us; the launch traced here: 58.7 us
  starting transfers between devices  30.1 us (51%)
  waiting for transfers between devices  15.8 us (27%)
  Pallas kernels  12 us (20%)
  between operations  0.75 us (1%)
    all_to_all x1, starting transfers between devices, on_device(): lax.all_to_all(chunks, FSDP, split_axis=0, concat_axis=0, tiled=True)  10.7 us
    ppermute x3, starting transfers between devices, on_device(): got.append(lax.ppermute(terms[d], 'x', [(x, x ^ d) for x in range(SIDE)]))  6.84 us
    all_to_all x1, starting transfers between devices, on_device(): lax.all_to_all(terms, ('yl', 'z'), split_axis=0, concat_axis=0, tiled=True)  6.58 us
    pallas_call x1, Pallas kernels, prepare(): pl.pallas_call(prepare_kernel, name='prepare', out_shape=(jax.ShapeDtypeS...  6.57 us
    all_to_all x1, waiting for transfers between devices, on_device(): lax.all_to_all(terms, ('yl', 'z'), split_axis=0, concat_axis=0, tiled=True)  5.86 us
    ppermute x3, waiting for transfers between devices, on_device(): got.append(lax.ppermute(terms[d], 'x', [(x, x ^ d) for x in range(SIDE)]))  3.16 us
    ppermute x1, starting transfers between devices, on_device(): far = lax.ppermute(near, 'yh', swap)  2.99 us
    ppermute x1, starting transfers between devices, on_device(): across = lax.ppermute(chunks, 'yh', swap)  2.89 us
  transfers between devices with their start and end apart: 10, of which 7 were waited for; matrix products, arithmetic and copies ran while one was open for 0% of the time, Pallas kernels for 19%

profile of v10, /device:TPU:32, one launch (start us, length us, event | category | flops | bytes accessed | tf_op | source)
XLA Modules:
  0.0 58.7 jit_solution(5038813763240023162)
XLA Ops:
  0.6 0.1 collective-permute-start
  0.7 0.0 copy-start.4
  0.7 0.0 copy-start
  0.8 0.0 copy-start.1
  0.8 0.0 copy-start.2
  0.8 0.0 copy-start.3
  0.8 6.6 %prepare.1 = (bf16[64,24,128]{2,1,0:T(8,128)(2,1)}, bf16[48,2880]{1,0:T(8,128)(2,1)S(1)}, bf16[48,2880]{1,0:T(8,128)(2,1)S(1)}, bf16[48,2880]{1,0:T(8,128)(2,1)S(1)}, bf16[48,2880]{1,0:T(8,128)(2,1)S(1)}) custom-call(s32[64]{0:T(128)} %place_ref.1, f32[45,64,64]{2,1,0:T(8,128)} %bitcast.27, bf16[2880,256]{1,0:T(8,128)(2,1)} %bitcast.18, s32[4,256]{1,0:T(4,128)} %bitcast.20, ...), custom_call_target="tpu_custom_call" | custom-call | flops 8000000000 | bytes 10000000 | tf_op jit(solution)/shard_map/prepare/pallas_call | solution.py:288
  7.4 0.0 collective-permute-done
  7.4 3.1 %collective-permute-start.1 = (bf16[48,2880]{1,0:T(8,128)(2,1)S(1)}, bf16[48,2880]{1,0:T(8,128)(2,1)S(1)}, u32[]{:S(2)}, u32[]{:S(2)}) collective-permute-start(bf16[48,2880]{1,0:T(8,128)(2,1)S(1)} %get-tuple-element.25), channel_id=1, source_target_pairs={{0,128},{64,192},{128,0},{192,64},{1,129},{65,193},{129,1},{193,65... | collective-permute-start | bytes 829448 | tf_op jit(solution)/shard_map/ppermute | solution.py:450
  10.5 10.7 %all-to-all-start = ((bf16[64,24,128]{2,1,0:T(8,128)(2,1)}), bf16[64,24,128]{2,1,0:T(8,128)(2,1)S(1)}, u32[]{:S(2)}, u32[]{:S(2)}) async-start(bf16[64,24,128]{2,1,0:T(8,128)(2,1)} %get-tuple-element.23), calls=%async_computation | async-start | bytes 786432 | tf_op jit(solution)/shard_map/all_to_all | solution.py:451
  21.2 1.6 %collective-permute-start.3 = (bf16[48,2880]{1,0:T(8,128)(2,1)S(1)}, bf16[48,2880]{1,0:T(8,128)(2,1)S(1)}, u32[]{:S(2)}, u32[]{:S(2)}) collective-permute-start(bf16[48,2880]{1,0:T(8,128)(2,1)S(1)} %get-tuple-element.29), channel_id=1, source_target_pairs={{0,64},{64,0},{128,192},{192,128},{1,65},{65,1},{129,193},{193,129... | collective-permute-start | bytes 829448 | tf_op jit(solution)/shard_map/ppermute | solution.py:450
  22.8 2.2 %collective-permute-start.4 = (bf16[48,2880]{1,0:T(8,128)(2,1)S(1)}, bf16[48,2880]{1,0:T(8,128)(2,1)S(1)}, u32[]{:S(2)}, u32[]{:S(2)}) collective-permute-start(bf16[48,2880]{1,0:T(8,128)(2,1)S(1)} %get-tuple-element.30), channel_id=1, source_target_pairs={{0,192},{64,128},{128,64},{192,0},{1,193},{65,129},{129,65},{193,1... | collective-permute-start | bytes 829448 | tf_op jit(solution)/shard_map/ppermute | solution.py:450
  24.9 0.0 collective-permute-done.1.got2_ref
  25.0 0.0 copy-done.4
  25.0 3.0 %collective-permute-start.2 = (bf16[2,8,720]{2,1,0:T(8,128)(2,1)S(1)}, bf16[2,8,720]{2,1,0:T(8,128)(2,1)S(1)}, u32[]{:S(2)}, u32[]{:S(2)}) collective-permute-start(bf16[2,8,720]{2,1,0:T(8,128)(2,1)S(1)} %pad_maximum_fusion.near_ref), channel_id=1, source_target_pairs={{0,2},{2,0},{1,3},{3,1},{4,6},{6,4},{5,7},{7,5},{8,10},{10,8},{9,1... | collective-permute-start | bytes 69128 | tf_op jit(solution)/shard_map/ppermute | solution.py:455
  28.0 2.5 %collective-permute-done.2.far_ref = bf16[2,8,720]{2,1,0:T(8,128)(2,1)S(1)} collective-permute-done((bf16[2,8,720]{2,1,0:T(8,128)(2,1)S(1)}, bf16[2,8,720]{2,1,0:T(8,128)(2,1)S(1)}, u32[]{:S(2)}, u32[]{:S(2)}) %collective-permute-start.2) | collective-permute-done | bytes 23072 | tf_op jit(solution)/shard_map/ppermute | solution.py:455
  30.4 0.0 copy-done
  30.4 0.0 copy-done.1
  30.4 0.0 copy-done.2
  30.4 0.0 copy-done.3
  30.4 1.8 %weigh.1 = (bf16[128,192]{1,0:T(8,128)(2,1)S(1)}, f32[4,2880]{1,0:T(4,128)S(1)}) custom-call(s32[64]{0:T(128)S(1)} %copy-done.3, s32[4,256]{1,0:T(4,128)S(1)} %bitcast.21, bf16[2,8,720]{2,1,0:T(8,128)(2,1)S(1)} %pad_maximum_fusion.near_ref, bf16[2,8,720]{2,1,0:T(8,128)(2,1)S(1)} %collective-permute-done.2.far_ref, bf16[2880,256]{1,0:T(8,128)(2,1)S(1)} %bitcast.19, ...), custom_call_target="tpu_custom_call" | custom-call | flops 1 | bytes 1 | tf_op jit(solution)/shard_map/weigh/pallas_call | solution.py:367
  32.3 0.8 %collective-permute-done.3.got1_ref = bf16[48,2880]{1,0:T(8,128)(2,1)S(1)} collective-permute-done((bf16[48,2880]{1,0:T(8,128)(2,1)S(1)}, bf16[48,2880]{1,0:T(8,128)(2,1)S(1)}, u32[]{:S(2)}, u32[]{:S(2)}) %collective-permute-start.3) | collective-permute-done | bytes 276512 | tf_op jit(solution)/shard_map/ppermute | solution.py:450
  33.0 2.4 %collective-permute-done.4.got3_ref = bf16[48,2880]{1,0:T(8,128)(2,1)S(1)} collective-permute-done((bf16[48,2880]{1,0:T(8,128)(2,1)S(1)}, bf16[48,2880]{1,0:T(8,128)(2,1)S(1)}, u32[]{:S(2)}, u32[]{:S(2)}) %collective-permute-start.4) | collective-permute-done | bytes 276512 | tf_op jit(solution)/shard_map/ppermute | solution.py:450
  35.4 1.2 %merge_side.1 = bf16[16,4,2880]{2,1,0:T(4,128)(2,1)} custom-call(bf16[128,192]{1,0:T(8,128)(2,1)S(1)} %get-tuple-element.27.table_ref, bf16[48,2880]{1,0:T(8,128)(2,1)S(1)} %get-tuple-element.28.got0_ref, bf16[48,2880]{1,0:T(8,128)(2,1)S(1)} %collective-permute-done.3.got1_ref, bf16[48,2880]{1,0:T(8,128)(2,1)S(1)} %collective-permute-done.1.got2_ref, ...), custom_call_target="tpu_custom_call" | custom-call | flops 4000000000 | bytes 1 | tf_op jit(solution)/shard_map/merge_side/pallas_call | solution.py:400
  36.6 0.6 %all-to-all-done.own_ref = bf16[64,24,128]{2,1,0:T(8,128)(2,1)S(1)} async-done(((bf16[64,24,128]{2,1,0:T(8,128)(2,1)}), bf16[64,24,128]{2,1,0:T(8,128)(2,1)S(1)}, u32[]{:S(2)}, u32[]{:S(2)}) %all-to-all-start) | async-done | bytes 393248 | tf_op jit(solution)/shard_map/all_to_all | solution.py:451
  37.2 2.9 %collective-permute-start.5 = (bf16[64,24,128]{2,1,0:T(8,128)(2,1)S(1)}, bf16[64,24,128]{2,1,0:T(8,128)(2,1)S(1)}, u32[]{:S(2)}, u32[]{:S(2)}) collective-permute-start(bf16[64,24,128]{2,1,0:T(8,128)(2,1)S(1)} %all-to-all-done.own_ref), channel_id=1, source_target_pairs={{0,2},{2,0},{1,3},{3,1},{4,6},{6,4},{5,7},{7,5},{8,10},{10,8},{9,1... | collective-permute-start | bytes 1179656 | tf_op jit(solution)/shard_map/ppermute | solution.py:461
  40.1 6.6 %all-to-all-start.1 = ((bf16[16,4,2880]{2,1,0:T(4,128)(2,1)}), bf16[16,4,2880]{2,1,0:T(4,128)(2,1)S(1)}, u32[]{:S(2)}, u32[]{:S(2)}) async-start(bf16[16,4,2880]{2,1,0:T(4,128)(2,1)} %merge_side.1), calls=%async_computation.1 | async-start | bytes 753664 | tf_op jit(solution)/shard_map/all_to_all | solution.py:463
  46.7 0.0 collective-permute-start.6
  46.7 2.0 %collective-permute-done.5.across_ref = bf16[64,24,128]{2,1,0:T(8,128)(2,1)S(1)} collective-permute-done((bf16[64,24,128]{2,1,0:T(8,128)(2,1)S(1)}, bf16[64,24,128]{2,1,0:T(8,128)(2,1)S(1)}, u32[]{:S(2)}, u32[]{:S(2)}) %collective-permute-start.5) | collective-permute-done | bytes 393248 | tf_op jit(solution)/shard_map/ppermute | solution.py:461
  48.7 0.0 collective-permute-start.7
  48.7 0.0 collective-permute-done.6.core_ref
  48.7 1.7 %collective-permute-done.7.both_ref = bf16[64,24,128]{2,1,0:T(8,128)(2,1)S(1)} collective-permute-done((bf16[64,24,128]{2,1,0:T(8,128)(2,1)S(1)}, bf16[64,24,128]{2,1,0:T(8,128)(2,1)S(1)}, u32[]{:S(2)}, u32[]{:S(2)}) %collective-permute-start.7) | collective-permute-done | bytes 393248 | tf_op jit(solution)/shard_map/ppermute | solution.py:462
  50.4 1.8 %assemble.1 = bf16[2880,256]{1,0:T(8,128)(2,1)} custom-call(bf16[64,24,128]{2,1,0:T(8,128)(2,1)S(1)} %all-to-all-done.own_ref, bf16[64,24,128]{2,1,0:T(8,128)(2,1)S(1)} %collective-permute-done.5.across_ref, bf16[64,24,128]{2,1,0:T(8,128)(2,1)S(1)} %collective-permute-done.6.core_ref, bf16[64,24,128]{2,1,0:T(8,128)(2,1)S(1)} %collective-permute-done.7.both_ref), custom_call_target="tpu_custom_call" | custom-call | flops 1000000000 | bytes 4000000 | tf_op jit(solution)/shard_map/assemble/pallas_call | solution.py:159
  52.2 5.9 %all-to-all-done.1.got_ref = bf16[16,4,2880]{2,1,0:T(4,128)(2,1)S(1)} async-done(((bf16[16,4,2880]{2,1,0:T(4,128)(2,1)}), bf16[16,4,2880]{2,1,0:T(4,128)(2,1)S(1)}, u32[]{:S(2)}, u32[]{:S(2)}) %all-to-all-start.1) | async-done | bytes 368672 | tf_op jit(solution)/shard_map/all_to_all | solution.py:463
  58.0 0.7 %finish.1 = bf16[4,2880]{1,0:T(4,128)(2,1)} custom-call(bf16[16,4,2880]{2,1,0:T(4,128)(2,1)S(1)} %all-to-all-done.1.got_ref, f32[4,2880]{1,0:T(4,128)S(1)} %get-tuple-element.35.rows_ref), custom_call_target="tpu_custom_call" | custom-call | flops 1000000 | bytes 1000000 | tf_op jit(solution)/shard_map/finish/pallas_call | solution.py:420
  (1 shorter events, 0.0 us)
Async XLA Ops:
  0.6 6.7 %collective-permute-start = (bf16[8,720]{1,0:T(8,128)(2,1)}, bf16[8,720]{1,0:T(8,128)(2,1)S(1)}, u32[]{:S(2)}, u32[]{:S(2)}) collective-permute-start(bf16[8,720]{1,0:T(8,128)(2,1)} %bitcast.23), channel_id=1, source_target_pairs={{0,1},{1,0},{2,3},{3,2},{4,5},{5,4},{6,7},{7,6},{8,9},{9,8},{10,11... | collective-permute-start | bytes 34568 | tf_op jit(solution)/shard_map/ppermute | solution.py:436
  0.7 24.2 %copy-start.4 = (bf16[720,8]{0,1:T(8,128)(2,1)S(1)}, bf16[720,8]{0,1:T(8,128)(2,1)}, u32[]{:S(2)}) copy-start(bf16[720,8]{0,1:T(8,128)(2,1)} %param.15) | copy-start | bytes 34564
  0.7 29.7 %copy-start = (bf16[1,256,2880]{1,2,0:T(8,128)(2,1)S(1)}, bf16[1,256,2880]{1,2,0:T(8,128)(2,1)}, u32[]{:S(2)}) copy-start(bf16[1,256,2880]{1,2,0:T(8,128)(2,1)} %param.12) | copy-start | bytes 4423684
  0.8 29.7 %copy-start.1 = (bf16[2880]{0:T(1024)(128)(2,1)S(1)}, bf16[2880]{0:T(1024)(128)(2,1)}, u32[]{:S(2)}) copy-start(bf16[2880]{0:T(1024)(128)(2,1)} %gain_ref.1) | copy-start | bytes 17284
  0.8 29.7 %copy-start.2 = (s32[1,256,4]{1,2,0:T(4,128)S(1)}, s32[1,256,4]{1,2,0:T(4,128)}, u32[]{:S(2)}) copy-start(s32[1,256,4]{1,2,0:T(4,128)} %param.13) | copy-start | bytes 12292
  0.8 29.7 %copy-start.3 = (s32[64]{0:T(128)S(1)}, s32[64]{0:T(128)}, u32[]{:S(2)}) copy-start(s32[64]{0:T(128)} %place_ref.1) | copy-start | bytes 772
  7.4 17.6 %collective-permute-start.1 = (bf16[48,2880]{1,0:T(8,128)(2,1)S(1)}, bf16[48,2880]{1,0:T(8,128)(2,1)S(1)}, u32[]{:S(2)}, u32[]{:S(2)}) collective-permute-start(bf16[48,2880]{1,0:T(8,128)(2,1)S(1)} %get-tuple-element.25), channel_id=1, source_target_pairs={{0,128},{64,192},{128,0},{192,64},{1,129},{65,193},{129,1},{193,65... | collective-permute-start | bytes 829448 | tf_op jit(solution)/shard_map/ppermute | solution.py:450
  10.5 26.7 %all-to-all-start = ((bf16[64,24,128]{2,1,0:T(8,128)(2,1)}), bf16[64,24,128]{2,1,0:T(8,128)(2,1)S(1)}, u32[]{:S(2)}, u32[]{:S(2)}) async-start(bf16[64,24,128]{2,1,0:T(8,128)(2,1)} %get-tuple-element.23), calls=%async_computation | async-start | bytes 786432 | tf_op jit(solution)/shard_map/all_to_all | solution.py:451
  21.2 11.8 %collective-permute-start.3 = (bf16[48,2880]{1,0:T(8,128)(2,1)S(1)}, bf16[48,2880]{1,0:T(8,128)(2,1)S(1)}, u32[]{:S(2)}, u32[]{:S(2)}) collective-permute-start(bf16[48,2880]{1,0:T(8,128)(2,1)S(1)} %get-tuple-element.29), channel_id=1, source_target_pairs={{0,64},{64,0},{128,192},{192,128},{1,65},{65,1},{129,193},{193,129... | collective-permute-start | bytes 829448 | tf_op jit(solution)/shard_map/ppermute | solution.py:450
  22.8 12.7 %collective-permute-start.4 = (bf16[48,2880]{1,0:T(8,128)(2,1)S(1)}, bf16[48,2880]{1,0:T(8,128)(2,1)S(1)}, u32[]{:S(2)}, u32[]{:S(2)}) collective-permute-start(bf16[48,2880]{1,0:T(8,128)(2,1)S(1)} %get-tuple-element.30), channel_id=1, source_target_pairs={{0,192},{64,128},{128,64},{192,0},{1,193},{65,129},{129,65},{193,1... | collective-permute-start | bytes 829448 | tf_op jit(solution)/shard_map/ppermute | solution.py:450
  25.0 5.5 %collective-permute-start.2 = (bf16[2,8,720]{2,1,0:T(8,128)(2,1)S(1)}, bf16[2,8,720]{2,1,0:T(8,128)(2,1)S(1)}, u32[]{:S(2)}, u32[]{:S(2)}) collective-permute-start(bf16[2,8,720]{2,1,0:T(8,128)(2,1)S(1)} %pad_maximum_fusion.near_ref), channel_id=1, source_target_pairs={{0,2},{2,0},{1,3},{3,1},{4,6},{6,4},{5,7},{7,5},{8,10},{10,8},{9,1... | collective-permute-start | bytes 69128 | tf_op jit(solution)/shard_map/ppermute | solution.py:455
  37.2 11.5 %collective-permute-start.5 = (bf16[64,24,128]{2,1,0:T(8,128)(2,1)S(1)}, bf16[64,24,128]{2,1,0:T(8,128)(2,1)S(1)}, u32[]{:S(2)}, u32[]{:S(2)}) collective-permute-start(bf16[64,24,128]{2,1,0:T(8,128)(2,1)S(1)} %all-to-all-done.own_ref), channel_id=1, source_target_pairs={{0,2},{2,0},{1,3},{3,1},{4,6},{6,4},{5,7},{7,5},{8,10},{10,8},{9,1... | collective-permute-start | bytes 1179656 | tf_op jit(solution)/shard_map/ppermute | solution.py:461
  40.1 17.9 %all-to-all-start.1 = ((bf16[16,4,2880]{2,1,0:T(4,128)(2,1)}), bf16[16,4,2880]{2,1,0:T(4,128)(2,1)S(1)}, u32[]{:S(2)}, u32[]{:S(2)}) async-start(bf16[16,4,2880]{2,1,0:T(4,128)(2,1)} %merge_side.1), calls=%async_computation.1 | async-start | bytes 753664 | tf_op jit(solution)/shard_map/all_to_all | solution.py:463
  46.7 2.0 %collective-permute-start.6 = (bf16[64,24,128]{2,1,0:T(8,128)(2,1)S(1)}, bf16[64,24,128]{2,1,0:T(8,128)(2,1)S(1)}, u32[]{:S(2)}, u32[]{:S(2)}) collective-permute-start(bf16[64,24,128]{2,1,0:T(8,128)(2,1)S(1)} %all-to-all-done.own_ref), channel_id=1, source_target_pairs={{0,1},{1,0},{2,3},{3,2},{4,5},{5,4},{6,7},{7,6},{8,9},{9,8},{10,11... | collective-permute-start | bytes 1179656 | tf_op jit(solution)/shard_map/ppermute | solution.py:460
  48.7 1.7 %collective-permute-start.7 = (bf16[64,24,128]{2,1,0:T(8,128)(2,1)S(1)}, bf16[64,24,128]{2,1,0:T(8,128)(2,1)S(1)}, u32[]{:S(2)}, u32[]{:S(2)}) collective-permute-start(bf16[64,24,128]{2,1,0:T(8,128)(2,1)S(1)} %collective-permute-done.5.across_ref), channel_id=1, source_target_pairs={{0,1},{1,0},{2,3},{3,2},{4,5},{5,4},{6,7},{7,6},{8,9},{9,8},{10,11... | collective-permute-start | bytes 1179656 | tf_op jit(solution)/shard_map/ppermute | solution.py:462

commit v11 on v10

--- a/solution.py
+++ b/solution.py
@@ -251,7 +251,7 @@
         chunks_ref[o] = held_ref[pl.ds(slot_ref[o], HALF, stride=STRIDE), :].astype(BF)
         return 0
 
-    lax.fori_loop(0, SLOTS, deal, 0, unroll=8)
+    lax.fori_loop(0, SLOTS, deal, 0, unroll=64)
 
     side = lax.axis_index("x")
     owner = side * INNER + lax.axis_index("yl") * DEPTH + lax.axis_index("z")

time: 59 us -> 59.6 us (1.010)
  Pallas kernels: 12 us -> 12.6 us
    pallas_call x1, Pallas kernels: 6.57 us -> 7.19 us  [prepare(): pl.pallas_call(prepare_kernel, name='prepare', out_shape=(jax.ShapeDtypeS...]
  transfers between devices with their start and end apart: 10 -> 10, of which waited for: 7 -> 7; matrix products, arithmetic and copies ran while one was open for 0% -> 0% of each run, Pallas kernels for 19% -> 20%
where the time goes in v11:
time: 59.6 us; the launch traced here: 59.4 us
  starting transfers between devices  30.1 us (51%)
  waiting for transfers between devices  15.8 us (27%)
  Pallas kernels  12.6 us (21%)
  between operations  0.75 us (1%)
    all_to_all x1, starting transfers between devices, on_device(): lax.all_to_all(chunks, FSDP, split_axis=0, concat_axis=0, tiled=True)  10.7 us
    pallas_call x1, Pallas kernels, prepare(): pl.pallas_call(prepare_kernel, name='prepare', out_shape=(jax.ShapeDtypeS...  7.19 us
    ppermute x3, starting transfers between devices, on_device(): got.append(lax.ppermute(terms[d], 'x', [(x, x ^ d) for x in range(SIDE)]))  6.84 us
    all_to_all x1, starting transfers between devices, on_device(): lax.all_to_all(terms, ('yl', 'z'), split_axis=0, concat_axis=0, tiled=True)  6.58 us
    all_to_all x1, waiting for transfers between devices, on_device(): lax.all_to_all(terms, ('yl', 'z'), split_axis=0, concat_axis=0, tiled=True)  5.86 us
    ppermute x3, waiting for transfers between devices, on_device(): got.append(lax.ppermute(terms[d], 'x', [(x, x ^ d) for x in range(SIDE)]))  3.14 us
    ppermute x1, starting transfers between devices, on_device(): far = lax.ppermute(near, 'yh', swap)  2.99 us
    ppermute x1, starting transfers between devices, on_device(): across = lax.ppermute(chunks, 'yh', swap)  2.9 us
  transfers between devices with their start and end apart: 10, of which 7 were waited for; matrix products, arithmetic and copies ran while one was open for 0% of the time, Pallas kernels for 20%

profile of v11, /device:TPU:32, one launch (start us, length us, event | category | flops | bytes accessed | tf_op | source)
XLA Modules:
  0.0 59.4 jit_solution(18380008777024810808)
XLA Ops:
  0.6 0.1 collective-permute-start
  0.7 0.0 copy-start.4
  0.7 0.0 copy-start
  0.8 0.0 copy-start.1
  0.8 0.0 copy-start.2
  0.8 0.0 copy-start.3
  0.8 7.2 %prepare.1 = (bf16[64,24,128]{2,1,0:T(8,128)(2,1)}, bf16[48,2880]{1,0:T(8,128)(2,1)S(1)}, bf16[48,2880]{1,0:T(8,128)(2,1)S(1)}, bf16[48,2880]{1,0:T(8,128)(2,1)S(1)}, bf16[48,2880]{1,0:T(8,128)(2,1)S(1)}) custom-call(s32[64]{0:T(128)} %place_ref.1, f32[45,64,64]{2,1,0:T(8,128)} %bitcast.27, bf16[2880,256]{1,0:T(8,128)(2,1)} %bitcast.18, s32[4,256]{1,0:T(4,128)} %bitcast.20, ...), custom_call_target="tpu_custom_call" | custom-call | flops 8000000000 | bytes 10000000 | tf_op jit(solution)/shard_map/prepare/pallas_call | solution.py:288
  8.0 0.0 collective-permute-done
  8.0 3.1 %collective-permute-start.1 = (bf16[48,2880]{1,0:T(8,128)(2,1)S(1)}, bf16[48,2880]{1,0:T(8,128)(2,1)S(1)}, u32[]{:S(2)}, u32[]{:S(2)}) collective-permute-start(bf16[48,2880]{1,0:T(8,128)(2,1)S(1)} %get-tuple-element.25), channel_id=1, source_target_pairs={{0,128},{64,192},{128,0},{192,64},{1,129},{65,193},{129,1},{193,65... | collective-permute-start | bytes 829448 | tf_op jit(solution)/shard_map/ppermute | solution.py:450
  11.1 10.7 %all-to-all-start = ((bf16[64,24,128]{2,1,0:T(8,128)(2,1)}), bf16[64,24,128]{2,1,0:T(8,128)(2,1)S(1)}, u32[]{:S(2)}, u32[]{:S(2)}) async-start(bf16[64,24,128]{2,1,0:T(8,128)(2,1)} %get-tuple-element.23), calls=%async_computation | async-start | bytes 786432 | tf_op jit(solution)/shard_map/all_to_all | solution.py:451
  21.8 1.6 %collective-permute-start.3 = (bf16[48,2880]{1,0:T(8,128)(2,1)S(1)}, bf16[48,2880]{1,0:T(8,128)(2,1)S(1)}, u32[]{:S(2)}, u32[]{:S(2)}) collective-permute-start(bf16[48,2880]{1,0:T(8,128)(2,1)S(1)} %get-tuple-element.29), channel_id=1, source_target_pairs={{0,64},{64,0},{128,192},{192,128},{1,65},{65,1},{129,193},{193,129... | collective-permute-start | bytes 829448 | tf_op jit(solution)/shard_map/ppermute | solution.py:450
  23.4 2.2 %collective-permute-start.4 = (bf16[48,2880]{1,0:T(8,128)(2,1)S(1)}, bf16[48,2880]{1,0:T(8,128)(2,1)S(1)}, u32[]{:S(2)}, u32[]{:S(2)}) collective-permute-start(bf16[48,2880]{1,0:T(8,128)(2,1)S(1)} %get-tuple-element.30), channel_id=1, source_target_pairs={{0,192},{64,128},{128,64},{192,0},{1,193},{65,129},{129,65},{193,1... | collective-permute-start | bytes 829448 | tf_op jit(solution)/shard_map/ppermute | solution.py:450
  25.5 0.0 collective-permute-done.1.got2_ref
  25.5 0.0 copy-done.4
  25.5 3.0 %collective-permute-start.2 = (bf16[2,8,720]{2,1,0:T(8,128)(2,1)S(1)}, bf16[2,8,720]{2,1,0:T(8,128)(2,1)S(1)}, u32[]{:S(2)}, u32[]{:S(2)}) collective-permute-start(bf16[2,8,720]{2,1,0:T(8,128)(2,1)S(1)} %pad_maximum_fusion.near_ref), channel_id=1, source_target_pairs={{0,2},{2,0},{1,3},{3,1},{4,6},{6,4},{5,7},{7,5},{8,10},{10,8},{9,1... | collective-permute-start | bytes 69128 | tf_op jit(solution)/shard_map/ppermute | solution.py:455
  28.5 2.5 %collective-permute-done.2.far_ref = bf16[2,8,720]{2,1,0:T(8,128)(2,1)S(1)} collective-permute-done((bf16[2,8,720]{2,1,0:T(8,128)(2,1)S(1)}, bf16[2,8,720]{2,1,0:T(8,128)(2,1)S(1)}, u32[]{:S(2)}, u32[]{:S(2)}) %collective-permute-start.2) | collective-permute-done | bytes 23072 | tf_op jit(solution)/shard_map/ppermute | solution.py:455
  31.0 0.0 copy-done
  31.0 0.0 copy-done.1
  31.0 0.0 copy-done.2
  31.0 0.0 copy-done.3
  31.0 1.8 %weigh.1 = (bf16[128,192]{1,0:T(8,128)(2,1)S(1)}, f32[4,2880]{1,0:T(4,128)S(1)}) custom-call(s32[64]{0:T(128)S(1)} %copy-done.3, s32[4,256]{1,0:T(4,128)S(1)} %bitcast.21, bf16[2,8,720]{2,1,0:T(8,128)(2,1)S(1)} %pad_maximum_fusion.near_ref, bf16[2,8,720]{2,1,0:T(8,128)(2,1)S(1)} %collective-permute-done.2.far_ref, bf16[2880,256]{1,0:T(8,128)(2,1)S(1)} %bitcast.19, ...), custom_call_target="tpu_custom_call" | custom-call | flops 1 | bytes 1 | tf_op jit(solution)/shard_map/weigh/pallas_call | solution.py:367
  32.9 0.8 %collective-permute-done.3.got1_ref = bf16[48,2880]{1,0:T(8,128)(2,1)S(1)} collective-permute-done((bf16[48,2880]{1,0:T(8,128)(2,1)S(1)}, bf16[48,2880]{1,0:T(8,128)(2,1)S(1)}, u32[]{:S(2)}, u32[]{:S(2)}) %collective-permute-start.3) | collective-permute-done | bytes 276512 | tf_op jit(solution)/shard_map/ppermute | solution.py:450
  33.6 2.4 %collective-permute-done.4.got3_ref = bf16[48,2880]{1,0:T(8,128)(2,1)S(1)} collective-permute-done((bf16[48,2880]{1,0:T(8,128)(2,1)S(1)}, bf16[48,2880]{1,0:T(8,128)(2,1)S(1)}, u32[]{:S(2)}, u32[]{:S(2)}) %collective-permute-start.4) | collective-permute-done | bytes 276512 | tf_op jit(solution)/shard_map/ppermute | solution.py:450
  36.0 1.2 %merge_side.1 = bf16[16,4,2880]{2,1,0:T(4,128)(2,1)} custom-call(bf16[128,192]{1,0:T(8,128)(2,1)S(1)} %get-tuple-element.27.table_ref, bf16[48,2880]{1,0:T(8,128)(2,1)S(1)} %get-tuple-element.28.got0_ref, bf16[48,2880]{1,0:T(8,128)(2,1)S(1)} %collective-permute-done.3.got1_ref, bf16[48,2880]{1,0:T(8,128)(2,1)S(1)} %collective-permute-done.1.got2_ref, ...), custom_call_target="tpu_custom_call" | custom-call | flops 4000000000 | bytes 1 | tf_op jit(solution)/shard_map/merge_side/pallas_call | solution.py:400
  37.2 0.7 %all-to-all-done.own_ref = bf16[64,24,128]{2,1,0:T(8,128)(2,1)S(1)} async-done(((bf16[64,24,128]{2,1,0:T(8,128)(2,1)}), bf16[64,24,128]{2,1,0:T(8,128)(2,1)S(1)}, u32[]{:S(2)}, u32[]{:S(2)}) %all-to-all-start) | async-done | bytes 393248 | tf_op jit(solution)/shard_map/all_to_all | solution.py:451
  37.8 2.9 %collective-permute-start.5 = (bf16[64,24,128]{2,1,0:T(8,128)(2,1)S(1)}, bf16[64,24,128]{2,1,0:T(8,128)(2,1)S(1)}, u32[]{:S(2)}, u32[]{:S(2)}) collective-permute-start(bf16[64,24,128]{2,1,0:T(8,128)(2,1)S(1)} %all-to-all-done.own_ref), channel_id=1, source_target_pairs={{0,2},{2,0},{1,3},{3,1},{4,6},{6,4},{5,7},{7,5},{8,10},{10,8},{9,1... | collective-permute-start | bytes 1179656 | tf_op jit(solution)/shard_map/ppermute | solution.py:461
  40.7 6.6 %all-to-all-start.1 = ((bf16[16,4,2880]{2,1,0:T(4,128)(2,1)}), bf16[16,4,2880]{2,1,0:T(4,128)(2,1)S(1)}, u32[]{:S(2)}, u32[]{:S(2)}) async-start(bf16[16,4,2880]{2,1,0:T(4,128)(2,1)} %merge_side.1), calls=%async_computation.1 | async-start | bytes 753664 | tf_op jit(solution)/shard_map/all_to_all | solution.py:463
  47.3 0.0 collective-permute-start.6
  47.3 2.0 %collective-permute-done.5.across_ref = bf16[64,24,128]{2,1,0:T(8,128)(2,1)S(1)} collective-permute-done((bf16[64,24,128]{2,1,0:T(8,128)(2,1)S(1)}, bf16[64,24,128]{2,1,0:T(8,128)(2,1)S(1)}, u32[]{:S(2)}, u32[]{:S(2)}) %collective-permute-start.5) | collective-permute-done | bytes 393248 | tf_op jit(solution)/shard_map/ppermute | solution.py:461
  49.3 0.0 collective-permute-start.7
  49.3 0.0 collective-permute-done.6.core_ref
  49.3 1.7 %collective-permute-done.7.both_ref = bf16[64,24,128]{2,1,0:T(8,128)(2,1)S(1)} collective-permute-done((bf16[64,24,128]{2,1,0:T(8,128)(2,1)S(1)}, bf16[64,24,128]{2,1,0:T(8,128)(2,1)S(1)}, u32[]{:S(2)}, u32[]{:S(2)}) %collective-permute-start.7) | collective-permute-done | bytes 393248 | tf_op jit(solution)/shard_map/ppermute | solution.py:462
  51.1 1.8 %assemble.1 = bf16[2880,256]{1,0:T(8,128)(2,1)} custom-call(bf16[64,24,128]{2,1,0:T(8,128)(2,1)S(1)} %all-to-all-done.own_ref, bf16[64,24,128]{2,1,0:T(8,128)(2,1)S(1)} %collective-permute-done.5.across_ref, bf16[64,24,128]{2,1,0:T(8,128)(2,1)S(1)} %collective-permute-done.6.core_ref, bf16[64,24,128]{2,1,0:T(8,128)(2,1)S(1)} %collective-permute-done.7.both_ref), custom_call_target="tpu_custom_call" | custom-call | flops 1000000000 | bytes 4000000 | tf_op jit(solution)/shard_map/assemble/pallas_call | solution.py:159
  52.8 5.9 %all-to-all-done.1.got_ref = bf16[16,4,2880]{2,1,0:T(4,128)(2,1)S(1)} async-done(((bf16[16,4,2880]{2,1,0:T(4,128)(2,1)}), bf16[16,4,2880]{2,1,0:T(4,128)(2,1)S(1)}, u32[]{:S(2)}, u32[]{:S(2)}) %all-to-all-start.1) | async-done | bytes 368672 | tf_op jit(solution)/shard_map/all_to_all | solution.py:463
  58.7 0.7 %finish.1 = bf16[4,2880]{1,0:T(4,128)(2,1)} custom-call(bf16[16,4,2880]{2,1,0:T(4,128)(2,1)S(1)} %all-to-all-done.1.got_ref, f32[4,2880]{1,0:T(4,128)S(1)} %get-tuple-element.35.rows_ref), custom_call_target="tpu_custom_call" | custom-call | flops 1000000 | bytes 1000000 | tf_op jit(solution)/shard_map/finish/pallas_call | solution.py:420
  (1 shorter events, 0.0 us)
Async XLA Ops:
  0.6 7.3 %collective-permute-start = (bf16[8,720]{1,0:T(8,128)(2,1)}, bf16[8,720]{1,0:T(8,128)(2,1)S(1)}, u32[]{:S(2)}, u32[]{:S(2)}) collective-permute-start(bf16[8,720]{1,0:T(8,128)(2,1)} %bitcast.23), channel_id=1, source_target_pairs={{0,1},{1,0},{2,3},{3,2},{4,5},{5,4},{6,7},{7,6},{8,9},{9,8},{10,11... | collective-permute-start | bytes 34568 | tf_op jit(solution)/shard_map/ppermute | solution.py:436
  0.7 24.8 %copy-start.4 = (bf16[720,8]{0,1:T(8,128)(2,1)S(1)}, bf16[720,8]{0,1:T(8,128)(2,1)}, u32[]{:S(2)}) copy-start(bf16[720,8]{0,1:T(8,128)(2,1)} %param.15) | copy-start | bytes 34564
  0.7 30.3 %copy-start = (bf16[1,256,2880]{1,2,0:T(8,128)(2,1)S(1)}, bf16[1,256,2880]{1,2,0:T(8,128)(2,1)}, u32[]{:S(2)}) copy-start(bf16[1,256,2880]{1,2,0:T(8,128)(2,1)} %param.12) | copy-start | bytes 4423684
  0.8 30.3 %copy-start.1 = (bf16[2880]{0:T(1024)(128)(2,1)S(1)}, bf16[2880]{0:T(1024)(128)(2,1)}, u32[]{:S(2)}) copy-start(bf16[2880]{0:T(1024)(128)(2,1)} %gain_ref.1) | copy-start | bytes 17284
  0.8 30.3 %copy-start.2 = (s32[1,256,4]{1,2,0:T(4,128)S(1)}, s32[1,256,4]{1,2,0:T(4,128)}, u32[]{:S(2)}) copy-start(s32[1,256,4]{1,2,0:T(4,128)} %param.13) | copy-start | bytes 12292
  0.8 30.3 %copy-start.3 = (s32[64]{0:T(128)S(1)}, s32[64]{0:T(128)}, u32[]{:S(2)}) copy-start(s32[64]{0:T(128)} %place_ref.1) | copy-start | bytes 772
  8.0 17.5 %collective-permute-start.1 = (bf16[48,2880]{1,0:T(8,128)(2,1)S(1)}, bf16[48,2880]{1,0:T(8,128)(2,1)S(1)}, u32[]{:S(2)}, u32[]{:S(2)}) collective-permute-start(bf16[48,2880]{1,0:T(8,128)(2,1)S(1)} %get-tuple-element.25), channel_id=1, source_target_pairs={{0,128},{64,192},{128,0},{192,64},{1,129},{65,193},{129,1},{193,65... | collective-permute-start | bytes 829448 | tf_op jit(solution)/shard_map/ppermute | solution.py:450
  11.1 26.7 %all-to-all-start = ((bf16[64,24,128]{2,1,0:T(8,128)(2,1)}), bf16[64,24,128]{2,1,0:T(8,128)(2,1)S(1)}, u32[]{:S(2)}, u32[]{:S(2)}) async-start(bf16[64,24,128]{2,1,0:T(8,128)(2,1)} %get-tuple-element.23), calls=%async_computation | async-start | bytes 786432 | tf_op jit(solution)/shard_map/all_to_all | solution.py:451
  21.8 11.8 %collective-permute-start.3 = (bf16[48,2880]{1,0:T(8,128)(2,1)S(1)}, bf16[48,2880]{1,0:T(8,128)(2,1)S(1)}, u32[]{:S(2)}, u32[]{:S(2)}) collective-permute-start(bf16[48,2880]{1,0:T(8,128)(2,1)S(1)} %get-tuple-element.29), channel_id=1, source_target_pairs={{0,64},{64,0},{128,192},{192,128},{1,65},{65,1},{129,193},{193,129... | collective-permute-start | bytes 829448 | tf_op jit(solution)/shard_map/ppermute | solution.py:450
  23.4 12.7 %collective-permute-start.4 = (bf16[48,2880]{1,0:T(8,128)(2,1)S(1)}, bf16[48,2880]{1,0:T(8,128)(2,1)S(1)}, u32[]{:S(2)}, u32[]{:S(2)}) collective-permute-start(bf16[48,2880]{1,0:T(8,128)(2,1)S(1)} %get-tuple-element.30), channel_id=1, source_target_pairs={{0,192},{64,128},{128,64},{192,0},{1,193},{65,129},{129,65},{193,1... | collective-permute-start | bytes 829448 | tf_op jit(solution)/shard_map/ppermute | solution.py:450
  25.5 5.5 %collective-permute-start.2 = (bf16[2,8,720]{2,1,0:T(8,128)(2,1)S(1)}, bf16[2,8,720]{2,1,0:T(8,128)(2,1)S(1)}, u32[]{:S(2)}, u32[]{:S(2)}) collective-permute-start(bf16[2,8,720]{2,1,0:T(8,128)(2,1)S(1)} %pad_maximum_fusion.near_ref), channel_id=1, source_target_pairs={{0,2},{2,0},{1,3},{3,1},{4,6},{6,4},{5,7},{7,5},{8,10},{10,8},{9,1... | collective-permute-start | bytes 69128 | tf_op jit(solution)/shard_map/ppermute | solution.py:455
  37.8 11.5 %collective-permute-start.5 = (bf16[64,24,128]{2,1,0:T(8,128)(2,1)S(1)}, bf16[64,24,128]{2,1,0:T(8,128)(2,1)S(1)}, u32[]{:S(2)}, u32[]{:S(2)}) collective-permute-start(bf16[64,24,128]{2,1,0:T(8,128)(2,1)S(1)} %all-to-all-done.own_ref), channel_id=1, source_target_pairs={{0,2},{2,0},{1,3},{3,1},{4,6},{6,4},{5,7},{7,5},{8,10},{10,8},{9,1... | collective-permute-start | bytes 1179656 | tf_op jit(solution)/shard_map/ppermute | solution.py:461
  40.7 17.9 %all-to-all-start.1 = ((bf16[16,4,2880]{2,1,0:T(4,128)(2,1)}), bf16[16,4,2880]{2,1,0:T(4,128)(2,1)S(1)}, u32[]{:S(2)}, u32[]{:S(2)}) async-start(bf16[16,4,2880]{2,1,0:T(4,128)(2,1)} %merge_side.1), calls=%async_computation.1 | async-start | bytes 753664 | tf_op jit(solution)/shard_map/all_to_all | solution.py:463
  47.3 2.0 %collective-permute-start.6 = (bf16[64,24,128]{2,1,0:T(8,128)(2,1)S(1)}, bf16[64,24,128]{2,1,0:T(8,128)(2,1)S(1)}, u32[]{:S(2)}, u32[]{:S(2)}) collective-permute-start(bf16[64,24,128]{2,1,0:T(8,128)(2,1)S(1)} %all-to-all-done.own_ref), channel_id=1, source_target_pairs={{0,1},{1,0},{2,3},{3,2},{4,5},{5,4},{6,7},{7,6},{8,9},{9,8},{10,11... | collective-permute-start | bytes 1179656 | tf_op jit(solution)/shard_map/ppermute | solution.py:460
  49.3 1.7 %collective-permute-start.7 = (bf16[64,24,128]{2,1,0:T(8,128)(2,1)S(1)}, bf16[64,24,128]{2,1,0:T(8,128)(2,1)S(1)}, u32[]{:S(2)}, u32[]{:S(2)}) collective-permute-start(bf16[64,24,128]{2,1,0:T(8,128)(2,1)S(1)} %collective-permute-done.5.across_ref), channel_id=1, source_target_pairs={{0,1},{1,0},{2,3},{3,2},{4,5},{5,4},{6,7},{7,6},{8,9},{9,8},{10,11... | collective-permute-start | bytes 1179656 | tf_op jit(solution)/shard_map/ppermute | solution.py:462
